TPU v7x, 128 devices: a whole 4x4x4 slice. The times are simulated.
128 devices in a mesh: tile: 8 (over y, core), seq: 16 (over z, x).
Axes of the slice: x: 4, y: 4, z: 4, core: 2. Of those that a mesh axis runs over, the one named last changes fastest.
Arguments:
- tokens: bfloat16 [128, 8, 16, 4, 1024], P(('tile', 'seq')), as said below
- levels: int32 [128, 8, 16, 4], P(('tile', 'seq')), may hold values from 0 to 5
- counts: int32 [8, 16, 128], replicated, may hold values from 1 to 4, 256 in all within a row
- level_table: bfloat16 [6, 1024], replicated, may hold values from -6 to 6
- norm_gain: float32 [1024], replicated, may hold values from 0.5 to 2
- project_weight: bfloat16 [16, 3, 64, 1024], replicated, may hold values from -0.1875 to 0.1875
- output_weight: bfloat16 [16, 64, 1024], replicated, may hold values from -0.1875 to 0.1875
- cotangent: bfloat16 [8, 4096, 1024], P('tile', 'seq'), may hold values from -6 to 6
Outputs:
- output: bfloat16 [8, 4096, 1024], P('tile', 'seq')
- token_grad: bfloat16 [128, 8, 16, 4, 1024], P(('tile', 'seq'))
- project_grad: float32 [16, 3, 64, 1024], P('seq', None, None, 'tile')
- output_grad: float32 [16, 64, 1024], P('seq', None, 'tile')
- gain_grad: float32 [1024], replicated
- table_grad: float32 [6, 1024], replicated
Inputs may be any that keep to these rules, and one draw needn't show every extreme that they name: For each map and shard, the 128 tile counts sum to 256, and one of them is 4. `tokens`: features in slots at or past a tile's count are never read.
All inputs are finite; a program needn't handle non-finite values.
Results may differ from a plain program's by a relative error of at most 0.025.
Values may be sent and summed in bfloat16 or wider, within the bound.
No kernel may reach another device: no remote copies, remote signals or barrier semaphores. Data moves between devices by JAX's collectives and lax.ppermute only.
A program may use at most 128 MiB of HBM per device.

v0:
```python
import math

import jax
import jax.numpy as jnp
from jax import lax
from jax.sharding import PartitionSpec as P

EPSILON = 1e-05


def pack_positions(counts, rows, slots):
    starts = jnp.cumsum(counts) - counts
    place = jnp.arange(rows, dtype=jnp.int32)
    before = (starts[None, :] <= place[:, None]).astype(jnp.int32)
    owner = jnp.sum(before, axis=1) - 1
    first = jnp.max(jnp.where(before > 0, starts[None, :], 0), axis=1)
    return owner * slots + place - first


def unpack_positions(counts, slots):
    starts = jnp.cumsum(counts) - counts
    within = jnp.arange(slots, dtype=jnp.int32)
    usable = within[None, :] < counts[:, None]
    return (jnp.where(usable, starts[:, None] + within[None, :], 0), usable)


def to_blocks(array, block):
    width, length = array.shape
    return array.reshape(width, length // block, block).transpose(1, 0, 2)


def from_blocks(array):
    count, width, block = array.shape
    return array.transpose(1, 0, 2).reshape(width, count * block)


def head_forward(query, keys, values, scale, shift):
    block = math.gcd(query.shape[1], 512)

    def one_block(rows):
        scores = (
            lax.dot_general(
                rows, keys, (((0,), (0,)), ((), ())), preferred_element_type=jnp.float32
            )
            * scale
            - shift
        )
        weights = jax.nn.sigmoid(scores).astype(jnp.bfloat16)
        return lax.dot_general(
            values, weights, (((1,), (1,)), ((), ())), preferred_element_type=jnp.float32
        ).astype(jnp.bfloat16)

    return from_blocks(lax.map(one_block, to_blocks(query, block)))


def head_backward(query, keys, values, grad_out, scale, shift):
    width, length = query.shape
    block = math.gcd(length, 512)

    def one_block(carry, pair):
        key_total, value_total = carry
        rows, grads = pair
        scores = (
            lax.dot_general(
                rows, keys, (((0,), (0,)), ((), ())), preferred_element_type=jnp.float32
            )
            * scale
            - shift
        )
        probs = jax.nn.sigmoid(scores)
        weights = probs.astype(jnp.bfloat16)
        grad_weights = lax.dot_general(
            grads, values, (((0,), (0,)), ((), ())), preferred_element_type=jnp.float32
        )
        grad_scores = (grad_weights * probs * (1.0 - probs)).astype(jnp.bfloat16)
        grad_query = lax.dot_general(
            keys, grad_scores, (((1,), (1,)), ((), ())), preferred_element_type=jnp.float32
        )
        grad_query = (grad_query * scale).astype(jnp.bfloat16)
        key_total = key_total + lax.dot_general(
            rows, grad_scores, (((1,), (0,)), ((), ())), preferred_element_type=jnp.float32
        )
        value_total = value_total + lax.dot_general(
            grads, weights, (((1,), (0,)), ((), ())), preferred_element_type=jnp.float32
        )
        return ((key_total, value_total), grad_query)

    zeros = jnp.zeros((width, length), jnp.float32)
    totals, grad_query = lax.scan(
        one_block, (zeros, zeros), (to_blocks(query, block), to_blocks(grad_out, block))
    )
    return (
        from_blocks(grad_query),
        (totals[0] * scale).astype(jnp.bfloat16),
        totals[1].astype(jnp.bfloat16),
    )


def on_device(
    tokens, levels, counts, level_table, norm_gain, project_weight, output_weight, cotangent
):
    tiles = lax.axis_size("tile")
    shards = lax.axis_size("seq")
    tile_index = lax.axis_index("tile")
    shard_index = lax.axis_index("seq")
    owners = tiles * shards
    slots = tokens.shape[3]
    width = tokens.shape[4]
    rows = cotangent.shape[1]
    length = rows * shards
    scale = 1.0 / math.sqrt(project_weight.shape[2])
    shift = math.log(length)
    factor = 1.0 / math.sqrt(tiles * length)
    onehot = (levels[0][..., None] == jnp.arange(level_table.shape[0], dtype=jnp.int32)).astype(
        jnp.bfloat16
    )
    embedded = tokens[0].astype(jnp.float32) + jnp.einsum(
        "msjl,ld->msjd", onehot, level_table, preferred_element_type=jnp.float32
    )
    embedded = embedded.astype(jnp.bfloat16)
    received = lax.all_to_all(
        embedded.reshape(owners, slots, width),
        ("tile", "seq"),
        split_axis=0,
        concat_axis=0,
        tiled=True,
    )
    received = received.reshape(owners * slots, width)
    map_counts = lax.dynamic_index_in_dim(counts, tile_index, 0, keepdims=False)
    own_counts = lax.dynamic_index_in_dim(map_counts, shard_index, 0, keepdims=False)
    features = jnp.take(received, pack_positions(own_counts, rows, slots), axis=0)
    activations = features.astype(jnp.float32)
    inverse = lax.rsqrt(jnp.mean(activations * activations, axis=1, keepdims=True) + EPSILON)
    normed = (activations * inverse * norm_gain).astype(jnp.bfloat16)
    projected = jnp.einsum(
        "td,hced->hcet", normed, project_weight, preferred_element_type=jnp.float32
    ).astype(jnp.bfloat16)
    head_major = lax.all_to_all(projected, "seq", split_axis=0, concat_axis=3, tiled=True)

    def attend(triple):
        return head_forward(triple[0], triple[1], triple[2], scale, shift)

    attended = lax.map(attend, (head_major[:, 0], head_major[:, 1], head_major[:, 2]))
    mixed = lax.all_to_all(attended, "seq", split_axis=2, concat_axis=0, tiled=True)
    output = activations + jnp.einsum(
        "het,hed->td", mixed, output_weight, preferred_element_type=jnp.float32
    )
    output = output.astype(jnp.bfloat16)
    grad_rows = cotangent[0]
    grad_mixed = jnp.einsum(
        "td,hed->het", grad_rows, output_weight, preferred_element_type=jnp.float32
    ).astype(jnp.bfloat16)
    grad_heads = lax.all_to_all(grad_mixed, "seq", split_axis=0, concat_axis=2, tiled=True)
    part = mixed
    output_share = lax.psum_scatter(
        (
            jnp.einsum("het,td->hed", part, grad_rows, preferred_element_type=jnp.float32) * factor
        ).astype(jnp.bfloat16),
        "seq",
        scatter_dimension=0,
        tiled=True,
    )
    output_grad = lax.psum_scatter(output_share, "tile", scatter_dimension=2, tiled=True).astype(
        jnp.float32
    )

    def backward(quad):
        return jnp.stack(head_backward(quad[0], quad[1], quad[2], quad[3], scale, shift), axis=0)

    grad_head_major = lax.map(
        backward, (head_major[:, 0], head_major[:, 1], head_major[:, 2], grad_heads)
    )
    grad_projected = lax.all_to_all(grad_head_major, "seq", split_axis=3, concat_axis=0, tiled=True)
    part = grad_projected
    project_share = lax.psum_scatter(
        (
            jnp.einsum("hcet,td->hced", part, normed, preferred_element_type=jnp.float32) * factor
        ).astype(jnp.bfloat16),
        "seq",
        scatter_dimension=0,
        tiled=True,
    )
    project_grad = lax.psum_scatter(project_share, "tile", scatter_dimension=3, tiled=True).astype(
        jnp.float32
    )
    grad_normed = jnp.einsum(
        "hcet,hced->td", grad_projected, project_weight, preferred_element_type=jnp.float32
    )
    scaled = norm_gain * grad_normed
    cubed = inverse * inverse * inverse
    grad_activations = inverse * scaled - activations * cubed * jnp.mean(
        activations * scaled, axis=1, keepdims=True
    )
    gain_term = jnp.sum(grad_normed * activations * inverse, axis=0) * factor
    grad_features = (grad_rows.astype(jnp.float32) + grad_activations).astype(jnp.bfloat16)
    places, usable = unpack_positions(own_counts, slots)
    taken = jnp.take(grad_features, places.reshape(-1), axis=0).reshape(owners, slots, width)
    outgoing = jnp.where(usable[..., None], taken, jnp.zeros((), jnp.bfloat16))
    returned = lax.all_to_all(outgoing, ("tile", "seq"), split_axis=0, concat_axis=0, tiled=True)
    token_grad = returned.reshape(tiles, shards, slots, width)
    table_term = (
        jnp.einsum("msjl,msjd->ld", onehot, token_grad, preferred_element_type=jnp.float32) * factor
    )
    gain_grad, table_grad = lax.psum((gain_term, table_term), ("tile", "seq"))
    return (output[None], token_grad[None], project_grad, output_grad, gain_grad, table_grad)


def solution(mesh):
    return jax.shard_map(
        on_device,
        mesh=mesh,
        in_specs=(
            P(("tile", "seq"), None, None, None, None),
            P(("tile", "seq"), None, None, None),
            P(),
            P(),
            P(),
            P(),
            P(),
            P("tile", "seq", None),
        ),
        out_specs=(
            P("tile", "seq", None),
            P(("tile", "seq"), None, None, None, None),
            P("seq", None, None, "tile"),
            P("seq", None, "tile"),
            P(),
            P(),
        ),
        check_vma=False,
    )
```

profile of v0, /device:TPU:0, one launch (start us, length us, event | category | flops | bytes accessed | tf_op | source)
XLA Modules:
  0.0 536.8 jit_solution(11047793657153228988)
XLA Ops:
  12.4 11.7 %all-to-all-start = ((bf16[128,4,1024]{2,1,0:T(4,128)(2,1)}), bf16[128,4,1024]{2,1,0:T(4,128)(2,1)}, u32[]{:S(2)}, u32[]{:S(2)}) async-start(bf16[128,4,1024]{2,1,0:T(4,128)(2,1)} %copy.69), calls=%async_computation | async-start | bytes 2097152 | tf_op jit(solution)/shard_map/all_to_all | solution.py:121
  26.6 16.0 %all-to-all-done = bf16[128,4,1024]{2,1,0:T(4,128)(2,1)} async-done(((bf16[128,4,1024]{2,1,0:T(4,128)(2,1)}), bf16[128,4,1024]{2,1,0:T(4,128)(2,1)}, u32[]{:S(2)}, u32[]{:S(2)}) %all-to-all-start) | async-done | bytes 1048608 | tf_op jit(solution)/shard_map/all_to_all | solution.py:121
  47.9 6.1 %fusion.36 = bf16[16,3,64,256]{3,2,1,0:T(8,128)(2,1)} fusion(bf16[16,3,64,1024]{3,2,1,0:T(8,128)(2,1)} %param.17, f32[1024]{0:T(1024)S(1)} %copy-done.17, f32[256]{0:T(256)S(1)} %get-tuple-element.298, bf16[256,1024]{1,0:T(8,128)(2,1)} %gather_fusion, pred[256]{0:T(512)(128)(4,1)S(1)} %compare_and_fusion.1), kind=kOutput, calls=%fused_computation.52 | convolution fusion | flops 1612709888 | bytes 8393984 | tf_op jit(solution)/shard_map/td,hced->hcet/dot_general | solution.py:135
  54.0 4.4 all-to-all-start.1
  60.0 23.1 %all-to-all-done.1 = bf16[16,3,64,256]{3,2,1,0:T(8,128)(2,1)} async-done(((bf16[16,3,64,256]{3,2,1,0:T(8,128)(2,1)}), bf16[16,3,64,256]{3,2,1,0:T(8,128)(2,1)}, u32[]{:S(2)}, u32[]{:S(2)}) %all-to-all-start.1) | async-done | bytes 1572896 | tf_op jit(solution)/shard_map/all_to_all | solution.py:138
  83.1 4.7 all-to-all-start.3
  91.6 40.4 %while.45 = (s32[]{:T(128)}, bf16[8,64,512]{2,1,0:T(8,128)(2,1)}, bf16[8,64,512]{2,1,0:T(8,128)(2,1)}, bf16[64,4096]{1,0:T(8,128)(2,1)S(1)}, bf16[64,4096]{1,0:T(8,128)(2,1)S(1)}, /*index=5*/s32[]{:T(128)}) while((s32[]{:T(128)}, bf16[8,64,512]{2,1,0:T(8,128)(2,1)}, bf16[8,64,512]{2,1,0:T(8,128)(2,1)}, bf16[64,4096]{1,0:T(8,128)(2,1)S(1)}, ...), condition=%wide.region_5.6_spmd, body=%wide.region_4.5_spmd.sunk | while | flops 549486592 | bytes 1180749 | solution.py:53
  91.6 5.0 fusion.103
  96.6 5.0 fusion.103
  101.6 5.1 fusion.103
  106.7 5.0 fusion.103
  111.8 5.1 fusion.103
  116.8 5.1 fusion.103
  121.9 5.1 fusion.103
  126.9 5.0 fusion.103
  132.0 2.7 copy.89
  134.7 6.9 %reshape.274 = bf16[1,64,4096]{1,0,2:T(2,128)(2,1)} reshape(bf16[64,8,512]{0,2,1:T(8,128)(2,1)} %copy.89) | data formatting | bytes 1048576 | tf_op jit(solution)/shard_map/while/body/jit(dynamic_update_index_in_dim)/broadcast_in_dim | solution.py:143
  142.1 24.4 %reduce.1 = bf16[4096,64]{1,0:T(8,128)(2,1)} reduce(bf16[4096,1,64]{2,1,0:T(2,128)(2,1)} %bitcast.197, bf16[]{:T(256)} %broadcast.267), dimensions={1}, to_apply=%bitcast.141.reduce_sub_computation | reduce | bytes 1048578
  166.5 3.0 reshape.283
  169.5 7.3 %all-to-all-start.2 = ((bf16[16,2,8192]{2,1,0:T(2,128)(2,1)}), bf16[16,2,8192]{2,1,0:T(2,128)(2,1)}, u32[]{:S(2)}, u32[]{:S(2)}) async-start(bf16[16,2,8192]{2,1,0:T(2,128)(2,1)} %reshape.283), calls=%async_computation.2 | async-start | bytes 1048576 | tf_op jit(solution)/shard_map/all_to_all | solution.py:144
  177.1 2.1 copy.76
  179.2 2.0 reshape.248
  183.3 3.7 all-to-all-done.2
  187.0 5.6 %reshape.284 = bf16[4096,1,64]{2,1,0:T(2,128)(2,1)} reshape(bf16[16,2,8192]{2,1,0:T(2,128)(2,1)} %all-to-all-done.2) | data formatting | bytes 1048576
  192.5 5.2 copy.74
  199.8 3.1 multiply_convert_fusion.2
  203.8 95.4 %while.46 = (s32[]{:T(128)}, f32[64,4096]{1,0:T(8,128)S(1)}, f32[64,4096]{1,0:T(8,128)}, bf16[8,64,512]{2,1,0:T(8,128)(2,1)}, bf16[8,64,512]{2,1,0:T(8,128)(2,1)...) while((s32[]{:T(128)}, f32[64,4096]{1,0:T(8,128)S(1)}, ...), condition=%wide.region_7.8_spmd.clone, body=%wide.region_6.7_spmd.clone.sunk | while | flops 1364262912 | bytes 56426744 | solution.py:89
  203.8 3.8 add_divide_fusion.2
  209.5 2.3 multiply_convert_fusion.5
  215.7 3.8 add_divide_fusion.2
  221.5 2.3 multiply_convert_fusion.5
  223.7 2.0 fusion.114
  227.6 3.8 add_divide_fusion.2
  233.4 2.3 multiply_convert_fusion.5
  239.6 3.8 add_divide_fusion.2
  245.3 2.3 multiply_convert_fusion.5
  247.6 2.0 fusion.114
  251.5 3.8 add_divide_fusion.2
  257.3 2.3 multiply_convert_fusion.5
  263.5 3.8 add_divide_fusion.2
  269.2 2.3 multiply_convert_fusion.5
  275.4 3.8 add_divide_fusion.2
  281.1 2.3 multiply_convert_fusion.5
  283.4 2.0 fusion.114
  287.3 3.8 add_divide_fusion.2
  293.1 2.3 multiply_convert_fusion.5
  299.2 2.2 copy.78
  301.4 2.1 reshape.249
  304.8 2.4 maximum_bitcast_fusion
  307.2 6.4 %copy.79 = bf16[1,3,64,4096]{2,1,0,3:T(4,128)(2,1)} copy(bf16[1,3,64,4096]{3,2,1,0:T(8,128)(2,1)} %maximum_bitcast_fusion) | data formatting | bytes 3145728 | tf_op jit(solution)/shard_map/while/body/jit(dynamic_update_index_in_dim)/broadcast_in_dim | solution.py:170
  313.6 7.3 %reshape.285 = bf16[16,2,24576]{2,1,0:T(2,128)(2,1)} reshape(bf16[4096,1,3,64]{3,2,1,0:T(4,128)(2,1)} %bitcast.194) | data formatting | bytes 3145728
  320.9 25.1 %all_to_all.79 = bf16[16,2,24576]{2,1,0:T(2,128)(2,1)} all-to-all(bf16[16,2,24576]{2,1,0:T(2,128)(2,1)} %reshape.285), channel_id=1, replica_groups=mesh['tile'=8,'seq'=16] {'seq'}, dimensions={0} | all-to-all | bytes 3145728 | tf_op jit(solution)/shard_map/all_to_all | solution.py:173
  345.9 7.1 %reshape.286 = bf16[4096,1,3,64]{3,2,1,0:T(4,128)(2,1)} reshape(bf16[16,2,24576]{2,1,0:T(2,128)(2,1)} %all_to_all.79) | data formatting | bytes 3145728
  353.0 6.6 %copy.91 = bf16[1,3,64,16,256]{4,2,1,3,0:T(8,128)(2,1)} copy(bf16[1,3,64,16,256]{2,1,4,3,0:T(4,128)(2,1)} %bitcast.192) | data formatting | bytes 3145728 | tf_op jit(solution)/shard_map/all_to_all | solution.py:173
  359.7 6.0 %multiply_convert_fusion.1 = bf16[16,3,64,1024]{3,2,1,0:T(8,128)(2,1)} fusion(bf16[1,3,64,16,256]{4,2,1,3,0:T(8,128)(2,1)} %copy.91, f32[1024]{0:T(1024)S(1)} %copy-done.18, f32[256]{0:T(256)S(1)} %copy-done.21, bf16[256,1024]{1,0:T(8,128)(2,1)S(1)} %copy-done.7, pred[256]{0:T(512)(128)(4,1)S(1)} %copy-done.16), kind=kOutput, calls=%fused_computation.34 | convolution fusion | flops 1618214912 | bytes 8393984 | tf_op jit(solution)/shard_map/hcet,td->hced/dot_general | solution.py:177
  367.0 5.4 %copy.90 = bf16[1,3,64,16,256]{4,3,2,1,0:T(8,128)(2,1)} copy(bf16[1,3,64,16,256]{2,1,4,3,0:T(4,128)(2,1)} %bitcast.193) | data formatting | bytes 3145728 | tf_op jit(solution)/shard_map/all_to_all | solution.py:173
  372.4 7.6 %fusion.63 = (f32[1024]{0:T(1024)S(1)}, f32[256]{0:T(256)S(1)}, f32[256,1024]{1,0:T(8,128)S(1)}) fusion(f32[256]{0:T(256)S(1)} %copy-done.21, bf16[256,1024]{1,0:T(8,128)(2,1)S(1)} %copy-done.7, pred[256]{0:T(512)(128)(4,1)S(1)} %copy-done.16, f32[1024]{0:T(1024)S(1)} %copy-done.18, bf16[16,3,64,1024]{3,2,1,0:T(8,128)(2,1)} %param.17, ...), kind=kOutput, calls=%fused_computation.69 | convolution fusion | flops 1612708608 | bytes 9447680 | tf_op jit(solution)/shard_map/hcet,hced->td/dot_general | solution.py:186
  380.5 2.8 gather_fusion.1
  390.2 4.6 all-to-all-start.5
  394.9 56.5 %reduce-scatter.17.cloned.1.call-done = bf16[1,3,64,1024]{3,2,1,0:T(8,128)(2,1)} async-done(((bf16[16,3,64,1024]{3,2,1,0:T(8,128)(2,1)}), bf16[1,3,64,1024]{3,2,1,0:T(8,128)(2,1)}) %reduce-scatter.17.cloned.1.call-update) | async-done | bytes 393232
  451.4 2.3 copy.92
  453.7 3.2 reshape.275
  456.9 3.5 fusion.50
  461.1 64.7 %all-reduce.2 = (f32[1024]{0:T(1024)}, f32[6,1024]{1,0:T(8,128)}) all-reduce(f32[1024]{0:T(1024)S(1)} %broadcast_multiply_fusion, f32[6,1024]{1,0:T(8,128)S(1)} %fusion.53), channel_id=1, replica_groups=mesh['tile'=8,'seq'=16] {'tile','seq'}, use_global_device_ids=true, to_apply=%region_14.15 | all-reduce | flops 7168 | bytes 57344 | tf_op jit(solution)/shard_map/psum | solution.py:204
  (188 shorter events, 78.9 us)
Async XLA Ops:
  7.2 51.3 %copy-start = (bf16[16,64,1024]{2,1,0:T(8,128)(2,1)S(1)}, bf16[16,64,1024]{2,1,0:T(8,128)(2,1)}, u32[]{:S(2)}) copy-start(bf16[16,64,1024]{2,1,0:T(8,128)(2,1)} %param.18) | copy-start | bytes 6291460
  8.0 0.6 copy-start.11
  12.4 30.3 %all-to-all-start = ((bf16[128,4,1024]{2,1,0:T(4,128)(2,1)}), bf16[128,4,1024]{2,1,0:T(4,128)(2,1)}, u32[]{:S(2)}, u32[]{:S(2)}) async-start(bf16[128,4,1024]{2,1,0:T(4,128)(2,1)} %copy.69), calls=%async_computation | async-start | bytes 2097152 | tf_op jit(solution)/shard_map/all_to_all | solution.py:121
  24.1 23.8 %copy-start.17 = (f32[1024]{0:T(1024)S(1)}, f32[1024]{0:T(1024)}, u32[]{:S(2)}) copy-start(f32[1024]{0:T(1024)} %param.16) | copy-start | bytes 12292
  25.9 0.5 copy-start.13
  26.6 27.4 %copy-start.15 = (pred[256]{0:T(512)(128)(4,1)}, pred[256]{0:T(512)(128)(4,1)S(1)}, u32[]{:S(2)}) copy-start(pred[256]{0:T(512)(128)(4,1)S(1)} %compare_and_fusion.1) | copy-start | bytes 772
  47.9 6.1 %copy-start.20 = (f32[256]{0:T(256)}, f32[256]{0:T(256)S(1)}, u32[]{:S(2)}) copy-start(f32[256]{0:T(256)S(1)} %get-tuple-element.298) | copy-start | bytes 3076
  47.9 10.5 %copy-start.9 = (bf16[1,256,1024]{2,1,0:T(8,128)(2,1)S(1)}, bf16[1,256,1024]{2,1,0:T(8,128)(2,1)}, u32[]{:S(2)}) copy-start(bf16[1,256,1024]{2,1,0:T(8,128)(2,1)} %param.19) | copy-start | bytes 1572868
  54.0 29.1 %all-to-all-start.1 = ((bf16[16,3,64,256]{3,2,1,0:T(8,128)(2,1)}), bf16[16,3,64,256]{3,2,1,0:T(8,128)(2,1)}, u32[]{:S(2)}, u32[]{:S(2)}) async-start(bf16[16,3,64,256]{3,2,1,0:T(8,128)(2,1)} %fusion.36), calls=%async_computation.1 | async-start | bytes 3145728 | tf_op jit(solution)/shard_map/all_to_all | solution.py:138
  83.1 86.4 %all-to-all-start.3 = ((bf16[16,64,256]{2,1,0:T(8,128)(2,1)}), bf16[16,64,256]{2,1,0:T(8,128)(2,1)}, u32[]{:S(2)}, u32[]{:S(2)}) async-start(bf16[16,64,256]{2,1,0:T(8,128)(2,1)} %convolution_convert_fusion.1), calls=%async_computation.3 | async-start | bytes 1048576 | tf_op jit(solution)/shard_map/all_to_all | solution.py:153
  132.0 37.5 %copy-start.3 = (bf16[64,4096]{1,0:T(8,128)(2,1)}, bf16[64,4096]{1,0:T(8,128)(2,1)S(1)}, u32[]{:S(2)}) copy-start(bf16[64,4096]{1,0:T(8,128)(2,1)S(1)} %get-tuple-element.448) | copy-start | bytes 1572868
  132.0 37.5 %copy-start.5 = (bf16[64,4096]{1,0:T(8,128)(2,1)}, bf16[64,4096]{1,0:T(8,128)(2,1)S(1)}, u32[]{:S(2)}) copy-start(bf16[64,4096]{1,0:T(8,128)(2,1)S(1)} %get-tuple-element.449) | copy-start | bytes 1572868
  169.5 17.5 %all-to-all-start.2 = ((bf16[16,2,8192]{2,1,0:T(2,128)(2,1)}), bf16[16,2,8192]{2,1,0:T(2,128)(2,1)}, u32[]{:S(2)}, u32[]{:S(2)}) async-start(bf16[16,2,8192]{2,1,0:T(2,128)(2,1)} %reshape.283), calls=%async_computation.2 | async-start | bytes 1048576 | tf_op jit(solution)/shard_map/all_to_all | solution.py:144
  176.8 207.9 %reduce-scatter.19.cloned.1.call-start = ((), (), s32[]{:S(2)}) async-start(), calls=%async_computation.13 | async-start | bytes 2228224
  198.9 0.8 copy-start.8
  202.9 248.5 %reduce-scatter.17.cloned.1.call-start = ((), (), s32[]{:S(2)}) async-start(), calls=%async_computation.12 | async-start | bytes 6684672
  203.8 3.8 copy-start.1
  207.6 1.9 copy-start.4
  209.5 2.3 copy-start.2
  209.5 2.3 copy-start.6
  215.7 3.8 copy-start.1
  219.5 1.9 copy-start.4
  221.4 2.3 copy-start.2
  221.4 2.3 copy-start.6
  227.6 3.8 copy-start.1
  231.4 1.9 copy-start.4
  233.4 2.3 copy-start.2
  233.4 2.3 copy-start.6
  239.6 3.8 copy-start.1
  243.4 1.9 copy-start.4
  245.3 2.3 copy-start.2
  245.3 2.3 copy-start.6
  251.5 3.8 copy-start.1
  255.3 1.9 copy-start.4
  257.3 2.3 copy-start.2
  257.3 2.3 copy-start.6
  263.4 3.8 copy-start.1
  267.2 1.9 copy-start.4
  269.2 2.3 copy-start.2
  269.2 2.3 copy-start.6
  275.4 3.8 copy-start.1
  279.2 1.9 copy-start.4
  281.1 2.3 copy-start.2
  281.1 2.3 copy-start.6
  287.3 3.8 copy-start.1
  291.1 1.9 copy-start.4
  293.0 2.3 copy-start.2
  293.0 2.3 copy-start.6
  353.0 6.6 %copy-start.7 = (bf16[256,1024]{1,0:T(8,128)(2,1)S(1)}, bf16[256,1024]{1,0:T(8,128)(2,1)}, u32[]{:S(2)}) copy-start(bf16[256,1024]{1,0:T(8,128)(2,1)} %gather_fusion) | copy-start | bytes 1572868
  353.0 6.6 %copy-start.16 = (pred[256]{0:T(512)(128)(4,1)S(1)}, pred[256]{0:T(512)(128)(4,1)}, u32[]{:S(2)}) copy-start(pred[256]{0:T(512)(128)(4,1)} %copy-done.15) | copy-start | bytes 772
  353.0 6.6 %copy-start.18 = (f32[1024]{0:T(1024)S(1)}, f32[1024]{0:T(1024)}, u32[]{:S(2)}) copy-start(f32[1024]{0:T(1024)} %param.16) | copy-start | bytes 12292
  353.0 6.6 %copy-start.21 = (f32[256]{0:T(256)S(1)}, f32[256]{0:T(256)}, u32[]{:S(2)}) copy-start(f32[256]{0:T(256)} %copy-done.20) | copy-start | bytes 3076
  365.7 1.0 copy-start.14
  365.7 160.2 %reduce-scatter.15.cloned.1.call-start = ((), (), s32[]{:S(2)}) async-start(), calls=%async_computation.11 | async-start | bytes 294912
  372.4 7.6 %copy-start.10 = (bf16[1,256,1024]{2,1,0:T(8,128)(2,1)S(1)}, bf16[1,256,1024]{2,1,0:T(8,128)(2,1)}, u32[]{:S(2)}) copy-start(bf16[1,256,1024]{2,1,0:T(8,128)(2,1)} %param.19) | copy-start | bytes 1572868
  372.4 7.7 %copy-start.19 = (f32[256]{0:T(256)S(1)}, f32[256]{0:T(256)}, u32[]{:S(2)}) copy-start(f32[256]{0:T(256)} %get-tuple-element.297) | copy-start | bytes 3076
  390.2 70.3 %all-to-all-start.5 = ((bf16[128,4,1024]{2,1,0:T(4,128)(2,1)}), bf16[128,4,1024]{2,1,0:T(4,128)(2,1)S(1)}, u32[]{:S(2)}, u32[]{:S(2)}) async-start(bf16[128,4,1024]{2,1,0:T(4,128)(2,1)} %select_select_fusion), calls=%async_computation.5 | async-start | bytes 2097152 | tf_op jit(solution)/shard_map/all_to_all | solution.py:199
  394.8 132.6 %reduce-scatter.13.cloned.1.call-start = ((), (), s32[]{:S(2)}) async-start(), calls=%async_computation.10 | async-start | bytes 589824
  456.9 3.9 copy-start.12
Sparse Core Ops, SparseCore 0:
  203.0 70.3 reduce-scatter.18
  365.8 85.5 reduce-scatter.16
  453.9 29.7 reduce-scatter.14
  486.0 29.7 reduce-scatter.12
where the time goes:
time: 547 us; the launch traced here: 537 us
  matrix products  165 us (30%)
  waiting for transfers between devices  99.5 us (18%)
  local copies, waits for them, and re-layouts  99.2 us (18%)
  blocking collectives  89.8 us (16%)
  other arithmetic  34.9 us (6%)
  starting transfers between devices  33.3 us (6%)
  between operations  14.4 us (3%)
    psum x1, blocking collectives, on_device(): gain_grad, table_grad = lax.psum((gain_term, table_term), ('tile', 'seq'))  64.7 us
    unnamed x8, waiting for transfers between devices  56.6 us
    unnamed x53, local copies, waits for them, and re-layouts  40.8 us
    dot_general x8, matrix products, one_block(): lax.dot_general(values, weights, (((1,), (1,)), ((), ())), preferred_elem...  40.4 us
    dot_general x8, matrix products, one_block(): lax.dot_general(rows, keys, (((0,), (0,)), ((), ())), preferred_element_t...  30.1 us
    all_to_all x1, blocking collectives, on_device(): lax.all_to_all(grad_head_major, 'seq', split_axis=3, concat_axis=0, tiled...  25.1 us
    unnamed x3, other arithmetic  24.4 us
    all_to_all x1, waiting for transfers between devices, on_device(): lax.all_to_all(projected, 'seq', split_axis=0, concat_axis=3, tiled=True)  23.1 us
  transfers between devices with their start and end apart: 9, of which 4 were waited for; matrix products, arithmetic and copies ran while one was open for 49% of the time, Pallas kernels for 0%

commit v1 on v0

v1 whole, which is shorter than its diff:
```python
import functools
import math

import jax
import jax.numpy as jnp
from jax import lax
from jax.experimental import pallas as pl
from jax.experimental.pallas import tpu as pltpu
from jax.sharding import PartitionSpec as P

EPSILON = 1e-05
BF16 = jnp.bfloat16
F32 = jnp.float32
MIB = 2**20
LANES = 128


def dot(a, b, ca, cb):
    return lax.dot_general(a, b, (((ca,), (cb,)), ((), ())), preferred_element_type=F32)


def whole(shape):
    zeros = (0,) * len(shape)
    return pl.BlockSpec(shape, lambda i: zeros)


def vmem(mib):
    return pltpu.CompilerParams(vmem_limit_bytes=mib * MIB)


def pack_positions(counts, rows, slots):
    starts = jnp.cumsum(counts) - counts
    place = jnp.arange(rows, dtype=jnp.int32)
    before = (starts[None, :] <= place[:, None]).astype(jnp.int32)
    owner = jnp.sum(before, axis=1) - 1
    first = jnp.max(jnp.where(before > 0, starts[None, :], 0), axis=1)
    return owner * slots + place - first


def project_body(
    received, place, gain, cotangent, weight, out_weight, packed, features, level, normed, heads
):
    rows, width = features.shape

    @pl.when(pl.program_id(0) == 0)
    def _():
        slot = lax.broadcasted_iota(jnp.int32, (rows, received.shape[0]), 1)
        pick = jnp.where(slot == place[...], 1.0, 0.0).astype(BF16)
        taken = dot(pick, received[...], 1, 0)
        active = taken[:, :width]
        features[...] = active.astype(BF16)
        level[...] = taken[:, width:].astype(BF16)
        inverse = lax.rsqrt(jnp.mean(active * active, axis=1, keepdims=True) + EPSILON)
        normed[...] = (active * inverse * gain[...]).astype(BF16)

    size = out_weight.shape[1]
    for h in range(heads):
        packed[h, : 3 * size, :] = dot(weight[h], normed[...], 1, 1).astype(BF16)
        packed[h, 3 * size :, :] = dot(out_weight[h], cotangent[...], 1, 1).astype(BF16)


def project(received, place, gain, cotangent, weight, out_weight):
    rows, width = cotangent.shape
    count, three, _ = weight.shape
    size = out_weight.shape[1]
    heads = 2
    return pl.pallas_call(
        functools.partial(project_body, heads=heads),
        grid=(count // heads,),
        in_specs=[
            whole(received.shape),
            whole((rows, 1)),
            whole((1, width)),
            whole((rows, width)),
            pl.BlockSpec((heads, three, width), lambda i: (i, 0, 0)),
            pl.BlockSpec((heads, size, width), lambda i: (i, 0, 0)),
        ],
        out_specs=[
            pl.BlockSpec((heads, three + size, rows), lambda i: (i, 0, 0)),
            whole((rows, width)),
            whole((rows, LANES)),
            whole((rows, width)),
        ],
        out_shape=[
            jax.ShapeDtypeStruct((count, three + size, rows), BF16),
            jax.ShapeDtypeStruct((rows, width), BF16),
            jax.ShapeDtypeStruct((rows, LANES), BF16),
            jax.ShapeDtypeStruct((rows, width), BF16),
        ],
        compiler_params=vmem(40),
        name="project",
    )(received, place, gain, cotangent, weight, out_weight)


def attend_body(
    packed, out, query, grad, keys, values, key_total, value_total, *, scale, shift, step
):
    shards, four, rows = packed.shape
    size = four // 4
    length = shards * rows
    rate = scale * math.log2(math.e)
    offset = shift * math.log2(math.e)
    for s in range(shards):
        part = slice(s * rows, (s + 1) * rows)
        query[part, :] = jnp.transpose(packed[s, :size, :])
        grad[part, :] = jnp.transpose(packed[s, 3 * size :, :])
        keys[:, part] = packed[s, size : 2 * size, :]
        values[:, part] = packed[s, 2 * size : 3 * size, :]
    key_total[...] = jnp.zeros_like(key_total)
    value_total[...] = jnp.zeros_like(value_total)

    def one_block(i, _):
        mine = pl.ds(pl.multiple_of(i * rows, rows), rows)
        q, g = query[mine, :], grad[mine, :]
        q_across, g_across = packed[i, :size, :], packed[i, 3 * size :, :]

        attended = jnp.zeros((size, rows), F32)
        grad_query = jnp.zeros((size, rows), F32)
        for j in range(length // step):
            part = slice(j * step, (j + 1) * step)
            k, v = keys[:, part], values[:, part]
            odds = jnp.exp2(offset - dot(q, k, 1, 0) * rate)
            probs = pl.reciprocal(1.0 + odds, approx=True)
            weights = probs.astype(BF16)
            slope = probs - probs * probs
            grad_scores = (dot(g, v, 1, 0) * slope).astype(BF16)
            attended = attended + dot(v, weights, 1, 1)
            grad_query = grad_query + dot(k, grad_scores, 1, 1)
            key_total[:, part] += dot(q_across, grad_scores, 1, 0)
            value_total[:, part] += dot(g_across, weights, 1, 0)
        out[i, :size, :] = attended.astype(BF16)
        out[i, size : 2 * size, :] = (grad_query * scale).astype(BF16)
        return 0

    lax.fori_loop(0, shards, one_block, 0)
    for s in range(shards):
        part = slice(s * rows, (s + 1) * rows)
        out[s, 2 * size : 3 * size, :] = (key_total[:, part] * scale).astype(BF16)
        out[s, 3 * size :, :] = value_total[:, part].astype(BF16)


def attend(packed, scale, shift):
    shards, four, rows = packed.shape
    size, length = four // 4, shards * rows
    return pl.pallas_call(
        functools.partial(attend_body, scale=scale, shift=shift, step=min(1024, length)),
        in_specs=[pl.BlockSpec(memory_space=pltpu.VMEM)],
        out_specs=pl.BlockSpec(memory_space=pltpu.VMEM),
        out_shape=jax.ShapeDtypeStruct(packed.shape, BF16),
        scratch_shapes=[
            pltpu.VMEM((length, size), BF16),
            pltpu.VMEM((length, size), BF16),
            pltpu.VMEM((size, length), BF16),
            pltpu.VMEM((size, length), BF16),
            pltpu.VMEM((size, length), F32),
            pltpu.VMEM((size, length), F32),
        ],
        compiler_params=vmem(48),
        cost_estimate=pl.CostEstimate(
            flops=48 * length * length * size, bytes_accessed=8 * length * size, transcendentals=0
        ),
        name="attend",
    )(packed)


def weight_grad_body(mixed, cotangent, normed, out, total, *, factor):
    shard = pl.program_id(0)
    size = mixed.shape[1] // 4

    @pl.when(shard == 0)
    def _():
        total[...] = jnp.zeros_like(total)

    total[:size, :] += dot(mixed[0, :size, :], cotangent[...], 1, 0)
    total[size:, :] += dot(mixed[0, size:, :], normed[...], 1, 0)

    @pl.when(shard == pl.num_programs(0) - 1)
    def _():
        tiles, _, part = out.shape
        for r in range(tiles):
            out[r] = (total[:, r * part : (r + 1) * part] * factor).astype(BF16)


def weight_grad(mixed, cotangent, normed, tiles, factor):
    shards, four, rows = mixed.shape
    width = normed.shape[1]
    shape = (tiles, four, width // tiles)
    return pl.pallas_call(
        functools.partial(weight_grad_body, factor=factor),
        grid=(shards,),
        in_specs=[
            pl.BlockSpec((1, four, rows), lambda i: (i, 0, 0)),
            pl.BlockSpec((rows, width), lambda i: (i, 0)),
            pl.BlockSpec((rows, width), lambda i: (i, 0)),
        ],
        out_specs=whole(shape),
        out_shape=jax.ShapeDtypeStruct(shape, BF16),
        scratch_shapes=[pltpu.VMEM((four, width), F32)],
        compiler_params=vmem(32),
        name="weight_grad",
    )(mixed, cotangent, normed)


def finish_body(
    mixed,
    weight,
    out_weight,
    features,
    normed_gain,
    cotangent,
    level,
    place,
    output,
    outgoing,
    small,
    out_total,
    grad_total,
    *,
    heads,
    factor,
):
    size = out_weight.shape[1]
    index = pl.program_id(0)

    @pl.when(index == 0)
    def _():
        out_total[...] = jnp.zeros_like(out_total)
        grad_total[...] = jnp.zeros_like(grad_total)

    attended = jnp.concatenate([mixed[h, :size, :] for h in range(heads)], axis=0)
    grads = jnp.concatenate([mixed[h, size:, :] for h in range(heads)], axis=0)
    out_total[...] += dot(attended, out_weight[...].reshape(heads * size, -1), 0, 0)
    grad_total[...] += dot(grads, weight[...].reshape(heads * 3 * size, -1), 0, 0)

    @pl.when(index == pl.num_programs(0) - 1)
    def _():
        rows, _ = features.shape
        active = features[...].astype(F32)
        output[...] = (active + out_total[...]).astype(BF16)
        inverse = lax.rsqrt(jnp.mean(active * active, axis=1, keepdims=True) + EPSILON)
        grad_normed = grad_total[...]
        scaled = normed_gain[...] * grad_normed
        cubed = inverse * inverse * inverse
        grad_active = inverse * scaled - active * cubed * jnp.mean(
            active * scaled, axis=1, keepdims=True
        )
        grad_features = (cotangent[...].astype(F32) + grad_active).astype(BF16)
        slot = lax.broadcasted_iota(jnp.int32, (outgoing.shape[0], rows), 0)
        pick = jnp.where(slot == place[...], 1.0, 0.0).astype(BF16)
        outgoing[...] = dot(pick, grad_features, 1, 0).astype(BF16)
        table = dot(level[...], grad_features, 0, 0)
        gain = jnp.sum(grad_normed * active * inverse, axis=0, keepdims=True)
        line = lax.broadcasted_iota(jnp.int32, small.shape, 0)
        small[...] = jnp.where(line == small.shape[0] - 1, gain, table[: small.shape[0]]) * factor


def finish(mixed, weight, out_weight, features, gain, cotangent, level, place, slots, factor):
    count, four, rows = mixed.shape
    width = features.shape[1]
    size = four // 4
    heads = 4
    return pl.pallas_call(
        functools.partial(finish_body, heads=heads, factor=factor),
        grid=(count // heads,),
        in_specs=[
            pl.BlockSpec((heads, four, rows), lambda i: (i, 0, 0)),
            pl.BlockSpec((heads, 3 * size, width), lambda i: (i, 0, 0)),
            pl.BlockSpec((heads, size, width), lambda i: (i, 0, 0)),
            whole((rows, width)),
            whole((1, width)),
            whole((rows, width)),
            whole((rows, LANES)),
            whole((1, rows)),
        ],
        out_specs=[whole((rows, width)), whole((slots, width)), whole((8, width))],
        out_shape=[
            jax.ShapeDtypeStruct((rows, width), BF16),
            jax.ShapeDtypeStruct((slots, width), BF16),
            jax.ShapeDtypeStruct((8, width), F32),
        ],
        scratch_shapes=[pltpu.VMEM((rows, width), F32), pltpu.VMEM((rows, width), F32)],
        compiler_params=vmem(40),
        name="finish",
    )(mixed, weight, out_weight, features, gain, cotangent, level, place)


def sum_all(value, axes):
    for axis in axes:
        count = lax.axis_size(axis)
        reach = 1
        while reach < count:
            value = value + lax.ppermute(value, axis, [(i, i ^ reach) for i in range(count)])
            reach *= 2
    return value


def on_device(
    tokens, levels, counts, level_table, norm_gain, project_weight, output_weight, cotangent
):
    tiles = lax.axis_size("tile")
    shards = lax.axis_size("seq")
    tile_index = lax.axis_index("tile")
    shard_index = lax.axis_index("seq")
    owners = tiles * shards
    slots = tokens.shape[3]
    width = tokens.shape[4]
    rows = cotangent.shape[1]
    length = rows * shards
    count, _, size, _ = project_weight.shape
    scale = 1.0 / math.sqrt(size)
    shift = math.log(length)
    factor = 1.0 / math.sqrt(tiles * length)
    kinds = level_table.shape[0]

    grad_rows = cotangent[0]
    all_grad_rows = lax.all_gather(grad_rows, "seq", tiled=True)

    me = tile_index * shards + shard_index
    my_counts = lax.dynamic_index_in_dim(counts, me, 2, keepdims=False)
    used = jnp.arange(slots, dtype=jnp.int32) < my_counts[..., None]
    onehot = (levels[0][..., None] == jnp.arange(LANES, dtype=jnp.int32)).astype(BF16)
    embedded = tokens[0].astype(F32) + jnp.einsum(
        "msjl,ld->msjd", onehot[..., :kinds], level_table, preferred_element_type=F32
    )
    embedded = jnp.concatenate([embedded.astype(BF16), onehot], axis=-1)
    embedded = jnp.where(used[..., None], embedded, jnp.zeros((), BF16))
    received = lax.all_to_all(
        embedded.reshape(owners, slots, width + LANES),
        ("tile", "seq"),
        split_axis=0,
        concat_axis=0,
        tiled=True,
    )
    map_counts = lax.dynamic_index_in_dim(counts, tile_index, 0, keepdims=False)
    own_counts = lax.dynamic_index_in_dim(map_counts, shard_index, 0, keepdims=False)
    place = pack_positions(own_counts, rows, slots)
    gain = norm_gain.reshape(1, width)
    weight = project_weight.reshape(count, 3 * size, width)

    packed, features, level, normed = project(
        received.reshape(owners * slots, width + LANES),
        place.reshape(rows, 1),
        gain,
        grad_rows,
        weight,
        output_weight,
    )
    by_head = lax.all_to_all(packed, "seq", split_axis=0, concat_axis=0, tiled=True)
    all_normed = lax.all_gather(normed, "seq", tiled=True)
    attended = attend(by_head, scale, shift)
    mixed = lax.all_to_all(attended, "seq", split_axis=0, concat_axis=0, tiled=True)
    shares = weight_grad(attended, all_grad_rows, all_normed, tiles, factor)
    output, outgoing, small = finish(
        mixed,
        weight,
        output_weight,
        features,
        gain,
        grad_rows,
        level,
        place.reshape(1, rows),
        owners * slots,
        factor,
    )
    returned = lax.all_to_all(
        outgoing.reshape(owners, slots, width),
        ("tile", "seq"),
        split_axis=0,
        concat_axis=0,
        tiled=True,
    )
    token_grad = returned.reshape(tiles, shards, slots, width)
    shares = lax.all_to_all(shares, "tile", split_axis=0, concat_axis=0, tiled=True)
    shares = jnp.sum(shares.astype(F32), axis=0)
    small = sum_all(small, ("tile", "seq"))
    return (
        output[None],
        token_grad[None],
        shares[size:].reshape(1, 3, size, width // tiles),
        shares[:size].reshape(1, size, width // tiles),
        small[7],
        small[:kinds],
    )


def solution(mesh):
    return jax.shard_map(
        on_device,
        mesh=mesh,
        in_specs=(
            P(("tile", "seq"), None, None, None, None),
            P(("tile", "seq"), None, None, None),
            P(),
            P(),
            P(),
            P(),
            P(),
            P("tile", "seq", None),
        ),
        out_specs=(
            P("tile", "seq", None),
            P(("tile", "seq"), None, None, None, None),
            P("seq", None, None, "tile"),
            P("seq", None, "tile"),
            P(),
            P(),
        ),
        check_vma=False,
    )
```

time: 547 us -> 304 us (0.56); the launches traced: 537 us -> 303 us
  matrix products: 165 us -> 1.87 us
  Pallas kernels: 0 us -> 79.8 us
  local copies, waits for them, and re-layouts: 99.2 us -> 30.6 us
  blocking collectives: 89.8 us -> 49.1 us
  other arithmetic: 34.9 us -> 1.01 us
  waiting for transfers between devices: 99.5 us -> 87.5 us
    dot_general x56 -> x1, matrix products: 165 us -> 1.87 us  [on_device(): jnp.einsum('msjl,ld->msjd', onehot[..., :kinds], level_table, preferred_e...]
    pallas_call x0 -> x4, Pallas kernels: none -> 79.8 us  [the longest x1 56.3 us: attend(): pl.pallas_call(functools.partial(attend_body, scale=scale, shift=shift, s...]
    psum x1 -> x0, blocking collectives: 64.7 us -> none  [on_device(): gain_grad, table_grad = lax.psum((gain_term, table_term), ('tile', 'seq'))]
    unnamed x8 -> x2, waiting for transfers between devices: 56.6 us -> 0.7 us
    unnamed x3 -> x0, other arithmetic: 24.4 us -> none
    all_to_all x1, blocking collectives: 25.1 us -> 49.1 us  [on_device(): lax.all_to_all(packed, 'seq', split_axis=0, concat_axis=0, tiled=True)]
    all_to_all x5 -> x4, waiting for transfers between devices: 42.9 us -> 66.7 us  [the longest x1 40 us: on_device(): lax.all_to_all(attended, 'seq', split_axis=0, concat_axis=0, tiled=True)]
    all_to_all x7 -> x0, local copies, waits for them, and re-layouts: 21.3 us -> none  [the longest x2 12 us: on_device(): lax.all_to_all(grad_head_major, 'seq', split_axis=3, concat_axis=0, tiled...]
  transfers between devices with their start and end apart: 9 -> 13, of which waited for: 4 -> 10; matrix products, arithmetic and copies ran while one was open for 49% -> 4% of each run, Pallas kernels for 0% -> 26%
where the time goes in v1:
time: 304 us; the launch traced here: 303 us
  waiting for transfers between devices  87.5 us (29%)
  Pallas kernels  79.8 us (26%)
  blocking collectives  49.1 us (16%)
  starting transfers between devices  38.4 us (13%)
  local copies, waits for them, and re-layouts  30.6 us (10%)
  between operations  14.3 us (5%)
    pallas_call x1, Pallas kernels, attend(): pl.pallas_call(functools.partial(attend_body, scale=scale, shift=shift, s...  56.3 us
    all_to_all x1, blocking collectives, on_device(): lax.all_to_all(packed, 'seq', split_axis=0, concat_axis=0, tiled=True)  49.1 us
    all_to_all x1, waiting for transfers between devices, on_device(): lax.all_to_all(attended, 'seq', split_axis=0, concat_axis=0, tiled=True)  40 us
    all_to_all x1, waiting for transfers between devices, on_device(): lax.all_to_all(embedded.reshape(owners, slots, width + LANES), ('tile', '...  26.2 us
    unnamed x36, local copies, waits for them, and re-layouts  21.3 us
    ppermute x7, waiting for transfers between devices, sum_all(): lax.ppermute(value, axis, [(i, i ^ reach) for i in range(count)])  20.1 us
    ppermute x7, starting transfers between devices, sum_all(): lax.ppermute(value, axis, [(i, i ^ reach) for i in range(count)])  13.5 us
    pallas_call x1, Pallas kernels, weight_grad(): pl.pallas_call(functools.partial(weight_grad_body, factor=factor), grid=(...  11.6 us
  transfers between devices with their start and end apart: 13, of which 10 were waited for; matrix products, arithmetic and copies ran while one was open for 4% of the time, Pallas kernels for 26%

profile of v1, /device:TPU:0, one launch (start us, length us, event | category | flops | bytes accessed | tf_op | source)
XLA Modules:
  0.0 302.6 jit_solution(17875449251868162329)
XLA Ops:
  7.2 0.0 all-gather.6.cloned.1.call-start
  7.2 0.7 all-gather.6.cloned.1.call-update
  7.9 0.7 copy.39
  8.6 0.1 eq.28
  8.7 1.9 fusion
  10.6 0.1 copy.38
  10.7 0.3 dynamic-slice_reduce_fusion
  11.0 0.1 lt.33
  11.1 0.1 fusion.1
  11.3 0.3 maximum_select_fusion
  11.5 1.9 copy.40
  13.5 11.6 %all-to-all-start = ((bf16[128,4,1152]{2,1,0:T(4,128)(2,1)}), bf16[128,4,1152]{2,1,0:T(4,128)(2,1)}, u32[]{:S(2)}, u32[]{:S(2)}) async-start(bf16[128,4,1152]{2,1,0:T(4,128)(2,1)} %copy.40), calls=%async_computation | async-start | bytes 2359296 | tf_op jit(solution)/shard_map/all_to_all | solution.py:327
  25.1 0.0 all-gather.4.cloned.1.call-start
  25.2 0.1 copy.41
  25.3 0.2 reduce-window.8
  25.5 0.1 reduce.1
  25.6 0.2 select_reduce_fusion
  25.8 0.1 copy.42
  25.9 0.1 copy.43
  26.1 26.2 %all-to-all-done = bf16[128,4,1152]{2,1,0:T(4,128)(2,1)} async-done(((bf16[128,4,1152]{2,1,0:T(4,128)(2,1)}), bf16[128,4,1152]{2,1,0:T(4,128)(2,1)}, u32[]{:S(2)}, u32[]{:S(2)}) %all-to-all-start) | async-done | bytes 1179680 | tf_op jit(solution)/shard_map/all_to_all | solution.py:327
  52.3 2.4 reshape.140.received
  54.8 3.5 %copy-done.1 = bf16[16,3,64,1024]{3,2,1,0:T(8,128)(2,1)S(1)} copy-done((bf16[16,3,64,1024]{3,2,1,0:T(8,128)(2,1)S(1)}, bf16[16,3,64,1024]{3,2,1,0:T(8,128)(2,1)}, u32[]{:S(2)}) %copy-start.1) | copy-done | bytes 6291480
  58.2 1.0 copy-done.7
  59.3 6.9 %project.1 = (bf16[16,256,256]{2,1,0:T(8,128)(2,1)S(1)}, bf16[256,1024]{1,0:T(8,128)(2,1)S(1)}, bf16[256,128]{1,0:T(8,128)(2,1)S(1)}, bf16[256,1024]{1,0:T(8,128)(2,1)S(1)}) custom-call(bf16[512,1152]{1,0:T(8,128)(2,1)S(1)} %reshape.140.received, s32[256,1]{1,0:T(8,128)S(1)} %sub.32.place, f32[1,1024]{1,0:T(1,128)S(1)} %bitcast.38, ...), custom_call_target="tpu_custom_call" | custom-call | tf_op jit(solution)/shard_map/project/pallas_call | solution.py:67
  66.2 1.3 copy-done.9
  67.6 0.8 copy-done.11
  68.4 0.8 copy-done.13
  69.1 0.0 all-gather.4.cloned.1.call-update
  69.2 49.1 %all_to_all.25.packed = bf16[16,256,256]{2,1,0:T(8,128)(2,1)S(1)} all-to-all(bf16[16,256,256]{2,1,0:T(8,128)(2,1)} %copy-done.9), channel_id=1, replica_groups=mesh['tile'=8,'seq'=16] {'seq'}, dimensions={0} | all-to-all | bytes 4194304 | tf_op jit(solution)/shard_map/all_to_all | solution.py:348
  118.3 56.3 %attend.1.mixed = bf16[16,256,256]{2,1,0:T(8,128)(2,1)} custom-call(bf16[16,256,256]{2,1,0:T(8,128)(2,1)S(1)} %all_to_all.25.packed), custom_call_target="tpu_custom_call" | custom-call | flops 51539607552 | bytes 2097152 | tf_op jit(solution)/shard_map/attend/pallas_call | solution.py:145
  174.6 3.8 %all-to-all-start.2 = ((bf16[16,256,256]{2,1,0:T(8,128)(2,1)}), bf16[16,256,256]{2,1,0:T(8,128)(2,1)S(1)}, u32[]{:S(2)}, u32[]{:S(2)}) async-start(bf16[16,256,256]{2,1,0:T(8,128)(2,1)} %attend.1.mixed), calls=%async_computation.2 | async-start | bytes 4194304 | tf_op jit(solution)/shard_map/all_to_all | solution.py:351
  178.5 40.0 %all-to-all-done.2.mixed = bf16[16,256,256]{2,1,0:T(8,128)(2,1)S(1)} async-done(((bf16[16,256,256]{2,1,0:T(8,128)(2,1)}), bf16[16,256,256]{2,1,0:T(8,128)(2,1)S(1)}, u32[]{:S(2)}, u32[]{:S(2)}) %all-to-all-start.2) | async-done | bytes 2097184 | tf_op jit(solution)/shard_map/all_to_all | solution.py:351
  218.5 2.8 copy-done.2
  221.3 1.6 copy-done.6
  222.9 4.9 %finish.1 = (bf16[256,1024]{1,0:T(8,128)(2,1)}, bf16[512,1024]{1,0:T(8,128)(2,1)S(1)}, f32[8,1024]{1,0:T(8,128)S(1)}) custom-call(bf16[16,256,256]{2,1,0:T(8,128)(2,1)S(1)} %all-to-all-done.2.mixed, bf16[16,192,1024]{2,1,0:T(8,128)(2,1)S(1)} %bitcast.34, bf16[16,64,1024]{2,1,0:T(8,128)(2,1)S(1)} %copy-done.6, bf16[256,1024]{1,0:T(8,128)(2,1)S(1)} %copy-done.12, ...), custom_call_target="tpu_custom_call" | custom-call | tf_op jit(solution)/shard_map/finish/pallas_call | solution.py:262
  227.8 1.0 copy-done.10
  228.8 2.2 reshape.146
  231.0 5.8 %all-to-all-start.3 = ((bf16[128,4,1024]{2,1,0:T(4,128)(2,1)}), bf16[128,4,1024]{2,1,0:T(4,128)(2,1)S(1)}, u32[]{:S(2)}, u32[]{:S(2)}) async-start(bf16[128,4,1024]{2,1,0:T(4,128)(2,1)} %reshape.146), calls=%async_computation.3 | async-start | bytes 2097152 | tf_op jit(solution)/shard_map/all_to_all | solution.py:365
  236.9 0.0 all-gather.6.cloned.1.call-done
  236.9 0.0 all-gather.4.cloned.1.call-done.normed
  236.9 3.4 %copy-done.3 = bf16[1,4096,1024]{2,1,0:T(8,128)(2,1)S(1)} copy-done((bf16[1,4096,1024]{2,1,0:T(8,128)(2,1)S(1)}, bf16[1,4096,1024]{2,1,0:T(8,128)(2,1)}, u32[]{:S(2)}) %copy-start.3) | copy-done | bytes 8388632
  240.3 3.4 %copy-done.4 = bf16[4096,1024]{1,0:T(8,128)(2,1)S(1)} copy-done((bf16[4096,1024]{1,0:T(8,128)(2,1)S(1)}, bf16[4096,1024]{1,0:T(8,128)(2,1)}, u32[]{:S(2)}) %copy-start.4) | copy-done | bytes 8388632
  243.7 11.6 %weight_grad.1 = bf16[8,256,128]{2,1,0:T(8,128)(2,1)} custom-call(bf16[16,256,256]{2,1,0:T(8,128)(2,1)} %attend.1.mixed, bf16[4096,1024]{1,0:T(8,128)(2,1)S(1)} %bitcast.35, bf16[4096,1024]{1,0:T(8,128)(2,1)S(1)} %copy-done.4), custom_call_target="tpu_custom_call" | custom-call | tf_op jit(solution)/shard_map/weight_grad/pallas_call | solution.py:188
  255.3 0.4 all-to-all-done.3
  255.7 3.5 %all-to-all-start.4 = ((bf16[8,256,128]{2,1,0:T(8,128)(2,1)}), bf16[8,256,128]{2,1,0:T(8,128)(2,1)S(1)}, u32[]{:S(2)}, u32[]{:S(2)}) async-start(bf16[8,256,128]{2,1,0:T(8,128)(2,1)} %weight_grad.1), calls=%async_computation.4 | async-start | bytes 1048576 | tf_op jit(solution)/shard_map/all_to_all | solution.py:373
  259.2 0.4 collective-permute-start
  259.6 0.9 collective-permute-done
  260.5 1.8 collective-permute-start.1
  262.4 6.3 %collective-permute-done.1 = f32[8,1024]{1,0:T(8,128)S(1)} collective-permute-done((f32[8,1024]{1,0:T(8,128)S(1)}, f32[8,1024]{1,0:T(8,128)S(1)}, u32[]{:S(2)}, u32[]{:S(2)}) %collective-permute-start.1) | collective-permute-done | bytes 32800 | tf_op jit(solution)/shard_map/ppermute | solution.py:292
  268.7 2.7 collective-permute-start.2
  271.4 2.7 collective-permute-done.2
  274.1 1.2 collective-permute-start.3
  275.3 2.7 collective-permute-done.3
  278.0 2.7 collective-permute-start.4
  280.8 2.7 collective-permute-done.4
  283.5 1.5 collective-permute-start.5
  284.9 2.5 collective-permute-done.5
  287.5 3.1 %collective-permute-start.6 = (f32[8,1024]{1,0:T(8,128)S(1)}, f32[8,1024]{1,0:T(8,128)S(1)}, u32[]{:S(2)}, u32[]{:S(2)}) collective-permute-start(f32[8,1024]{1,0:T(8,128)S(1)} %add.90), channel_id=1, source_target_pairs={{0,8},{1,9},{2,10},{3,11},{4,12},{5,13},{6,14},{7,15},{8,0},{9,1},... | collective-permute-start | bytes 98312 | tf_op jit(solution)/shard_map/ppermute | solution.py:292
  290.6 2.3 collective-permute-done.6
  292.9 0.6 slice.22
  293.5 0.1 convert_reduce_fusion
  293.6 0.6 slice.20
  294.2 0.6 slice_bitcast_fusion
  294.8 1.0 copy.47
  (39 shorter events, 0.2 us)
Async XLA Ops:
  7.2 1.6 copy-start
  7.2 229.7 %all-gather.6.cloned.1.call-start = ((), (), s32[]{:S(2)}) async-start(), calls=%async_computation.6 | async-start | bytes 8912896 | tf_op jit(solution)/shard_map/all_gather | solution.py:316
  8.7 2.0 copy-start.15
  13.5 38.9 %all-to-all-start = ((bf16[128,4,1152]{2,1,0:T(4,128)(2,1)}), bf16[128,4,1152]{2,1,0:T(4,128)(2,1)}, u32[]{:S(2)}, u32[]{:S(2)}) async-start(bf16[128,4,1152]{2,1,0:T(4,128)(2,1)} %copy.40), calls=%async_computation | async-start | bytes 2359296 | tf_op jit(solution)/shard_map/all_to_all | solution.py:327
  25.1 29.6 %copy-start.5 = (bf16[16,64,1024]{2,1,0:T(8,128)(2,1)S(1)}, bf16[16,64,1024]{2,1,0:T(8,128)(2,1)}, u32[]{:S(2)}) copy-start(bf16[16,64,1024]{2,1,0:T(8,128)(2,1)} %out_weight.3) | copy-start | bytes 6291460
  25.1 29.6 %copy-start.14 = (f32[1024]{0:T(1024)S(1)}, f32[1024]{0:T(1024)}, u32[]{:S(2)}) copy-start(f32[1024]{0:T(1024)} %param.12) | copy-start | bytes 12292
  25.1 211.8 %all-gather.4.cloned.1.call-start = ((), (), s32[]{:S(2)}) async-start(), calls=%async_computation.5 | async-start | bytes 8912896 | tf_op jit(solution)/shard_map/all_gather | solution.py:349
  54.7 3.5 %copy-start.1 = (bf16[16,3,64,1024]{3,2,1,0:T(8,128)(2,1)S(1)}, bf16[16,3,64,1024]{3,2,1,0:T(8,128)(2,1)}, u32[]{:S(2)}) copy-start(bf16[16,3,64,1024]{3,2,1,0:T(8,128)(2,1)} %param.13) | copy-start | bytes 18874372
  58.2 1.0 copy-start.7
  66.2 1.3 copy-start.9
  67.6 0.8 copy-start.11
  68.4 0.8 copy-start.13
  174.6 43.9 %copy-start.8 = (bf16[1,256,1024]{2,1,0:T(8,128)(2,1)S(1)}, bf16[1,256,1024]{2,1,0:T(8,128)(2,1)}, u32[]{:S(2)}) copy-start(bf16[1,256,1024]{2,1,0:T(8,128)(2,1)} %param.15) | copy-start | bytes 1572868
  174.6 43.9 %copy-start.12 = (bf16[256,1024]{1,0:T(8,128)(2,1)S(1)}, bf16[256,1024]{1,0:T(8,128)(2,1)}, u32[]{:S(2)}) copy-start(bf16[256,1024]{1,0:T(8,128)(2,1)} %copy-done.11) | copy-start | bytes 1572868
  174.6 43.9 %all-to-all-start.2 = ((bf16[16,256,256]{2,1,0:T(8,128)(2,1)}), bf16[16,256,256]{2,1,0:T(8,128)(2,1)S(1)}, u32[]{:S(2)}, u32[]{:S(2)}) async-start(bf16[16,256,256]{2,1,0:T(8,128)(2,1)} %attend.1.mixed), calls=%async_computation.2 | async-start | bytes 4194304 | tf_op jit(solution)/shard_map/all_to_all | solution.py:351
  218.5 2.8 copy-start.2
  221.3 1.6 copy-start.6
  227.8 1.0 copy-start.10
  231.0 24.7 %all-to-all-start.3 = ((bf16[128,4,1024]{2,1,0:T(4,128)(2,1)}), bf16[128,4,1024]{2,1,0:T(4,128)(2,1)S(1)}, u32[]{:S(2)}, u32[]{:S(2)}) async-start(bf16[128,4,1024]{2,1,0:T(4,128)(2,1)} %reshape.146), calls=%async_computation.3 | async-start | bytes 2097152 | tf_op jit(solution)/shard_map/all_to_all | solution.py:365
  236.9 3.4 %copy-start.3 = (bf16[1,4096,1024]{2,1,0:T(8,128)(2,1)S(1)}, bf16[1,4096,1024]{2,1,0:T(8,128)(2,1)}, u32[]{:S(2)}) copy-start(bf16[1,4096,1024]{2,1,0:T(8,128)(2,1)} %all-gather.6.cloned.1.call-done) | copy-start | bytes 25165828
  240.3 3.4 %copy-start.4 = (bf16[4096,1024]{1,0:T(8,128)(2,1)S(1)}, bf16[4096,1024]{1,0:T(8,128)(2,1)}, u32[]{:S(2)}) copy-start(bf16[4096,1024]{1,0:T(8,128)(2,1)} %all-gather.4.cloned.1.call-done.normed) | copy-start | bytes 25165828
  255.7 37.8 %all-to-all-start.4 = ((bf16[8,256,128]{2,1,0:T(8,128)(2,1)}), bf16[8,256,128]{2,1,0:T(8,128)(2,1)S(1)}, u32[]{:S(2)}, u32[]{:S(2)}) async-start(bf16[8,256,128]{2,1,0:T(8,128)(2,1)} %weight_grad.1), calls=%async_computation.4 | async-start | bytes 1048576 | tf_op jit(solution)/shard_map/all_to_all | solution.py:373
  259.2 1.3 collective-permute-start
  260.5 8.2 %collective-permute-start.1 = (f32[8,1024]{1,0:T(8,128)S(1)}, f32[8,1024]{1,0:T(8,128)S(1)}, u32[]{:S(2)}, u32[]{:S(2)}) collective-permute-start(f32[8,1024]{1,0:T(8,128)S(1)} %add.85), channel_id=1, source_target_pairs={{0,32},{16,48},{32,0},{48,16},{64,96},{80,112},{96,64},{112,80},{1... | collective-permute-start | bytes 98312 | tf_op jit(solution)/shard_map/ppermute | solution.py:292
  268.7 5.4 %collective-permute-start.2 = (f32[8,1024]{1,0:T(8,128)S(1)}, f32[8,1024]{1,0:T(8,128)S(1)}, u32[]{:S(2)}, u32[]{:S(2)}) collective-permute-start(f32[8,1024]{1,0:T(8,128)S(1)} %add.86), channel_id=1, source_target_pairs={{0,64},{16,80},{32,96},{48,112},{64,0},{80,16},{96,32},{112,48},{1... | collective-permute-start | bytes 98312 | tf_op jit(solution)/shard_map/ppermute | solution.py:292
  274.1 3.9 %collective-permute-start.3 = (f32[8,1024]{1,0:T(8,128)S(1)}, f32[8,1024]{1,0:T(8,128)S(1)}, u32[]{:S(2)}, u32[]{:S(2)}) collective-permute-start(f32[8,1024]{1,0:T(8,128)S(1)} %add.87), channel_id=1, source_target_pairs={{0,1},{1,0},{2,3},{3,2},{4,5},{5,4},{6,7},{7,6},{8,9},{9,8},{10,11... | collective-permute-start | bytes 98312 | tf_op jit(solution)/shard_map/ppermute | solution.py:292
  278.0 5.4 %collective-permute-start.4 = (f32[8,1024]{1,0:T(8,128)S(1)}, f32[8,1024]{1,0:T(8,128)S(1)}, u32[]{:S(2)}, u32[]{:S(2)}) collective-permute-start(f32[8,1024]{1,0:T(8,128)S(1)} %add.88), channel_id=1, source_target_pairs={{0,2},{1,3},{2,0},{3,1},{4,6},{5,7},{6,4},{7,5},{8,10},{9,11},{10,... | collective-permute-start | bytes 98312 | tf_op jit(solution)/shard_map/ppermute | solution.py:292
  283.5 4.0 %collective-permute-start.5 = (f32[8,1024]{1,0:T(8,128)S(1)}, f32[8,1024]{1,0:T(8,128)S(1)}, u32[]{:S(2)}, u32[]{:S(2)}) collective-permute-start(f32[8,1024]{1,0:T(8,128)S(1)} %add.89), channel_id=1, source_target_pairs={{0,4},{1,5},{2,6},{3,7},{4,0},{5,1},{6,2},{7,3},{8,12},{9,13},{10,... | collective-permute-start | bytes 98312 | tf_op jit(solution)/shard_map/ppermute | solution.py:292
  287.5 5.4 %collective-permute-start.6 = (f32[8,1024]{1,0:T(8,128)S(1)}, f32[8,1024]{1,0:T(8,128)S(1)}, u32[]{:S(2)}, u32[]{:S(2)}) collective-permute-start(f32[8,1024]{1,0:T(8,128)S(1)} %add.90), channel_id=1, source_target_pairs={{0,8},{1,9},{2,10},{3,11},{4,12},{5,13},{6,14},{7,15},{8,0},{9,1},... | collective-permute-start | bytes 98312 | tf_op jit(solution)/shard_map/ppermute | solution.py:292
  292.9 2.9 copy-start.16
Sparse Core Ops, SparseCore 0:
  10.2 105.5 all-gather.5
  117.9 92.1 all-gather.3

commit v2 on v1

--- a/solution.py
+++ b/solution.py
@@ -13,6 +13,7 @@
 F32 = jnp.float32
 MIB = 2**20
 LANES = 128
+LINES = 8
 
 
 def dot(a, b, ca, cb):
@@ -38,7 +39,7 @@
 
 
 def project_body(
-    received, place, gain, cotangent, weight, out_weight, packed, features, level, normed, heads
+    received, place, gain, cotangent, weight, out_weight, packed, features, normed, local, heads
 ):
     rows, width = features.shape
 
@@ -49,21 +50,28 @@
         taken = dot(pick, received[...], 1, 0)
         active = taken[:, :width]
         features[...] = active.astype(BF16)
-        level[...] = taken[:, width:].astype(BF16)
+        level = taken[:, width:]
         inverse = lax.rsqrt(jnp.mean(active * active, axis=1, keepdims=True) + EPSILON)
-        normed[...] = (active * inverse * gain[...]).astype(BF16)
+        normed[:rows, :] = (active * inverse * gain[...]).astype(BF16)
+        kept = jnp.transpose(level * inverse)[:LINES]
+        kept = jnp.concatenate([kept, kept - kept.astype(BF16).astype(F32)], axis=0)
+        normed[rows:, :rows] = kept.astype(BF16)
+        normed[rows:, rows:] = jnp.zeros((2 * LINES, width - rows), BF16)
+        local[...] = dot(level.astype(BF16), cotangent[...], 0, 0)[:LINES]
 
     size = out_weight.shape[1]
-    for h in range(heads):
-        packed[h, : 3 * size, :] = dot(weight[h], normed[...], 1, 1).astype(BF16)
-        packed[h, 3 * size :, :] = dot(out_weight[h], cotangent[...], 1, 1).astype(BF16)
+    rows, width = features.shape
+    projected = dot(weight[...].reshape(heads * 3 * size, width), normed[:rows, :], 1, 1)
+    grads = dot(out_weight[...].reshape(heads * size, width), cotangent[...], 1, 1)
+    packed[:, : 3 * size, :] = projected.astype(BF16).reshape(heads, 3 * size, rows)
+    packed[:, 3 * size :, :] = grads.astype(BF16).reshape(heads, size, rows)
 
 
 def project(received, place, gain, cotangent, weight, out_weight):
     rows, width = cotangent.shape
     count, three, _ = weight.shape
     size = out_weight.shape[1]
-    heads = 2
+    heads = 4
     return pl.pallas_call(
         functools.partial(project_body, heads=heads),
         grid=(count // heads,),
@@ -78,16 +86,16 @@
         out_specs=[
             pl.BlockSpec((heads, three + size, rows), lambda i: (i, 0, 0)),
             whole((rows, width)),
-            whole((rows, LANES)),
-            whole((rows, width)),
+            whole((rows + 2 * LINES, width)),
+            whole((LINES, width)),
         ],
         out_shape=[
             jax.ShapeDtypeStruct((count, three + size, rows), BF16),
             jax.ShapeDtypeStruct((rows, width), BF16),
-            jax.ShapeDtypeStruct((rows, LANES), BF16),
-            jax.ShapeDtypeStruct((rows, width), BF16),
-        ],
-        compiler_params=vmem(40),
+            jax.ShapeDtypeStruct((rows + 2 * LINES, width), BF16),
+            jax.ShapeDtypeStruct((LINES, width), F32),
+        ],
+        compiler_params=vmem(60),
         name="project",
     )(received, place, gain, cotangent, weight, out_weight)
 
@@ -163,42 +171,145 @@
     )(packed)
 
 
-def weight_grad_body(mixed, cotangent, normed, out, total, *, factor):
-    shard = pl.program_id(0)
-    size = mixed.shape[1] // 4
-
-    @pl.when(shard == 0)
+def weight_grad_body(
+    head,
+    mixed,
+    projected,
+    normed,
+    weight,
+    gain,
+    local,
+    out,
+    attended,
+    small,
+    total,
+    by_level,
+    *,
+    factor,
+):
+    del head
+    step = pl.program_id(0)
+    rows = mixed.shape[2]
+    first = mixed.shape[1] // 4
+    width = normed.shape[2]
+
+    @pl.when(step == 0)
     def _():
         total[...] = jnp.zeros_like(total)
-
-    total[:size, :] += dot(mixed[0, :size, :], cotangent[...], 1, 0)
-    total[size:, :] += dot(mixed[0, size:, :], normed[...], 1, 0)
-
-    @pl.when(shard == pl.num_programs(0) - 1)
+        by_level[...] = jnp.zeros_like(by_level)
+
+    attended[...] = mixed[:, :first, :]
+    for s in range(mixed.shape[0]):
+        grads = mixed[s, first:, :]
+        features = normed[s, :rows, :]
+        level = normed[s, rows:, :rows].astype(F32)
+        level = level[:LINES] + level[LINES:]
+        by_level[...] += dot(level.astype(BF16), grads, 1, 1)
+        along = jnp.sum(
+            grads.astype(F32) * projected[s, : 3 * first, :].astype(F32), axis=0, keepdims=True
+        )
+        drift = level * (along * (1.0 / width))
+        drift = jnp.concatenate([drift, jnp.zeros_like(drift)], axis=0).astype(BF16)
+        total[...] += dot(jnp.concatenate([grads, drift], axis=0), features, 1, 0)
+
+    @pl.when(step == pl.num_programs(0) - 1)
     def _():
         tiles, _, part = out.shape
         for r in range(tiles):
-            out[r] = (total[:, r * part : (r + 1) * part] * factor).astype(BF16)
-
-
-def weight_grad(mixed, cotangent, normed, tiles, factor):
+            out[r] = (total[: 3 * first, r * part : (r + 1) * part] * factor).astype(BF16)
+        scale = gain[...]
+        drift = total[3 * first : 3 * first + LINES, :] / scale
+        table = dot(by_level[...].astype(BF16), weight[0], 1, 0) * scale - drift
+        table = table + local[...]
+        for_gain = weight[0].astype(F32) * total[: 3 * first, :]
+        for_gain = jnp.sum(for_gain, axis=0, keepdims=True) / scale
+        line = lax.broadcasted_iota(jnp.int32, table.shape, 0)
+        both = jnp.where(line == LINES - 1, for_gain, table) * factor
+        for c in range(width // LANES):
+            small[c * LINES : (c + 1) * LINES, :] = both[:, c * LANES : (c + 1) * LANES]
+
+
+def weight_grad(head, mixed, projected, normed, weight, gain, local, tiles, factor):
     shards, four, rows = mixed.shape
-    width = normed.shape[1]
-    shape = (tiles, four, width // tiles)
+    width = normed.shape[-1]
+    first = four // 4
+    lines = four - first
+    each = 2
+    shape = (tiles, lines, width // tiles)
+    small = (width // LANES * LINES, LANES)
+
+    def by_step(shape):
+        return pl.BlockSpec((each,) + shape[1:], lambda i, h: (i, 0, 0))
+
+    def fixed(shape):
+        zeros = (0,) * len(shape)
+        return pl.BlockSpec(shape, lambda i, h: zeros)
+
     return pl.pallas_call(
         functools.partial(weight_grad_body, factor=factor),
-        grid=(shards,),
-        in_specs=[
-            pl.BlockSpec((1, four, rows), lambda i: (i, 0, 0)),
-            pl.BlockSpec((rows, width), lambda i: (i, 0)),
-            pl.BlockSpec((rows, width), lambda i: (i, 0)),
-        ],
-        out_specs=whole(shape),
+        grid_spec=pltpu.PrefetchScalarGridSpec(
+            num_scalar_prefetch=1,
+            grid=(shards // each,),
+            in_specs=[by_step(part.shape) for part in (mixed, projected, normed)]
+            + [
+                pl.BlockSpec((1, lines, width), lambda i, h: (h[0], 0, 0)),
+                fixed(gain.shape),
+                fixed(local.shape),
+            ],
+            out_specs=[fixed(shape), by_step((shards, first, rows)), fixed(small)],
+            scratch_shapes=[
+                pltpu.VMEM((lines + 2 * LINES, width), F32),
+                pltpu.VMEM((LINES, lines), F32),
+            ],
+        ),
+        out_shape=[
+            jax.ShapeDtypeStruct(shape, BF16),
+            jax.ShapeDtypeStruct((shards, first, rows), BF16),
+            jax.ShapeDtypeStruct(small, F32),
+        ],
+        compiler_params=vmem(60),
+        cost_estimate=pl.CostEstimate(flops=1, bytes_accessed=1, transcendentals=0),
+        name="weight_grad",
+    )(head, mixed, projected, normed, weight, gain, local)
+
+
+def out_grad_body(column, small, *refs, factor):
+    out = refs[-1]
+    ways = out.shape[0]
+    attended, cotangents = refs[:ways], refs[ways : 2 * ways]
+    shards, size, _ = attended[0].shape
+    total = 0.0
+    for k, cotangent in enumerate(cotangents):
+        s = (column[0] + shards - k) % shards
+        rows = jnp.concatenate([part[s] for part in attended], axis=0)
+        total = total + dot(rows, cotangent[...], 1, 0)
+    total = (total * factor).astype(BF16)
+    tiles = total.shape[1] // LANES
+    high = small[...].astype(BF16)
+    low = (small[...] - high.astype(F32)).astype(BF16)
+    for h in range(ways):
+        for r in range(tiles):
+            out[h, r * size : (r + 1) * size, :] = total[
+                h * size : (h + 1) * size, r * LANES : (r + 1) * LANES
+            ]
+        out[h, tiles * size : tiles * size + high.shape[0], :] = high
+        out[h, tiles * size + high.shape[0] :, :] = low
+
+
+def out_grad(column, small, attended, cotangents, factor):
+    _, size, _ = attended[0].shape
+    tiles = cotangents[0].shape[-1] // LANES
+    shape = (len(attended), tiles * size + 2 * small.shape[0], LANES)
+    return pl.pallas_call(
+        functools.partial(out_grad_body, factor=factor),
+        in_specs=[pl.BlockSpec(memory_space=pltpu.SMEM)]
+        + [pl.BlockSpec(memory_space=pltpu.VMEM)] * (1 + len(attended) + len(cotangents)),
+        out_specs=pl.BlockSpec(memory_space=pltpu.VMEM),
         out_shape=jax.ShapeDtypeStruct(shape, BF16),
-        scratch_shapes=[pltpu.VMEM((four, width), F32)],
-        compiler_params=vmem(32),
-        name="weight_grad",
-    )(mixed, cotangent, normed)
+        compiler_params=vmem(48),
+        cost_estimate=pl.CostEstimate(flops=1, bytes_accessed=1, transcendentals=0),
+        name="out_grad",
+    )(column, small, *attended, *cotangents)
 
 
 def finish_body(
@@ -208,16 +319,13 @@
     features,
     normed_gain,
     cotangent,
-    level,
     place,
     output,
     outgoing,
-    small,
     out_total,
     grad_total,
     *,
     heads,
-    factor,
 ):
     size = out_weight.shape[1]
     index = pl.program_id(0)
@@ -248,19 +356,15 @@
         slot = lax.broadcasted_iota(jnp.int32, (outgoing.shape[0], rows), 0)
         pick = jnp.where(slot == place[...], 1.0, 0.0).astype(BF16)
         outgoing[...] = dot(pick, grad_features, 1, 0).astype(BF16)
-        table = dot(level[...], grad_features, 0, 0)
-        gain = jnp.sum(grad_normed * active * inverse, axis=0, keepdims=True)
-        line = lax.broadcasted_iota(jnp.int32, small.shape, 0)
-        small[...] = jnp.where(line == small.shape[0] - 1, gain, table[: small.shape[0]]) * factor
-
-
-def finish(mixed, weight, out_weight, features, gain, cotangent, level, place, slots, factor):
+
+
+def finish(mixed, weight, out_weight, features, gain, cotangent, place, slots):
     count, four, rows = mixed.shape
     width = features.shape[1]
     size = four // 4
     heads = 4
     return pl.pallas_call(
-        functools.partial(finish_body, heads=heads, factor=factor),
+        functools.partial(finish_body, heads=heads),
         grid=(count // heads,),
         in_specs=[
             pl.BlockSpec((heads, four, rows), lambda i: (i, 0, 0)),
@@ -269,29 +373,46 @@
             whole((rows, width)),
             whole((1, width)),
             whole((rows, width)),
-            whole((rows, LANES)),
             whole((1, rows)),
         ],
-        out_specs=[whole((rows, width)), whole((slots, width)), whole((8, width))],
+        out_specs=[whole((rows, width)), whole((slots, width))],
         out_shape=[
             jax.ShapeDtypeStruct((rows, width), BF16),
             jax.ShapeDtypeStruct((slots, width), BF16),
-            jax.ShapeDtypeStruct((8, width), F32),
         ],
         scratch_shapes=[pltpu.VMEM((rows, width), F32), pltpu.VMEM((rows, width), F32)],
-        compiler_params=vmem(40),
+        compiler_params=vmem(60),
         name="finish",
-    )(mixed, weight, out_weight, features, gain, cotangent, level, place)
-
-
-def sum_all(value, axes):
-    for axis in axes:
-        count = lax.axis_size(axis)
-        reach = 1
-        while reach < count:
-            value = value + lax.ppermute(value, axis, [(i, i ^ reach) for i in range(count)])
-            reach *= 2
-    return value
+    )(mixed, weight, out_weight, features, gain, cotangent, place)
+
+
+def pick(value, k, axis=0):
+    return lax.dynamic_index_in_dim(value, k, axis, keepdims=False)
+
+
+def sum_to_tiles(value, small, tile_index):
+    tiles, lines, lanes = value.shape
+    ways = tiles // 2
+    core, place = tile_index % 2, tile_index // 2
+    value = value.reshape(ways, 2, lines, lanes)
+
+    def mine(k):
+        return pick(value, k, 1).reshape(ways * lines, lanes)
+
+    other = jnp.concatenate([mine(1 - core), small], axis=0)
+    other = lax.ppermute(other, "tile", [(i, i ^ 1) for i in range(tiles)])
+    both = jnp.concatenate([mine(core), small], axis=0) + other
+    value, small = both[: ways * lines].reshape(ways, lines, lanes), both[ways * lines :]
+    parts = [jnp.concatenate([pick(value, place), small], axis=0)] + [
+        lax.ppermute(
+            jnp.concatenate([pick(value, (place + k) % ways), small], axis=0),
+            "tile",
+            [(i, (i + 2 * k) % tiles) for i in range(tiles)],
+        )
+        for k in range(1, ways)
+    ]
+    both = sum(parts[1:], parts[0])
+    return both[:lines], both[lines:]
 
 
 def on_device(
@@ -313,7 +434,16 @@
     kinds = level_table.shape[0]
 
     grad_rows = cotangent[0]
-    all_grad_rows = lax.all_gather(grad_rows, "seq", tiled=True)
+    side = math.isqrt(shards)
+    line, column = shard_index // side, shard_index % side
+
+    def along_line(value, k):
+        return lax.ppermute(
+            value, "seq", [(i, i // side * side + (i + k) % side) for i in range(shards)]
+        )
+
+    def along_column(value, k):
+        return lax.ppermute(value, "seq", [(i, (i + k * side) % shards) for i in range(shards)])
 
     me = tile_index * shards + shard_index
     my_counts = lax.dynamic_index_in_dim(counts, me, 2, keepdims=False)
@@ -337,7 +467,7 @@
     gain = norm_gain.reshape(1, width)
     weight = project_weight.reshape(count, 3 * size, width)
 
-    packed, features, level, normed = project(
+    packed, features, normed, local = project(
         received.reshape(owners * slots, width + LANES),
         place.reshape(rows, 1),
         gain,
@@ -346,21 +476,43 @@
         output_weight,
     )
     by_head = lax.all_to_all(packed, "seq", split_axis=0, concat_axis=0, tiled=True)
-    all_normed = lax.all_gather(normed, "seq", tiled=True)
+    all_normed = lax.all_gather(normed, "seq")
+    by_head, line_rows = lax.optimization_barrier((by_head, grad_rows))
+    line_rows = [line_rows] + [along_line(line_rows, k) for k in range(1, side)]
     attended = attend(by_head, scale, shift)
+    attended, line_rows = lax.optimization_barrier((attended, line_rows))
     mixed = lax.all_to_all(attended, "seq", split_axis=0, concat_axis=0, tiled=True)
-    shares = weight_grad(attended, all_grad_rows, all_normed, tiles, factor)
-    output, outgoing, small = finish(
+
+    shares, head_attended, small = weight_grad(
+        shard_index.reshape(1),
+        attended,
+        by_head,
+        all_normed,
+        weight,
+        gain,
+        local,
+        tiles,
+        factor,
+    )
+    head_attended = head_attended.reshape(side, side, size, rows)
+    column_attended = [pick(head_attended, line)] + [
+        along_column(pick(head_attended, (line + k) % side), k) for k in range(1, side)
+    ]
+    out_shares = out_grad(column.reshape(1), small, column_attended, line_rows, factor)
+    out_shares = sum(
+        [along_column(out_shares[k], -k).astype(F32) for k in range(1, side)],
+        out_shares[0].astype(F32),
+    )
+    mixed, out_shares, shares = lax.optimization_barrier((mixed, out_shares, shares))
+    output, outgoing = finish(
         mixed,
         weight,
         output_weight,
         features,
         gain,
         grad_rows,
-        level,
         place.reshape(1, rows),
         owners * slots,
-        factor,
     )
     returned = lax.all_to_all(
         outgoing.reshape(owners, slots, width),
@@ -370,15 +522,20 @@
         tiled=True,
     )
     token_grad = returned.reshape(tiles, shards, slots, width)
-    shares = lax.all_to_all(shares, "tile", split_axis=0, concat_axis=0, tiled=True)
-    shares = jnp.sum(shares.astype(F32), axis=0)
-    small = sum_all(small, ("tile", "seq"))
+    lines = tiles * size
+    small_lines = (out_shares.shape[0] - lines) // 2
+    small = out_shares[lines : lines + small_lines] + out_shares[lines + small_lines :]
+    out_shares = out_shares[:lines].reshape(tiles, size, LANES)
+    shares = jnp.concatenate([out_shares, shares.astype(F32)], axis=1)
+    shares, small = sum_to_tiles(shares, small, tile_index)
+    small = sum([along_line(small, k) for k in range(1, side)], small)
+    small = small.reshape(width // LANES, LINES, LANES).transpose(1, 0, 2).reshape(LINES, width)
     return (
         output[None],
         token_grad[None],
         shares[size:].reshape(1, 3, size, width // tiles),
         shares[:size].reshape(1, size, width // tiles),
-        small[7],
+        small[LINES - 1],
         small[:kinds],
     )
 

time: 304 us -> 258 us (0.85)
  waiting for transfers between devices: 87.5 us -> 52.5 us
  local copies, waits for them, and re-layouts: 30.6 us -> 15 us
  blocking collectives: 49.1 us -> 40.9 us
  starting transfers between devices: 38.4 us -> 45 us
  Pallas kernels: 79.8 us -> 83.5 us
    all_to_all x1, waiting for transfers between devices: 40 us -> 0.01 us  [on_device(): lax.all_to_all(attended, 'seq', split_axis=0, concat_axis=0, tiled=True)]
    unnamed x36 -> x22, local copies, waits for them, and re-layouts: 21.3 us -> 4.7 us
    ppermute x7 -> x16, waiting for transfers between devices: 20.1 us -> 33.2 us  [the longest x6 21.8 us: along_column(): lax.ppermute(value, 'seq', [(i, (i + k * side) % shards) for i in range(s...]
    all_to_all x1, waiting for transfers between devices: 26.2 us -> 17.4 us  [on_device(): lax.all_to_all(embedded.reshape(owners, slots, width + LANES), ('tile', '...]
    all_to_all x1, blocking collectives: 49.1 us -> 40.9 us  [on_device(): lax.all_to_all(packed, 'seq', split_axis=0, concat_axis=0, tiled=True)]
    ppermute x7 -> x16, starting transfers between devices: 13.5 us -> 21.1 us  [the longest x6 8.57 us: along_line(): lax.ppermute(value, 'seq', [(i, i // side * side + (i + k) % side) for i...]
    all_to_all x1 -> x0, starting transfers between devices: 3.49 us -> none  [on_device(): lax.all_to_all(shares, 'tile', split_axis=0, concat_axis=0, tiled=True)]
    pallas_call x2 -> x3, Pallas kernels: 16.6 us -> 19.3 us  [the longest x1 9.8 us: weight_grad(): pl.pallas_call(functools.partial(weight_grad_body, factor=factor), grid_s...]
  transfers between devices with their start and end apart: 13 -> 20, of which waited for: 10 -> 10; matrix products, arithmetic and copies ran while one was open for 4% -> 4% of each run, Pallas kernels for 26% -> 29%
where the time goes in v2:
time: 258 us; the launch traced here: 257 us
  Pallas kernels  83.5 us (32%)
  waiting for transfers between devices  52.5 us (20%)
  starting transfers between devices  45 us (17%)
  blocking collectives  40.9 us (16%)
  local copies, waits for them, and re-layouts  15 us (6%)
  between operations  14.6 us (6%)
  other arithmetic  3.82 us (1%)
    pallas_call x1, Pallas kernels, attend(): pl.pallas_call(functools.partial(attend_body, scale=scale, shift=shift, s...  56.3 us
    all_to_all x1, blocking collectives, on_device(): lax.all_to_all(packed, 'seq', split_axis=0, concat_axis=0, tiled=True)  40.9 us
    ppermute x6, waiting for transfers between devices, along_column(): lax.ppermute(value, 'seq', [(i, (i + k * side) % shards) for i in range(s...  21.8 us
    all_to_all x1, waiting for transfers between devices, on_device(): lax.all_to_all(embedded.reshape(owners, slots, width + LANES), ('tile', '...  17.4 us
    all_to_all x1, starting transfers between devices, on_device(): lax.all_to_all(embedded.reshape(owners, slots, width + LANES), ('tile', '...  11.1 us
    pallas_call x1, Pallas kernels, weight_grad(): pl.pallas_call(functools.partial(weight_grad_body, factor=factor), grid_s...  9.8 us
    ppermute x6, waiting for transfers between devices, along_line(): lax.ppermute(value, 'seq', [(i, i // side * side + (i + k) % side) for i...  9.55 us
    pallas_call x1, Pallas kernels, finish(): pl.pallas_call(functools.partial(finish_body, heads=heads), grid=(count /...  8.81 us
  transfers between devices with their start and end apart: 20, of which 10 were waited for; matrix products, arithmetic and copies ran while one was open for 4% of the time, Pallas kernels for 29%

profile of v2, /device:TPU:0, one launch (start us, length us, event | category | flops | bytes accessed | tf_op | source)
XLA Modules:
  0.0 257.2 jit_solution(17366319497929245424)
XLA Ops:
  7.2 1.1 dynamic-slice_reduce_fusion
  8.3 0.1 lt.100
  8.4 0.7 copy.43
  9.1 1.8 fusion
  11.0 0.1 copy.42
  11.2 0.1 fusion.6
  11.3 0.3 maximum_select_fusion
  11.6 1.9 copy.44
  13.5 11.1 %all-to-all-start = ((bf16[128,4,1152]{2,1,0:T(4,128)(2,1)}), bf16[128,4,1152]{2,1,0:T(4,128)(2,1)S(1)}, u32[]{:S(2)}, u32[]{:S(2)}) async-start(bf16[128,4,1152]{2,1,0:T(4,128)(2,1)} %copy.44), calls=%async_computation | async-start | bytes 2359296 | tf_op jit(solution)/shard_map/all_to_all | solution.py:457
  24.8 0.7 fusion.14
  25.4 0.1 copy.45
  25.6 0.2 reduce-window.8
  25.7 0.1 reduce.1
  25.8 0.7 bitcast_subtract_fusion
  26.5 0.2 select_reduce_fusion
  26.7 0.1 copy.46
  26.9 0.1 copy.47
  27.0 0.7 sub.42.place
  27.7 17.4 %all-to-all-done = bf16[128,4,1152]{2,1,0:T(4,128)(2,1)S(1)} async-done(((bf16[128,4,1152]{2,1,0:T(4,128)(2,1)}), bf16[128,4,1152]{2,1,0:T(4,128)(2,1)S(1)}, u32[]{:S(2)}, u32[]{:S(2)}) %all-to-all-start) | async-done | bytes 1179680 | tf_op jit(solution)/shard_map/all_to_all | solution.py:457
  45.1 1.2 reshape.175.received
  46.3 7.9 %project.1 = (bf16[16,256,256]{2,1,0:T(8,128)(2,1)}, bf16[256,1024]{1,0:T(8,128)(2,1)}, bf16[272,1024]{1,0:T(8,128)(2,1)}, f32[8,1024]{1,0:T(8,128)}) custom-call(bf16[512,1152]{1,0:T(8,128)(2,1)} %reshape.175.received, s32[256,1]{1,0:T(8,128)} %sub.42.place, f32[1,1024]{1,0:T(1,128)} %bitcast.101, bf16[256,1024]{1,0:T(8,128)(2,1)} %bitcast.79, ...), custom_call_target="tpu_custom_call" | custom-call | tf_op jit(solution)/shard_map/project/pallas_call | solution.py:75
  54.2 40.9 %all_to_all.20.packed.projected = bf16[16,256,256]{2,1,0:T(8,128)(2,1)S(1)} all-to-all(bf16[16,256,256]{2,1,0:T(8,128)(2,1)} %get-tuple-element.25), channel_id=1, replica_groups=mesh['tile'=8,'seq'=16] {'seq'}, dimensions={0} | all-to-all | bytes 4194304 | tf_op jit(solution)/shard_map/all_to_all | solution.py:478
  95.1 0.6 collective-permute-start
  95.7 1.2 collective-permute-start.1
  96.8 1.7 collective-permute-start.2
  98.5 56.3 %attend.1.mixed = bf16[16,256,256]{2,1,0:T(8,128)(2,1)} custom-call(bf16[16,256,256]{2,1,0:T(8,128)(2,1)S(1)} %all_to_all.20.packed.projected), custom_call_target="tpu_custom_call" | custom-call | flops 51539607552 | bytes 2097152 | tf_op jit(solution)/shard_map/attend/pallas_call | solution.py:153
  154.8 0.8 copy-done.3
  155.6 0.8 copy-done.5
  156.4 4.5 %all-to-all-start.2 = ((bf16[16,256,256]{2,1,0:T(8,128)(2,1)}), bf16[16,256,256]{2,1,0:T(8,128)(2,1)}, u32[]{:S(2)}, u32[]{:S(2)}) async-start(bf16[16,256,256]{2,1,0:T(8,128)(2,1)} %attend.1.mixed), calls=%async_computation.2 | async-start | bytes 4194304 | tf_op jit(solution)/shard_map/all_to_all | solution.py:484
  161.0 9.8 %weight_grad.1 = (bf16[8,192,128]{2,1,0:T(8,128)(2,1)}, bf16[16,64,256]{2,1,0:T(8,128)(2,1)}, f32[64,128]{1,0:T(8,128)}) custom-call(s32[1]{0:T(128)} %bitcast.13.head, bf16[16,256,256]{2,1,0:T(8,128)(2,1)} %attend.1.mixed, bf16[16,256,256]{2,1,0:T(8,128)(2,1)} %copy-done.1, bf16[16,272,1024]{2,1,0:T(8,128)(2,1)} %bitcast.88, ...), custom_call_target="tpu_custom_call" | custom-call | flops 1 | bytes 1 | tf_op jit(solution)/shard_map/weight_grad/pallas_call | solution.py:248
  170.8 1.1 dynamic-slice_bitcast_fusion.4
  171.9 1.9 collective-permute-start.3
  173.8 2.7 %collective-permute-start.4 = (bf16[4,64,256]{2,1,0:T(8,128)(2,1)S(1)}, bf16[4,64,256]{2,1,0:T(8,128)(2,1)S(1)}, u32[]{:S(2)}, u32[]{:S(2)}) collective-permute-start(bf16[4,64,256]{2,1,0:T(8,128)(2,1)S(1)} %get-tuple-element.56), channel_id=1, source_target_pairs={{0,8},{1,9},{2,10},{3,11},{4,12},{5,13},{6,14},{7,15},{8,0},{9,1},... | collective-permute-start | bytes 393224 | tf_op jit(solution)/shard_map/ppermute | solution.py:446
  176.5 1.5 collective-permute-start.5
  177.9 9.6 %collective-permute-done.3.refs_1_ = bf16[4,64,256]{2,1,0:T(8,128)(2,1)S(1)} collective-permute-done((bf16[4,64,256]{2,1,0:T(8,128)(2,1)S(1)}, bf16[4,64,256]{2,1,0:T(8,128)(2,1)S(1)}, u32[]{:S(2)}, u32[]{:S(2)}) %collective-permute-start.3) | collective-permute-done | bytes 131104 | tf_op jit(solution)/shard_map/ppermute | solution.py:446
  187.5 3.4 %collective-permute-done.4.refs_2_ = bf16[4,64,256]{2,1,0:T(8,128)(2,1)S(1)} collective-permute-done((bf16[4,64,256]{2,1,0:T(8,128)(2,1)S(1)}, bf16[4,64,256]{2,1,0:T(8,128)(2,1)S(1)}, u32[]{:S(2)}, u32[]{:S(2)}) %collective-permute-start.4) | collective-permute-done | bytes 131104 | tf_op jit(solution)/shard_map/ppermute | solution.py:446
  190.9 0.7 copy-done.7
  191.7 0.7 out_grad.1
  192.5 0.4 collective-permute-start.6
  192.8 1.9 collective-permute-start.7
  194.7 0.3 collective-permute-start.8
  195.0 5.1 %collective-permute-done.6 = bf16[640,128]{1,0:T(8,128)(2,1)S(1)} collective-permute-done((bf16[640,128]{1,0:T(8,128)(2,1)S(1)}, bf16[640,128]{1,0:T(8,128)(2,1)S(1)}, u32[]{:S(2)}, u32[]{:S(2)}) %collective-permute-start.6) | collective-permute-done | bytes 163872 | tf_op jit(solution)/shard_map/ppermute | solution.py:446
  200.1 1.4 collective-permute-done.7
  201.4 2.3 collective-permute-done.8
  204.1 0.1 collective-permute-start.9
  204.3 1.9 collective-permute-done.9
  206.4 0.6 collective-permute-start.10
  206.9 2.0 collective-permute-start.11
  208.9 1.4 collective-permute-start.12
  210.3 0.6 add_subtract_fusion.place
  210.9 8.8 %finish.1 = (bf16[256,1024]{1,0:T(8,128)(2,1)}, bf16[512,1024]{1,0:T(8,128)(2,1)}) custom-call(bf16[16,256,256]{2,1,0:T(8,128)(2,1)} %all-to-all-done.2.mixed, bf16[16,192,1024]{2,1,0:T(8,128)(2,1)} %bitcast.87, bf16[16,64,1024]{2,1,0:T(8,128)(2,1)} %out_weight.3, bf16[256,1024]{1,0:T(8,128)(2,1)} %get-tuple-element.39.features, f32[1,1024]{1,0:T(1,128)} %bitcast.103, ...), custom_call_target="tpu_custom_call" | custom-call | tf_op jit(solution)/shard_map/finish/pallas_call | solution.py:366
  219.7 2.3 reshape.184
  221.9 8.2 %all-to-all-start.3 = ((bf16[128,4,1024]{2,1,0:T(4,128)(2,1)}), bf16[128,4,1024]{2,1,0:T(4,128)(2,1)S(1)}, u32[]{:S(2)}, u32[]{:S(2)}) async-start(bf16[128,4,1024]{2,1,0:T(4,128)(2,1)} %reshape.184), calls=%async_computation.3 | async-start | bytes 2097152 | tf_op jit(solution)/shard_map/all_to_all | solution.py:517
  230.3 1.0 collective-permute-start.13
  231.3 2.7 %collective-permute-start.14 = (f32[64,128]{1,0:T(8,128)S(1)}, f32[64,128]{1,0:T(8,128)S(1)}, u32[]{:S(2)}, u32[]{:S(2)}) collective-permute-start(f32[64,128]{1,0:T(8,128)S(1)} %slice.76), channel_id=1, source_target_pairs={{0,2},{1,3},{2,0},{3,1},{4,6},{5,7},{6,4},{7,5},{8,10},{9,11},{10,... | collective-permute-start | bytes 98312 | tf_op jit(solution)/shard_map/ppermute | solution.py:441
  234.0 1.5 collective-permute-start.15
  235.4 0.6 slice.74
  236.1 8.7 %collective-permute-done.13 = f32[64,128]{1,0:T(8,128)S(1)} collective-permute-done((f32[64,128]{1,0:T(8,128)S(1)}, f32[64,128]{1,0:T(8,128)S(1)}, u32[]{:S(2)}, u32[]{:S(2)}) %collective-permute-start.13) | collective-permute-done | bytes 32800 | tf_op jit(solution)/shard_map/ppermute | solution.py:441
  244.8 0.8 collective-permute-done.14
  245.6 0.6 add_bitcast_fusion
  246.3 0.6 copy.54
  246.9 0.6 slice_bitcast_fusion.6
  247.5 1.9 all-to-all-done.3
  249.4 1.0 copy.57
  (47 shorter events, 0.8 us)
Async XLA Ops:
  7.2 2.0 copy-start
  13.5 31.6 %all-to-all-start = ((bf16[128,4,1152]{2,1,0:T(4,128)(2,1)}), bf16[128,4,1152]{2,1,0:T(4,128)(2,1)S(1)}, u32[]{:S(2)}, u32[]{:S(2)}) async-start(bf16[128,4,1152]{2,1,0:T(4,128)(2,1)} %copy.44), calls=%async_computation | async-start | bytes 2359296 | tf_op jit(solution)/shard_map/all_to_all | solution.py:457
  24.7 136.3 %all-gather.3.cloned.1.call-start = ((), (), s32[]{:S(2)}) async-start(), calls=%async_computation.4 | async-start | bytes 9469952 | tf_op jit(solution)/shard_map/all_gather | solution.py:479
  54.2 40.9 %copy-start.2 = (bf16[1,256,1024]{2,1,0:T(8,128)(2,1)S(1)}, bf16[1,256,1024]{2,1,0:T(8,128)(2,1)}, u32[]{:S(2)}) copy-start(bf16[1,256,1024]{2,1,0:T(8,128)(2,1)} %param.15) | copy-start | bytes 1572868
  95.1 59.7 %copy-start.1 = (bf16[16,256,256]{2,1,0:T(8,128)(2,1)}, bf16[16,256,256]{2,1,0:T(8,128)(2,1)S(1)}, u32[]{:S(2)}) copy-start(bf16[16,256,256]{2,1,0:T(8,128)(2,1)S(1)} %all_to_all.20.packed.projected) | copy-start | bytes 6291460
  95.1 59.7 %collective-permute-start = (bf16[256,1024]{1,0:T(8,128)(2,1)S(1)}, bf16[256,1024]{1,0:T(8,128)(2,1)S(1)}, u32[]{:S(2)}, u32[]{:S(2)}) collective-permute-start(bf16[256,1024]{1,0:T(8,128)(2,1)S(1)} %bitcast.81), channel_id=1, source_target_pairs={{0,1},{1,2},{2,3},{3,0},{4,5},{5,6},{6,7},{7,4},{8,9},{9,10},{10,1... | collective-permute-start | bytes 1572872 | tf_op jit(solution)/shard_map/ppermute | solution.py:441
  95.7 59.1 %collective-permute-start.1 = (bf16[256,1024]{1,0:T(8,128)(2,1)S(1)}, bf16[256,1024]{1,0:T(8,128)(2,1)S(1)}, u32[]{:S(2)}, u32[]{:S(2)}) collective-permute-start(bf16[256,1024]{1,0:T(8,128)(2,1)S(1)} %bitcast.82), channel_id=1, source_target_pairs={{0,2},{1,3},{2,0},{3,1},{4,6},{5,7},{6,4},{7,5},{8,10},{9,11},{10,... | collective-permute-start | bytes 1572872 | tf_op jit(solution)/shard_map/ppermute | solution.py:441
  96.8 58.8 %collective-permute-start.2 = (bf16[256,1024]{1,0:T(8,128)(2,1)S(1)}, bf16[256,1024]{1,0:T(8,128)(2,1)S(1)}, u32[]{:S(2)}, u32[]{:S(2)}) collective-permute-start(bf16[256,1024]{1,0:T(8,128)(2,1)S(1)} %bitcast.83), channel_id=1, source_target_pairs={{0,3},{1,0},{2,1},{3,2},{4,7},{5,4},{6,5},{7,6},{8,11},{9,8},{10,9... | collective-permute-start | bytes 1572872 | tf_op jit(solution)/shard_map/ppermute | solution.py:441
  154.8 0.8 copy-start.3
  155.6 0.8 copy-start.5
  156.4 47.5 %all-to-all-start.2 = ((bf16[16,256,256]{2,1,0:T(8,128)(2,1)}), bf16[16,256,256]{2,1,0:T(8,128)(2,1)}, u32[]{:S(2)}, u32[]{:S(2)}) async-start(bf16[16,256,256]{2,1,0:T(8,128)(2,1)} %attend.1.mixed), calls=%async_computation.2 | async-start | bytes 4194304 | tf_op jit(solution)/shard_map/all_to_all | solution.py:484
  161.0 30.0 %copy-start.4 = (bf16[256,1024]{1,0:T(8,128)(2,1)S(1)}, bf16[256,1024]{1,0:T(8,128)(2,1)}, u32[]{:S(2)}) copy-start(bf16[256,1024]{1,0:T(8,128)(2,1)} %copy-done.3) | copy-start | bytes 1572868
  161.0 29.9 %copy-start.6 = (bf16[256,1024]{1,0:T(8,128)(2,1)S(1)}, bf16[256,1024]{1,0:T(8,128)(2,1)}, u32[]{:S(2)}) copy-start(bf16[256,1024]{1,0:T(8,128)(2,1)} %copy-done.5) | copy-start | bytes 1572868
  171.9 15.6 %collective-permute-start.3 = (bf16[4,64,256]{2,1,0:T(8,128)(2,1)S(1)}, bf16[4,64,256]{2,1,0:T(8,128)(2,1)S(1)}, u32[]{:S(2)}, u32[]{:S(2)}) collective-permute-start(bf16[4,64,256]{2,1,0:T(8,128)(2,1)S(1)} %get-tuple-element.57), channel_id=1, source_target_pairs={{0,4},{1,5},{2,6},{3,7},{4,8},{5,9},{6,10},{7,11},{8,12},{9,13},{1... | collective-permute-start | bytes 393224 | tf_op jit(solution)/shard_map/ppermute | solution.py:446
  173.8 17.1 %collective-permute-start.4 = (bf16[4,64,256]{2,1,0:T(8,128)(2,1)S(1)}, bf16[4,64,256]{2,1,0:T(8,128)(2,1)S(1)}, u32[]{:S(2)}, u32[]{:S(2)}) collective-permute-start(bf16[4,64,256]{2,1,0:T(8,128)(2,1)S(1)} %get-tuple-element.56), channel_id=1, source_target_pairs={{0,8},{1,9},{2,10},{3,11},{4,12},{5,13},{6,14},{7,15},{8,0},{9,1},... | collective-permute-start | bytes 393224 | tf_op jit(solution)/shard_map/ppermute | solution.py:446
  176.5 14.5 %collective-permute-start.5 = (bf16[4,64,256]{2,1,0:T(8,128)(2,1)S(1)}, bf16[4,64,256]{2,1,0:T(8,128)(2,1)S(1)}, u32[]{:S(2)}, u32[]{:S(2)}) collective-permute-start(bf16[4,64,256]{2,1,0:T(8,128)(2,1)S(1)} %get-tuple-element.55), channel_id=1, source_target_pairs={{0,12},{1,13},{2,14},{3,15},{4,0},{5,1},{6,2},{7,3},{8,4},{9,5},{1... | collective-permute-start | bytes 393224 | tf_op jit(solution)/shard_map/ppermute | solution.py:446
  190.9 0.8 copy-start.7
  192.4 11.5 %copy-start.8 = (bf16[8,192,128]{2,1,0:T(8,128)(2,1)S(1)}, bf16[8,192,128]{2,1,0:T(8,128)(2,1)}, u32[]{:S(2)}) copy-start(bf16[8,192,128]{2,1,0:T(8,128)(2,1)} %get-tuple-element.43) | copy-start | bytes 1179652
  192.5 7.6 %collective-permute-start.6 = (bf16[640,128]{1,0:T(8,128)(2,1)S(1)}, bf16[640,128]{1,0:T(8,128)(2,1)S(1)}, u32[]{:S(2)}, u32[]{:S(2)}) collective-permute-start(bf16[640,128]{1,0:T(8,128)(2,1)S(1)} %get-tuple-element.48), channel_id=1, source_target_pairs={{0,12},{1,13},{2,14},{3,15},{4,0},{5,1},{6,2},{7,3},{8,4},{9,5},{1... | collective-permute-start | bytes 491528 | tf_op jit(solution)/shard_map/ppermute | solution.py:446
  192.8 8.6 %collective-permute-start.7 = (bf16[640,128]{1,0:T(8,128)(2,1)S(1)}, bf16[640,128]{1,0:T(8,128)(2,1)S(1)}, u32[]{:S(2)}, u32[]{:S(2)}) collective-permute-start(bf16[640,128]{1,0:T(8,128)(2,1)S(1)} %get-tuple-element.50), channel_id=1, source_target_pairs={{0,8},{1,9},{2,10},{3,11},{4,12},{5,13},{6,14},{7,15},{8,0},{9,1},... | collective-permute-start | bytes 491528 | tf_op jit(solution)/shard_map/ppermute | solution.py:446
  194.7 9.1 %collective-permute-start.8 = (bf16[640,128]{1,0:T(8,128)(2,1)S(1)}, bf16[640,128]{1,0:T(8,128)(2,1)S(1)}, u32[]{:S(2)}, u32[]{:S(2)}) collective-permute-start(bf16[640,128]{1,0:T(8,128)(2,1)S(1)} %get-tuple-element.49), channel_id=1, source_target_pairs={{0,4},{1,5},{2,6},{3,7},{4,8},{5,9},{6,10},{7,11},{8,12},{9,13},{1... | collective-permute-start | bytes 491528 | tf_op jit(solution)/shard_map/ppermute | solution.py:446
  204.1 2.0 collective-permute-start.9
  206.4 23.8 %collective-permute-start.10 = (f32[320,128]{1,0:T(8,128)S(1)}, f32[320,128]{1,0:T(8,128)S(1)}, u32[]{:S(2)}, u32[]{:S(2)}) collective-permute-start(f32[320,128]{1,0:T(8,128)S(1)} %get-tuple-element.61), channel_id=1, source_target_pairs={{0,32},{16,48},{32,64},{48,80},{64,96},{80,112},{96,0},{112,16},{1... | collective-permute-start | bytes 491528 | tf_op jit(solution)/shard_map/ppermute | solution.py:407
  206.9 23.2 %collective-permute-start.11 = (f32[320,128]{1,0:T(8,128)S(1)}, f32[320,128]{1,0:T(8,128)S(1)}, u32[]{:S(2)}, u32[]{:S(2)}) collective-permute-start(f32[320,128]{1,0:T(8,128)S(1)} %get-tuple-element.62), channel_id=1, source_target_pairs={{0,64},{16,80},{32,96},{48,112},{64,0},{80,16},{96,32},{112,48},{1... | collective-permute-start | bytes 491528 | tf_op jit(solution)/shard_map/ppermute | solution.py:407
  208.9 21.3 %collective-permute-start.12 = (f32[320,128]{1,0:T(8,128)S(1)}, f32[320,128]{1,0:T(8,128)S(1)}, u32[]{:S(2)}, u32[]{:S(2)}) collective-permute-start(f32[320,128]{1,0:T(8,128)S(1)} %get-tuple-element.63), channel_id=1, source_target_pairs={{0,96},{16,112},{32,0},{48,16},{64,32},{80,48},{96,64},{112,80},{1... | collective-permute-start | bytes 491528 | tf_op jit(solution)/shard_map/ppermute | solution.py:407
  221.9 27.4 %all-to-all-start.3 = ((bf16[128,4,1024]{2,1,0:T(4,128)(2,1)}), bf16[128,4,1024]{2,1,0:T(4,128)(2,1)S(1)}, u32[]{:S(2)}, u32[]{:S(2)}) async-start(bf16[128,4,1024]{2,1,0:T(4,128)(2,1)} %reshape.184), calls=%async_computation.3 | async-start | bytes 2097152 | tf_op jit(solution)/shard_map/all_to_all | solution.py:517
  230.3 14.5 %collective-permute-start.13 = (f32[64,128]{1,0:T(8,128)S(1)}, f32[64,128]{1,0:T(8,128)S(1)}, u32[]{:S(2)}, u32[]{:S(2)}) collective-permute-start(f32[64,128]{1,0:T(8,128)S(1)} %slice.76), channel_id=1, source_target_pairs={{0,1},{1,2},{2,3},{3,0},{4,5},{5,6},{6,7},{7,4},{8,9},{9,10},{10,1... | collective-permute-start | bytes 98312 | tf_op jit(solution)/shard_map/ppermute | solution.py:441
  231.3 14.3 %collective-permute-start.14 = (f32[64,128]{1,0:T(8,128)S(1)}, f32[64,128]{1,0:T(8,128)S(1)}, u32[]{:S(2)}, u32[]{:S(2)}) collective-permute-start(f32[64,128]{1,0:T(8,128)S(1)} %slice.76), channel_id=1, source_target_pairs={{0,2},{1,3},{2,0},{3,1},{4,6},{5,7},{6,4},{7,5},{8,10},{9,11},{10,... | collective-permute-start | bytes 98312 | tf_op jit(solution)/shard_map/ppermute | solution.py:441
  234.0 11.7 %collective-permute-start.15 = (f32[64,128]{1,0:T(8,128)S(1)}, f32[64,128]{1,0:T(8,128)S(1)}, u32[]{:S(2)}, u32[]{:S(2)}) collective-permute-start(f32[64,128]{1,0:T(8,128)S(1)} %slice.76), channel_id=1, source_target_pairs={{0,3},{1,0},{2,1},{3,2},{4,7},{5,4},{6,5},{7,6},{8,11},{9,8},{10,9... | collective-permute-start | bytes 98312 | tf_op jit(solution)/shard_map/ppermute | solution.py:441
Sparse Core Ops, SparseCore 0:
  54.3 102.4 all-gather.2

commit v3 on v2

--- a/solution.py
+++ b/solution.py
@@ -39,15 +39,16 @@
 
 
 def project_body(
-    received, place, gain, cotangent, weight, out_weight, packed, features, normed, local, heads
+    received, place, gain, cotangent, weight, grads, packed, features, normed, local, heads
 ):
     rows, width = features.shape
 
     @pl.when(pl.program_id(0) == 0)
     def _():
-        slot = lax.broadcasted_iota(jnp.int32, (rows, received.shape[0]), 1)
+        count = received.shape[0] * received.shape[1]
+        slot = lax.broadcasted_iota(jnp.int32, (rows, count), 1)
         pick = jnp.where(slot == place[...], 1.0, 0.0).astype(BF16)
-        taken = dot(pick, received[...], 1, 0)
+        taken = dot(pick, received[...].reshape(count, received.shape[2]), 1, 0)
         active = taken[:, :width]
         features[...] = active.astype(BF16)
         level = taken[:, width:]
@@ -59,18 +60,41 @@
         normed[rows:, rows:] = jnp.zeros((2 * LINES, width - rows), BF16)
         local[...] = dot(level.astype(BF16), cotangent[...], 0, 0)[:LINES]
 
-    size = out_weight.shape[1]
+    size = grads.shape[1]
     rows, width = features.shape
     projected = dot(weight[...].reshape(heads * 3 * size, width), normed[:rows, :], 1, 1)
-    grads = dot(out_weight[...].reshape(heads * size, width), cotangent[...], 1, 1)
     packed[:, : 3 * size, :] = projected.astype(BF16).reshape(heads, 3 * size, rows)
-    packed[:, 3 * size :, :] = grads.astype(BF16).reshape(heads, size, rows)
-
-
-def project(received, place, gain, cotangent, weight, out_weight):
+    packed[:, 3 * size :, :] = grads[...]
+
+
+def project_grads_body(cotangent, weight, out):
+    heads, size, rows = out.shape
+    grads = dot(weight[...].reshape(heads * size, -1), cotangent[...], 1, 1)
+    out[...] = grads.astype(BF16).reshape(heads, size, rows)
+
+
+def project_grads(cotangent, weight):
+    rows, width = cotangent.shape
+    count, size, _ = weight.shape
+    heads = 4
+    return pl.pallas_call(
+        project_grads_body,
+        grid=(count // heads,),
+        in_specs=[
+            whole((rows, width)),
+            pl.BlockSpec((heads, size, width), lambda i: (i, 0, 0)),
+        ],
+        out_specs=pl.BlockSpec((heads, size, rows), lambda i: (i, 0, 0)),
+        out_shape=jax.ShapeDtypeStruct((count, size, rows), BF16),
+        compiler_params=vmem(60),
+        name="project_grads",
+    )(cotangent, weight)
+
+
+def project(received, place, gain, cotangent, weight, grads):
     rows, width = cotangent.shape
     count, three, _ = weight.shape
-    size = out_weight.shape[1]
+    size = grads.shape[1]
     heads = 4
     return pl.pallas_call(
         functools.partial(project_body, heads=heads),
@@ -81,7 +105,7 @@
             whole((1, width)),
             whole((rows, width)),
             pl.BlockSpec((heads, three, width), lambda i: (i, 0, 0)),
-            pl.BlockSpec((heads, size, width), lambda i: (i, 0, 0)),
+            pl.BlockSpec((heads, size, rows), lambda i: (i, 0, 0)),
         ],
         out_specs=[
             pl.BlockSpec((heads, three + size, rows), lambda i: (i, 0, 0)),
@@ -97,11 +121,11 @@
         ],
         compiler_params=vmem(60),
         name="project",
-    )(received, place, gain, cotangent, weight, out_weight)
+    )(received, place, gain, cotangent, weight, grads)
 
 
 def attend_body(
-    packed, out, query, grad, keys, values, key_total, value_total, *, scale, shift, step
+    packed, out, only, query, grad, keys, values, key_total, value_total, *, scale, shift, step
 ):
     shards, four, rows = packed.shape
     size = four // 4
@@ -137,6 +161,7 @@
             key_total[:, part] += dot(q_across, grad_scores, 1, 0)
             value_total[:, part] += dot(g_across, weights, 1, 0)
         out[i, :size, :] = attended.astype(BF16)
+        only[i] = attended.astype(BF16)
         out[i, size : 2 * size, :] = (grad_query * scale).astype(BF16)
         return 0
 
@@ -153,8 +178,11 @@
     return pl.pallas_call(
         functools.partial(attend_body, scale=scale, shift=shift, step=min(1024, length)),
         in_specs=[pl.BlockSpec(memory_space=pltpu.VMEM)],
-        out_specs=pl.BlockSpec(memory_space=pltpu.VMEM),
-        out_shape=jax.ShapeDtypeStruct(packed.shape, BF16),
+        out_specs=[pl.BlockSpec(memory_space=pltpu.VMEM)] * 2,
+        out_shape=[
+            jax.ShapeDtypeStruct(packed.shape, BF16),
+            jax.ShapeDtypeStruct((shards, size, rows), BF16),
+        ],
         scratch_shapes=[
             pltpu.VMEM((length, size), BF16),
             pltpu.VMEM((length, size), BF16),
@@ -163,7 +191,7 @@
             pltpu.VMEM((size, length), F32),
             pltpu.VMEM((size, length), F32),
         ],
-        compiler_params=vmem(48),
+        compiler_params=vmem(60),
         cost_estimate=pl.CostEstimate(
             flops=48 * length * length * size, bytes_accessed=8 * length * size, transcendentals=0
         ),
@@ -180,7 +208,6 @@
     gain,
     local,
     out,
-    attended,
     small,
     total,
     by_level,
@@ -198,7 +225,6 @@
         total[...] = jnp.zeros_like(total)
         by_level[...] = jnp.zeros_like(by_level)
 
-    attended[...] = mixed[:, :first, :]
     for s in range(mixed.shape[0]):
         grads = mixed[s, first:, :]
         features = normed[s, :rows, :]
@@ -256,7 +282,7 @@
                 fixed(gain.shape),
                 fixed(local.shape),
             ],
-            out_specs=[fixed(shape), by_step((shards, first, rows)), fixed(small)],
+            out_specs=[fixed(shape), fixed(small)],
             scratch_shapes=[
                 pltpu.VMEM((lines + 2 * LINES, width), F32),
                 pltpu.VMEM((LINES, lines), F32),
@@ -264,11 +290,9 @@
         ),
         out_shape=[
             jax.ShapeDtypeStruct(shape, BF16),
-            jax.ShapeDtypeStruct((shards, first, rows), BF16),
             jax.ShapeDtypeStruct(small, F32),
         ],
         compiler_params=vmem(60),
-        cost_estimate=pl.CostEstimate(flops=1, bytes_accessed=1, transcendentals=0),
         name="weight_grad",
     )(head, mixed, projected, normed, weight, gain, local)
 
@@ -307,83 +331,95 @@
         out_specs=pl.BlockSpec(memory_space=pltpu.VMEM),
         out_shape=jax.ShapeDtypeStruct(shape, BF16),
         compiler_params=vmem(48),
-        cost_estimate=pl.CostEstimate(flops=1, bytes_accessed=1, transcendentals=0),
         name="out_grad",
     )(column, small, *attended, *cotangents)
 
 
-def finish_body(
-    mixed,
-    weight,
-    out_weight,
-    features,
-    normed_gain,
-    cotangent,
-    place,
-    output,
-    outgoing,
-    out_total,
-    grad_total,
-    *,
-    heads,
-):
-    size = out_weight.shape[1]
+def finish_output_body(mixed, weight, features, output, total):
+    heads, size, rows = mixed.shape
     index = pl.program_id(0)
 
     @pl.when(index == 0)
     def _():
-        out_total[...] = jnp.zeros_like(out_total)
-        grad_total[...] = jnp.zeros_like(grad_total)
-
-    attended = jnp.concatenate([mixed[h, :size, :] for h in range(heads)], axis=0)
-    grads = jnp.concatenate([mixed[h, size:, :] for h in range(heads)], axis=0)
-    out_total[...] += dot(attended, out_weight[...].reshape(heads * size, -1), 0, 0)
-    grad_total[...] += dot(grads, weight[...].reshape(heads * 3 * size, -1), 0, 0)
+        total[...] = features[...].astype(F32)
+
+    attended = mixed[...].reshape(heads * size, rows)
+    total[...] += dot(attended, weight[...].reshape(heads * size, -1), 0, 0)
 
     @pl.when(index == pl.num_programs(0) - 1)
     def _():
-        rows, _ = features.shape
+        output[...] = total[...].astype(BF16)
+
+
+def finish_output(mixed, weight, features):
+    count, _, rows = mixed.shape
+    _, size, width = weight.shape
+    heads = 4
+    return pl.pallas_call(
+        finish_output_body,
+        grid=(count // heads,),
+        in_specs=[
+            pl.BlockSpec((heads, size, rows), lambda i: (i, 0, 0)),
+            pl.BlockSpec((heads, size, width), lambda i: (i, 0, 0)),
+            whole((rows, width)),
+        ],
+        out_specs=whole((rows, width)),
+        out_shape=jax.ShapeDtypeStruct((rows, width), BF16),
+        scratch_shapes=[pltpu.VMEM((rows, width), F32)],
+        compiler_params=vmem(60),
+        name="finish_output",
+    )(mixed, weight, features)
+
+
+def finish_grad_body(mixed, weight, features, gain, cotangent, place, outgoing, total):
+    heads, four, rows = mixed.shape
+    size = four // 4
+    index = pl.program_id(0)
+
+    @pl.when(index == 0)
+    def _():
+        total[...] = jnp.zeros_like(total)
+
+    grads = mixed[:, size:, :].reshape(heads * 3 * size, rows)
+    total[...] += dot(grads, weight[...].reshape(heads * 3 * size, -1), 0, 0)
+
+    @pl.when(index == pl.num_programs(0) - 1)
+    def _():
         active = features[...].astype(F32)
-        output[...] = (active + out_total[...]).astype(BF16)
         inverse = lax.rsqrt(jnp.mean(active * active, axis=1, keepdims=True) + EPSILON)
-        grad_normed = grad_total[...]
-        scaled = normed_gain[...] * grad_normed
+        scaled = gain[...] * total[...]
         cubed = inverse * inverse * inverse
         grad_active = inverse * scaled - active * cubed * jnp.mean(
             active * scaled, axis=1, keepdims=True
         )
         grad_features = (cotangent[...].astype(F32) + grad_active).astype(BF16)
-        slot = lax.broadcasted_iota(jnp.int32, (outgoing.shape[0], rows), 0)
+        count = outgoing.shape[0] * outgoing.shape[1]
+        slot = lax.broadcasted_iota(jnp.int32, (count, rows), 0)
         pick = jnp.where(slot == place[...], 1.0, 0.0).astype(BF16)
-        outgoing[...] = dot(pick, grad_features, 1, 0).astype(BF16)
-
-
-def finish(mixed, weight, out_weight, features, gain, cotangent, place, slots):
+        outgoing[...] = dot(pick, grad_features, 1, 0).astype(BF16).reshape(outgoing.shape)
+
+
+def finish_grad(mixed, weight, features, gain, cotangent, place, owners, slots):
     count, four, rows = mixed.shape
     width = features.shape[1]
-    size = four // 4
     heads = 4
     return pl.pallas_call(
-        functools.partial(finish_body, heads=heads),
+        finish_grad_body,
         grid=(count // heads,),
         in_specs=[
             pl.BlockSpec((heads, four, rows), lambda i: (i, 0, 0)),
-            pl.BlockSpec((heads, 3 * size, width), lambda i: (i, 0, 0)),
-            pl.BlockSpec((heads, size, width), lambda i: (i, 0, 0)),
+            pl.BlockSpec((heads, four - four // 4, width), lambda i: (i, 0, 0)),
             whole((rows, width)),
             whole((1, width)),
             whole((rows, width)),
             whole((1, rows)),
         ],
-        out_specs=[whole((rows, width)), whole((slots, width))],
-        out_shape=[
-            jax.ShapeDtypeStruct((rows, width), BF16),
-            jax.ShapeDtypeStruct((slots, width), BF16),
-        ],
-        scratch_shapes=[pltpu.VMEM((rows, width), F32), pltpu.VMEM((rows, width), F32)],
+        out_specs=whole((owners, slots, width)),
+        out_shape=jax.ShapeDtypeStruct((owners, slots, width), BF16),
+        scratch_shapes=[pltpu.VMEM((rows, width), F32)],
         compiler_params=vmem(60),
-        name="finish",
-    )(mixed, weight, out_weight, features, gain, cotangent, place)
+        name="finish_grad",
+    )(mixed, weight, features, gain, cotangent, place)
 
 
 def pick(value, k, axis=0):
@@ -468,22 +504,24 @@
     weight = project_weight.reshape(count, 3 * size, width)
 
     packed, features, normed, local = project(
-        received.reshape(owners * slots, width + LANES),
+        received,
         place.reshape(rows, 1),
         gain,
         grad_rows,
         weight,
-        output_weight,
+        project_grads(grad_rows, output_weight),
     )
     by_head = lax.all_to_all(packed, "seq", split_axis=0, concat_axis=0, tiled=True)
     all_normed = lax.all_gather(normed, "seq")
     by_head, line_rows = lax.optimization_barrier((by_head, grad_rows))
     line_rows = [line_rows] + [along_line(line_rows, k) for k in range(1, side)]
-    attended = attend(by_head, scale, shift)
-    attended, line_rows = lax.optimization_barrier((attended, line_rows))
+    attended, head_attended = attend(by_head, scale, shift)
+    attended, head_attended, line_rows = lax.optimization_barrier(
+        (attended, head_attended, line_rows)
+    )
     mixed = lax.all_to_all(attended, "seq", split_axis=0, concat_axis=0, tiled=True)
 
-    shares, head_attended, small = weight_grad(
+    shares, small = weight_grad(
         shard_index.reshape(1),
         attended,
         by_head,
@@ -503,19 +541,13 @@
         [along_column(out_shares[k], -k).astype(F32) for k in range(1, side)],
         out_shares[0].astype(F32),
     )
-    mixed, out_shares, shares = lax.optimization_barrier((mixed, out_shares, shares))
-    output, outgoing = finish(
-        mixed,
-        weight,
-        output_weight,
-        features,
-        gain,
-        grad_rows,
-        place.reshape(1, rows),
-        owners * slots,
-    )
+    outgoing = finish_grad(
+        mixed, weight, features, gain, grad_rows, place.reshape(1, rows), owners, slots
+    )
+    output = finish_output(mixed, output_weight, features)
+    outgoing, out_shares, shares = lax.optimization_barrier((outgoing, out_shares, shares))
     returned = lax.all_to_all(
-        outgoing.reshape(owners, slots, width),
+        outgoing,
         ("tile", "seq"),
         split_axis=0,
         concat_axis=0,

time: 258 us -> 247 us (0.957)
  waiting for transfers between devices: 52.5 us -> 37.9 us
  Pallas kernels: 83.5 us -> 92 us
  local copies, waits for them, and re-layouts: 15 us -> 8.82 us
    pallas_call x1 -> x3, Pallas kernels: 8.81 us -> 16 us  [the longest x1 7.42 us: finish_grad(): pl.pallas_call(finish_grad_body, grid=(count // heads,), in_specs=[pl.Blo...]
    ppermute x6, waiting for transfers between devices: 21.8 us -> 15.2 us  [along_column(): lax.ppermute(value, 'seq', [(i, (i + k * side) % shards) for i in range(s...]
    all_to_all x1, waiting for transfers between devices: 17.4 us -> 13.2 us  [on_device(): lax.all_to_all(embedded.reshape(owners, slots, width + LANES), ('tile', '...]
    ppermute x6, waiting for transfers between devices: 9.55 us -> 5.52 us  [along_line(): lax.ppermute(value, 'seq', [(i, i // side * side + (i + k) % side) for i...]
    reshape x2 -> x0, local copies, waits for them, and re-layouts: 3.42 us -> none  [the longest x1 2.26 us: on_device(): outgoing.reshape(owners, slots, width)]
  transfers between devices with their start and end apart: 20 -> 20, of which waited for: 10 -> 7; matrix products, arithmetic and copies ran while one was open for 4% -> 2% of each run, Pallas kernels for 29% -> 34%
where the time goes in v3:
time: 247 us; the launch traced here: 246 us
  Pallas kernels  92 us (37%)
  starting transfers between devices  43.6 us (18%)
  blocking collectives  41.6 us (17%)
  waiting for transfers between devices  37.9 us (15%)
  between operations  14.5 us (6%)
  local copies, waits for them, and re-layouts  8.82 us (4%)
  other arithmetic  5.27 us (2%)
    pallas_call x1, Pallas kernels, attend(): pl.pallas_call(functools.partial(attend_body, scale=scale, shift=shift, s...  58.5 us
    all_to_all x1, blocking collectives, on_device(): lax.all_to_all(packed, 'seq', split_axis=0, concat_axis=0, tiled=True)  41.6 us
    ppermute x6, waiting for transfers between devices, along_column(): lax.ppermute(value, 'seq', [(i, (i + k * side) % shards) for i in range(s...  15.2 us
    all_to_all x1, waiting for transfers between devices, on_device(): lax.all_to_all(embedded.reshape(owners, slots, width + LANES), ('tile', '...  13.2 us
    all_to_all x1, starting transfers between devices, on_device(): lax.all_to_all(embedded.reshape(owners, slots, width + LANES), ('tile', '...  11.1 us
    pallas_call x1, Pallas kernels, weight_grad(): pl.pallas_call(functools.partial(weight_grad_body, factor=factor), grid_s...  9.5 us
    all_to_all x1, starting transfers between devices, on_device(): lax.all_to_all(outgoing, ('tile', 'seq'), split_axis=0, concat_axis=0, ti...  8.3 us
    ppermute x6, starting transfers between devices, along_column(): lax.ppermute(value, 'seq', [(i, (i + k * side) % shards) for i in range(s...  7.62 us
  transfers between devices with their start and end apart: 20, of which 7 were waited for; matrix products, arithmetic and copies ran while one was open for 2% of the time, Pallas kernels for 34%

profile of v3, /device:TPU:0, one launch (start us, length us, event | category | flops | bytes accessed | tf_op | source)
XLA Modules:
  0.0 245.7 jit_solution(5631882582959439428)
XLA Ops:
  7.2 1.1 dynamic-slice_reduce_fusion
  8.3 0.1 lt.100
  8.4 0.1 iota_compare_fusion.2
  8.5 0.8 copy.43
  9.3 0.2 fusion.6
  9.6 1.8 fusion
  11.4 0.8 copy.35
  12.2 1.6 maximum_select_fusion
  13.8 11.1 %all-to-all-start = ((bf16[128,4,1152]{2,1,0:T(4,128)(2,1)}), bf16[128,4,1152]{2,1,0:T(4,128)(2,1)S(1)}, u32[]{:S(2)}, u32[]{:S(2)}) async-start(bf16[128,4,1152]{2,1,0:T(4,128)(2,1)} %maximum_select_fusion), calls=%async_computation | async-start | bytes 2359296 | tf_op jit(solution)/shard_map/all_to_all | solution.py:493
  25.0 0.0 all-gather.3.cloned.1.call-start
  25.0 0.7 fusion.14
  25.7 0.1 copy.38
  25.8 0.2 reduce-window.8
  26.0 0.1 reduce.1
  26.1 0.7 bitcast_subtract_fusion
  26.8 0.2 select_reduce_fusion
  27.0 0.1 copy.39
  27.1 0.1 copy.40
  27.3 0.7 sub.42.place
  27.9 4.3 %project_grads.1.grads = bf16[16,64,256]{2,1,0:T(8,128)(2,1)} custom-call(bf16[256,1024]{1,0:T(8,128)(2,1)} %bitcast.76, bf16[16,64,1024]{2,1,0:T(8,128)(2,1)} %weight.3), custom_call_target="tpu_custom_call" | custom-call | tf_op jit(solution)/shard_map/project_grads/pallas_call | solution.py:80
  32.2 13.2 %all-to-all-done.received = bf16[128,4,1152]{2,1,0:T(4,128)(2,1)S(1)} async-done(((bf16[128,4,1152]{2,1,0:T(4,128)(2,1)}), bf16[128,4,1152]{2,1,0:T(4,128)(2,1)S(1)}, u32[]{:S(2)}, u32[]{:S(2)}) %all-to-all-start) | async-done | bytes 1179680 | tf_op jit(solution)/shard_map/all_to_all | solution.py:493
  45.4 1.1 copy-done.3
  46.4 7.3 %project.1 = (bf16[16,256,256]{2,1,0:T(8,128)(2,1)}, bf16[256,1024]{1,0:T(8,128)(2,1)}, bf16[272,1024]{1,0:T(8,128)(2,1)}, f32[8,1024]{1,0:T(8,128)}) custom-call(bf16[128,4,1152]{2,1,0:T(4,128)(2,1)} %copy-done.3, s32[256,1]{1,0:T(8,128)} %sub.42.place, f32[1,1024]{1,0:T(1,128)} %bitcast.101, bf16[256,1024]{1,0:T(8,128)(2,1)} %bitcast.77, ...), custom_call_target="tpu_custom_call" | custom-call | tf_op jit(solution)/shard_map/project/pallas_call | solution.py:99
  53.7 41.6 %all_to_all.20.packed.projected = bf16[16,256,256]{2,1,0:T(8,128)(2,1)} all-to-all(bf16[16,256,256]{2,1,0:T(8,128)(2,1)} %get-tuple-element.25), channel_id=1, replica_groups=mesh['tile'=8,'seq'=16] {'seq'}, dimensions={0} | all-to-all | bytes 4194304 | tf_op jit(solution)/shard_map/all_to_all | solution.py:514
  95.4 0.3 collective-permute-start.2
  95.6 2.4 collective-permute-start.1
  98.0 58.5 %attend.1 = (bf16[16,256,256]{2,1,0:T(8,128)(2,1)}, bf16[16,64,256]{2,1,0:T(8,128)(2,1)}) custom-call(bf16[16,256,256]{2,1,0:T(8,128)(2,1)} %all_to_all.20.packed.projected), custom_call_target="tpu_custom_call" | custom-call | flops 51539607552 | bytes 2097152 | tf_op jit(solution)/shard_map/attend/pallas_call | solution.py:178
  156.6 4.9 %all-to-all-start.2 = ((bf16[16,256,256]{2,1,0:T(8,128)(2,1)}), bf16[16,256,256]{2,1,0:T(8,128)(2,1)}, u32[]{:S(2)}, u32[]{:S(2)}) async-start(bf16[16,256,256]{2,1,0:T(8,128)(2,1)} %get-tuple-element.30.mixed), calls=%async_computation.2 | async-start | bytes 4194304 | tf_op jit(solution)/shard_map/all_to_all | solution.py:522
  161.5 0.1 dynamic-slice_bitcast_fusion.4
  161.6 3.1 %collective-permute-start.5 = (bf16[4,64,256]{2,1,0:T(8,128)(2,1)S(1)}, bf16[4,64,256]{2,1,0:T(8,128)(2,1)S(1)}, u32[]{:S(2)}, u32[]{:S(2)}) collective-permute-start(bf16[4,64,256]{2,1,0:T(8,128)(2,1)S(1)} %get-tuple-element.55), channel_id=1, source_target_pairs={{0,12},{1,13},{2,14},{3,15},{4,0},{5,1},{6,2},{7,3},{8,4},{9,5},{1... | collective-permute-start | bytes 393224 | tf_op jit(solution)/shard_map/ppermute | solution.py:482
  164.7 0.9 collective-permute-start.4
  165.5 0.9 collective-permute-start.3
  166.4 9.5 %weight_grad.1 = (bf16[8,192,128]{2,1,0:T(8,128)(2,1)}, f32[64,128]{1,0:T(8,128)}) custom-call(s32[1]{0:T(128)} %bitcast.17.head, bf16[16,256,256]{2,1,0:T(8,128)(2,1)} %get-tuple-element.30.mixed, bf16[16,256,256]{2,1,0:T(8,128)(2,1)} %all_to_all.20.packed.projected, bf16[16,272,1024]{2,1,0:T(8,128)(2,1)} %bitcast.86, bf16[16,192,1024]{2,1,0:T(8,128)(2,1)} %bitcast.84, ...), custom_call_target="tpu_custom_call" | custom-call | tf_op jit(solution)/shard_map/weight_grad/pallas_call | solution.py:274
  175.9 12.3 %collective-permute-done.5.refs_3_ = bf16[4,64,256]{2,1,0:T(8,128)(2,1)S(1)} collective-permute-done((bf16[4,64,256]{2,1,0:T(8,128)(2,1)S(1)}, bf16[4,64,256]{2,1,0:T(8,128)(2,1)S(1)}, u32[]{:S(2)}, u32[]{:S(2)}) %collective-permute-start.5) | collective-permute-done | bytes 131104 | tf_op jit(solution)/shard_map/ppermute | solution.py:482
  188.2 1.7 collective-permute-done.4.refs_2_
  189.9 1.2 collective-permute-done.3.refs_1_
  191.1 0.8 copy-done.2
  191.8 0.7 out_grad.1
  192.6 1.3 collective-permute-start.6
  193.9 0.8 collective-permute-start.8
  194.7 0.7 collective-permute-start.7
  195.4 0.6 add_subtract_fusion.place
  196.0 7.4 %finish_grad.1 = bf16[128,4,1024]{2,1,0:T(4,128)(2,1)} custom-call(bf16[16,256,256]{2,1,0:T(8,128)(2,1)} %all-to-all-done.2.mixed, bf16[16,192,1024]{2,1,0:T(8,128)(2,1)} %bitcast.85, bf16[256,1024]{1,0:T(8,128)(2,1)} %get-tuple-element.31.features, f32[1,1024]{1,0:T(1,128)} %bitcast.103, bf16[256,1024]{1,0:T(8,128)(2,1)} %bitcast.78, ...), custom_call_target="tpu_custom_call" | custom-call | tf_op jit(solution)/shard_map/finish_grad/pallas_call | solution.py:406
  203.4 0.1 fusion.5
  203.6 0.1 convert.5
  203.6 0.1 fusion.3
  203.8 0.1 collective-permute-start.9
  204.0 1.9 collective-permute-done.9
  205.8 0.1 fusion.1
  206.0 0.7 collective-permute-start.10
  206.7 1.8 collective-permute-start.11
  208.5 1.9 collective-permute-start.12
  210.4 8.3 %all-to-all-start.3 = ((bf16[128,4,1024]{2,1,0:T(4,128)(2,1)}), bf16[128,4,1024]{2,1,0:T(4,128)(2,1)S(1)}, u32[]{:S(2)}, u32[]{:S(2)}) async-start(bf16[128,4,1024]{2,1,0:T(4,128)(2,1)} %finish_grad.1), calls=%async_computation.3 | async-start | bytes 2097152 | tf_op jit(solution)/shard_map/all_to_all | solution.py:549
  218.8 2.5 %collective-permute-start.14 = (f32[64,128]{1,0:T(8,128)S(1)}, f32[64,128]{1,0:T(8,128)S(1)}, u32[]{:S(2)}, u32[]{:S(2)}) collective-permute-start(f32[64,128]{1,0:T(8,128)S(1)} %slice.76), channel_id=1, source_target_pairs={{0,2},{1,3},{2,0},{3,1},{4,6},{5,7},{6,4},{7,5},{8,10},{9,11},{10,... | collective-permute-start | bytes 98312 | tf_op jit(solution)/shard_map/ppermute | solution.py:477
  221.3 1.2 collective-permute-start.15
  222.5 0.9 collective-permute-start.13
  223.3 4.3 %finish_output.1 = bf16[256,1024]{1,0:T(8,128)(2,1)} custom-call(bf16[16,256,256]{2,1,0:T(8,128)(2,1)} %all-to-all-done.2.mixed, bf16[16,64,1024]{2,1,0:T(8,128)(2,1)} %weight.3, bf16[256,1024]{1,0:T(8,128)(2,1)} %get-tuple-element.31.features), custom_call_target="tpu_custom_call" | custom-call | tf_op jit(solution)/shard_map/finish_output/pallas_call | solution.py:358
  227.7 0.6 slice.74
  228.3 5.5 %collective-permute-done.14 = f32[64,128]{1,0:T(8,128)S(1)} collective-permute-done((f32[64,128]{1,0:T(8,128)S(1)}, f32[64,128]{1,0:T(8,128)S(1)}, u32[]{:S(2)}, u32[]{:S(2)}) %collective-permute-start.14) | collective-permute-done | bytes 32800 | tf_op jit(solution)/shard_map/ppermute | solution.py:477
  233.8 0.6 add_bitcast_fusion
  234.5 0.6 copy.49
  235.1 0.6 slice_bitcast_fusion.6
  235.7 2.2 all-to-all-done.3
  237.8 1.0 copy.52
  (39 shorter events, 0.4 us)
Async XLA Ops:
  7.2 2.4 copy-start
  13.8 31.6 %all-to-all-start = ((bf16[128,4,1152]{2,1,0:T(4,128)(2,1)}), bf16[128,4,1152]{2,1,0:T(4,128)(2,1)S(1)}, u32[]{:S(2)}, u32[]{:S(2)}) async-start(bf16[128,4,1152]{2,1,0:T(4,128)(2,1)} %maximum_select_fusion), calls=%async_computation | async-start | bytes 2359296 | tf_op jit(solution)/shard_map/all_to_all | solution.py:493
  25.0 141.4 %all-gather.3.cloned.1.call-start = ((), (), s32[]{:S(2)}) async-start(), calls=%async_computation.4 | async-start | bytes 9469952 | tf_op jit(solution)/shard_map/all_gather | solution.py:515
  45.4 1.1 copy-start.3
  53.7 41.7 %copy-start.1 = (bf16[1,256,1024]{2,1,0:T(8,128)(2,1)S(1)}, bf16[1,256,1024]{2,1,0:T(8,128)(2,1)}, u32[]{:S(2)}) copy-start(bf16[1,256,1024]{2,1,0:T(8,128)(2,1)} %param.15) | copy-start | bytes 1572868
  95.4 61.1 %collective-permute-start.2 = (bf16[256,1024]{1,0:T(8,128)(2,1)S(1)}, bf16[256,1024]{1,0:T(8,128)(2,1)S(1)}, u32[]{:S(2)}, u32[]{:S(2)}) collective-permute-start(bf16[256,1024]{1,0:T(8,128)(2,1)S(1)} %bitcast.79), channel_id=1, source_target_pairs={{0,3},{1,0},{2,1},{3,2},{4,7},{5,4},{6,5},{7,6},{8,11},{9,8},{10,9... | collective-permute-start | bytes 1572872 | tf_op jit(solution)/shard_map/ppermute | solution.py:477
  95.6 60.9 %collective-permute-start.1 = (bf16[256,1024]{1,0:T(8,128)(2,1)S(1)}, bf16[256,1024]{1,0:T(8,128)(2,1)S(1)}, u32[]{:S(2)}, u32[]{:S(2)}) collective-permute-start(bf16[256,1024]{1,0:T(8,128)(2,1)S(1)} %bitcast.80), channel_id=1, source_target_pairs={{0,2},{1,3},{2,0},{3,1},{4,6},{5,7},{6,4},{7,5},{8,10},{9,11},{10,... | collective-permute-start | bytes 1572872 | tf_op jit(solution)/shard_map/ppermute | solution.py:477
  98.0 58.5 %collective-permute-start = (bf16[256,1024]{1,0:T(8,128)(2,1)S(1)}, bf16[256,1024]{1,0:T(8,128)(2,1)S(1)}, u32[]{:S(2)}, u32[]{:S(2)}) collective-permute-start(bf16[256,1024]{1,0:T(8,128)(2,1)S(1)} %bitcast.81), channel_id=1, source_target_pairs={{0,1},{1,2},{2,3},{3,0},{4,5},{5,6},{6,7},{7,4},{8,9},{9,10},{10,1... | collective-permute-start | bytes 1572872 | tf_op jit(solution)/shard_map/ppermute | solution.py:477
  156.5 5.0 %copy-start.4 = (bf16[16,64,256]{2,1,0:T(8,128)(2,1)S(1)}, bf16[16,64,256]{2,1,0:T(8,128)(2,1)}, u32[]{:S(2)}) copy-start(bf16[16,64,256]{2,1,0:T(8,128)(2,1)} %get-tuple-element.35) | copy-start | bytes 1572868
  156.6 39.4 %all-to-all-start.2 = ((bf16[16,256,256]{2,1,0:T(8,128)(2,1)}), bf16[16,256,256]{2,1,0:T(8,128)(2,1)}, u32[]{:S(2)}, u32[]{:S(2)}) async-start(bf16[16,256,256]{2,1,0:T(8,128)(2,1)} %get-tuple-element.30.mixed), calls=%async_computation.2 | async-start | bytes 4194304 | tf_op jit(solution)/shard_map/all_to_all | solution.py:522
  161.6 26.6 %collective-permute-start.5 = (bf16[4,64,256]{2,1,0:T(8,128)(2,1)S(1)}, bf16[4,64,256]{2,1,0:T(8,128)(2,1)S(1)}, u32[]{:S(2)}, u32[]{:S(2)}) collective-permute-start(bf16[4,64,256]{2,1,0:T(8,128)(2,1)S(1)} %get-tuple-element.55), channel_id=1, source_target_pairs={{0,12},{1,13},{2,14},{3,15},{4,0},{5,1},{6,2},{7,3},{8,4},{9,5},{1... | collective-permute-start | bytes 393224 | tf_op jit(solution)/shard_map/ppermute | solution.py:482
  164.7 25.2 %collective-permute-start.4 = (bf16[4,64,256]{2,1,0:T(8,128)(2,1)S(1)}, bf16[4,64,256]{2,1,0:T(8,128)(2,1)S(1)}, u32[]{:S(2)}, u32[]{:S(2)}) collective-permute-start(bf16[4,64,256]{2,1,0:T(8,128)(2,1)S(1)} %get-tuple-element.56), channel_id=1, source_target_pairs={{0,8},{1,9},{2,10},{3,11},{4,12},{5,13},{6,14},{7,15},{8,0},{9,1},... | collective-permute-start | bytes 393224 | tf_op jit(solution)/shard_map/ppermute | solution.py:482
  165.5 25.6 %collective-permute-start.3 = (bf16[4,64,256]{2,1,0:T(8,128)(2,1)S(1)}, bf16[4,64,256]{2,1,0:T(8,128)(2,1)S(1)}, u32[]{:S(2)}, u32[]{:S(2)}) collective-permute-start(bf16[4,64,256]{2,1,0:T(8,128)(2,1)S(1)} %get-tuple-element.57), channel_id=1, source_target_pairs={{0,4},{1,5},{2,6},{3,7},{4,8},{5,9},{6,10},{7,11},{8,12},{9,13},{1... | collective-permute-start | bytes 393224 | tf_op jit(solution)/shard_map/ppermute | solution.py:482
  191.1 0.8 copy-start.2
  192.6 10.8 %collective-permute-start.6 = (bf16[640,128]{1,0:T(8,128)(2,1)S(1)}, bf16[640,128]{1,0:T(8,128)(2,1)S(1)}, u32[]{:S(2)}, u32[]{:S(2)}) collective-permute-start(bf16[640,128]{1,0:T(8,128)(2,1)S(1)} %get-tuple-element.48), channel_id=1, source_target_pairs={{0,12},{1,13},{2,14},{3,15},{4,0},{5,1},{6,2},{7,3},{8,4},{9,5},{1... | collective-permute-start | bytes 491528 | tf_op jit(solution)/shard_map/ppermute | solution.py:482
  193.9 9.5 %collective-permute-start.8 = (bf16[640,128]{1,0:T(8,128)(2,1)S(1)}, bf16[640,128]{1,0:T(8,128)(2,1)S(1)}, u32[]{:S(2)}, u32[]{:S(2)}) collective-permute-start(bf16[640,128]{1,0:T(8,128)(2,1)S(1)} %get-tuple-element.49), channel_id=1, source_target_pairs={{0,4},{1,5},{2,6},{3,7},{4,8},{5,9},{6,10},{7,11},{8,12},{9,13},{1... | collective-permute-start | bytes 491528 | tf_op jit(solution)/shard_map/ppermute | solution.py:482
  194.7 8.7 %collective-permute-start.7 = (bf16[640,128]{1,0:T(8,128)(2,1)S(1)}, bf16[640,128]{1,0:T(8,128)(2,1)S(1)}, u32[]{:S(2)}, u32[]{:S(2)}) collective-permute-start(bf16[640,128]{1,0:T(8,128)(2,1)S(1)} %get-tuple-element.50), channel_id=1, source_target_pairs={{0,8},{1,9},{2,10},{3,11},{4,12},{5,13},{6,14},{7,15},{8,0},{9,1},... | collective-permute-start | bytes 491528 | tf_op jit(solution)/shard_map/ppermute | solution.py:482
  196.0 7.6 %copy-start.5 = (bf16[8,192,128]{2,1,0:T(8,128)(2,1)S(1)}, bf16[8,192,128]{2,1,0:T(8,128)(2,1)}, u32[]{:S(2)}) copy-start(bf16[8,192,128]{2,1,0:T(8,128)(2,1)} %get-tuple-element.43) | copy-start | bytes 1179652
  203.8 2.0 collective-permute-start.9
  206.0 12.6 %collective-permute-start.10 = (f32[320,128]{1,0:T(8,128)S(1)}, f32[320,128]{1,0:T(8,128)S(1)}, u32[]{:S(2)}, u32[]{:S(2)}) collective-permute-start(f32[320,128]{1,0:T(8,128)S(1)} %get-tuple-element.61), channel_id=1, source_target_pairs={{0,32},{16,48},{32,64},{48,80},{64,96},{80,112},{96,0},{112,16},{1... | collective-permute-start | bytes 491528 | tf_op jit(solution)/shard_map/ppermute | solution.py:443
  206.7 12.0 %collective-permute-start.11 = (f32[320,128]{1,0:T(8,128)S(1)}, f32[320,128]{1,0:T(8,128)S(1)}, u32[]{:S(2)}, u32[]{:S(2)}) collective-permute-start(f32[320,128]{1,0:T(8,128)S(1)} %get-tuple-element.62), channel_id=1, source_target_pairs={{0,64},{16,80},{32,96},{48,112},{64,0},{80,16},{96,32},{112,48},{1... | collective-permute-start | bytes 491528 | tf_op jit(solution)/shard_map/ppermute | solution.py:443
  208.5 10.2 %collective-permute-start.12 = (f32[320,128]{1,0:T(8,128)S(1)}, f32[320,128]{1,0:T(8,128)S(1)}, u32[]{:S(2)}, u32[]{:S(2)}) collective-permute-start(f32[320,128]{1,0:T(8,128)S(1)} %get-tuple-element.63), channel_id=1, source_target_pairs={{0,96},{16,112},{32,0},{48,16},{64,32},{80,48},{96,64},{112,80},{1... | collective-permute-start | bytes 491528 | tf_op jit(solution)/shard_map/ppermute | solution.py:443
  210.4 27.5 %all-to-all-start.3 = ((bf16[128,4,1024]{2,1,0:T(4,128)(2,1)}), bf16[128,4,1024]{2,1,0:T(4,128)(2,1)S(1)}, u32[]{:S(2)}, u32[]{:S(2)}) async-start(bf16[128,4,1024]{2,1,0:T(4,128)(2,1)} %finish_grad.1), calls=%async_computation.3 | async-start | bytes 2097152 | tf_op jit(solution)/shard_map/all_to_all | solution.py:549
  218.8 15.0 %collective-permute-start.14 = (f32[64,128]{1,0:T(8,128)S(1)}, f32[64,128]{1,0:T(8,128)S(1)}, u32[]{:S(2)}, u32[]{:S(2)}) collective-permute-start(f32[64,128]{1,0:T(8,128)S(1)} %slice.76), channel_id=1, source_target_pairs={{0,2},{1,3},{2,0},{3,1},{4,6},{5,7},{6,4},{7,5},{8,10},{9,11},{10,... | collective-permute-start | bytes 98312 | tf_op jit(solution)/shard_map/ppermute | solution.py:477
  221.3 12.5 %collective-permute-start.15 = (f32[64,128]{1,0:T(8,128)S(1)}, f32[64,128]{1,0:T(8,128)S(1)}, u32[]{:S(2)}, u32[]{:S(2)}) collective-permute-start(f32[64,128]{1,0:T(8,128)S(1)} %slice.76), channel_id=1, source_target_pairs={{0,3},{1,0},{2,1},{3,2},{4,7},{5,4},{6,5},{7,6},{8,11},{9,8},{10,9... | collective-permute-start | bytes 98312 | tf_op jit(solution)/shard_map/ppermute | solution.py:477
  222.5 11.3 %collective-permute-start.13 = (f32[64,128]{1,0:T(8,128)S(1)}, f32[64,128]{1,0:T(8,128)S(1)}, u32[]{:S(2)}, u32[]{:S(2)}) collective-permute-start(f32[64,128]{1,0:T(8,128)S(1)} %slice.76), channel_id=1, source_target_pairs={{0,1},{1,2},{2,3},{3,0},{4,5},{5,6},{6,7},{7,4},{8,9},{9,10},{10,1... | collective-permute-start | bytes 98312 | tf_op jit(solution)/shard_map/ppermute | solution.py:477
Sparse Core Ops, SparseCore 0:
  53.8 102.7 all-gather.2

commit v4 on v3

--- a/solution.py
+++ b/solution.py
@@ -125,21 +125,41 @@
 
 
 def attend_body(
-    packed, out, only, query, grad, keys, values, key_total, value_total, *, scale, shift, step
+    source,
+    out,
+    only,
+    packed,
+    query,
+    grad,
+    keys,
+    values,
+    key_total,
+    value_total,
+    arrived,
+    *,
+    scale,
+    shift,
+    step,
 ):
     shards, four, rows = packed.shape
+    copies = [
+        pltpu.make_async_copy(source.at[s], packed.at[s], arrived.at[s]) for s in range(shards)
+    ]
+    for copy in copies:
+        copy.start()
     size = four // 4
     length = shards * rows
     rate = scale * math.log2(math.e)
     offset = shift * math.log2(math.e)
+    key_total[...] = jnp.zeros_like(key_total)
+    value_total[...] = jnp.zeros_like(value_total)
     for s in range(shards):
+        copies[s].wait()
         part = slice(s * rows, (s + 1) * rows)
         query[part, :] = jnp.transpose(packed[s, :size, :])
         grad[part, :] = jnp.transpose(packed[s, 3 * size :, :])
         keys[:, part] = packed[s, size : 2 * size, :]
         values[:, part] = packed[s, 2 * size : 3 * size, :]
-    key_total[...] = jnp.zeros_like(key_total)
-    value_total[...] = jnp.zeros_like(value_total)
 
     def one_block(i, _):
         mine = pl.ds(pl.multiple_of(i * rows, rows), rows)
@@ -177,19 +197,21 @@
     size, length = four // 4, shards * rows
     return pl.pallas_call(
         functools.partial(attend_body, scale=scale, shift=shift, step=min(1024, length)),
-        in_specs=[pl.BlockSpec(memory_space=pltpu.VMEM)],
+        in_specs=[pl.BlockSpec(memory_space=pl.ANY)],
         out_specs=[pl.BlockSpec(memory_space=pltpu.VMEM)] * 2,
         out_shape=[
             jax.ShapeDtypeStruct(packed.shape, BF16),
             jax.ShapeDtypeStruct((shards, size, rows), BF16),
         ],
         scratch_shapes=[
+            pltpu.VMEM(packed.shape, BF16),
             pltpu.VMEM((length, size), BF16),
             pltpu.VMEM((length, size), BF16),
             pltpu.VMEM((size, length), BF16),
             pltpu.VMEM((size, length), BF16),
             pltpu.VMEM((size, length), F32),
             pltpu.VMEM((size, length), F32),
+            pltpu.SemaphoreType.DMA((shards,)),
         ],
         compiler_params=vmem(60),
         cost_estimate=pl.CostEstimate(
@@ -367,6 +389,7 @@
         out_shape=jax.ShapeDtypeStruct((rows, width), BF16),
         scratch_shapes=[pltpu.VMEM((rows, width), F32)],
         compiler_params=vmem(60),
+        cost_estimate=pl.CostEstimate(flops=1, bytes_accessed=1, transcendentals=0),
         name="finish_output",
     )(mixed, weight, features)
 
@@ -481,15 +504,11 @@
     def along_column(value, k):
         return lax.ppermute(value, "seq", [(i, (i + k * side) % shards) for i in range(shards)])
 
-    me = tile_index * shards + shard_index
-    my_counts = lax.dynamic_index_in_dim(counts, me, 2, keepdims=False)
-    used = jnp.arange(slots, dtype=jnp.int32) < my_counts[..., None]
     onehot = (levels[0][..., None] == jnp.arange(LANES, dtype=jnp.int32)).astype(BF16)
     embedded = tokens[0].astype(F32) + jnp.einsum(
         "msjl,ld->msjd", onehot[..., :kinds], level_table, preferred_element_type=F32
     )
     embedded = jnp.concatenate([embedded.astype(BF16), onehot], axis=-1)
-    embedded = jnp.where(used[..., None], embedded, jnp.zeros((), BF16))
     received = lax.all_to_all(
         embedded.reshape(owners, slots, width + LANES),
         ("tile", "seq"),

time: 247 us -> 245 us (level)
  transfers between devices with their start and end apart: 20 -> 20, of which waited for: 7 -> 7; matrix products, arithmetic and copies ran while one was open for 2% -> 2% of each run, Pallas kernels for 34% -> 35%
where the time goes in v4:
time: 245 us; the launch traced here: 244 us
  Pallas kernels  91.6 us (37%)
  starting transfers between devices  43.9 us (18%)
  blocking collectives  41.6 us (17%)
  waiting for transfers between devices  38.1 us (16%)
  between operations  14.6 us (6%)
  local copies, waits for them, and re-layouts  8.03 us (3%)
  other arithmetic  4.56 us (2%)
    pallas_call x1, Pallas kernels, attend(): pl.pallas_call(functools.partial(attend_body, scale=scale, shift=shift, s...  58.1 us
    all_to_all x1, blocking collectives, on_device(): lax.all_to_all(packed, 'seq', split_axis=0, concat_axis=0, tiled=True)  41.6 us
    ppermute x6, waiting for transfers between devices, along_column(): lax.ppermute(value, 'seq', [(i, (i + k * side) % shards) for i in range(s...  15.3 us
    all_to_all x1, waiting for transfers between devices, on_device(): lax.all_to_all(embedded.reshape(owners, slots, width + LANES), ('tile', '...  13.2 us
    all_to_all x1, starting transfers between devices, on_device(): lax.all_to_all(embedded.reshape(owners, slots, width + LANES), ('tile', '...  11.1 us
    pallas_call x1, Pallas kernels, weight_grad(): pl.pallas_call(functools.partial(weight_grad_body, factor=factor), grid_s...  9.5 us
    all_to_all x1, starting transfers between devices, on_device(): lax.all_to_all(outgoing, ('tile', 'seq'), split_axis=0, concat_axis=0, ti...  8.23 us
    ppermute x6, starting transfers between devices, along_column(): lax.ppermute(value, 'seq', [(i, (i + k * side) % shards) for i in range(s...  7.63 us
  transfers between devices with their start and end apart: 20, of which 7 were waited for; matrix products, arithmetic and copies ran while one was open for 2% of the time, Pallas kernels for 35%

profile of v4, /device:TPU:0, one launch (start us, length us, event | category | flops | bytes accessed | tf_op | source)
XLA Modules:
  0.0 244.2 jit_solution(2925499733359968324)
XLA Ops:
  7.2 0.0 copy-start
  7.2 1.0 iota_compare_fusion
  8.2 0.6 copy.34
  8.9 1.8 fusion
  10.7 0.1 pad_maximum_fusion
  10.8 1.5 copy.35
  12.3 11.1 %all-to-all-start = ((bf16[128,4,1152]{2,1,0:T(4,128)(2,1)}), bf16[128,4,1152]{2,1,0:T(4,128)(2,1)S(1)}, u32[]{:S(2)}, u32[]{:S(2)}) async-start(bf16[128,4,1152]{2,1,0:T(4,128)(2,1)} %bitcast.4), calls=%async_computation | async-start | bytes 2359296 | tf_op jit(solution)/shard_map/all_to_all | solution.py:512
  23.5 0.0 all-gather.3.cloned.1.call-start
  23.5 0.7 fusion.11
  24.2 0.1 copy.36
  24.3 0.2 reduce-window.8
  24.5 0.1 reduce
  24.6 0.7 bitcast_subtract_fusion
  25.3 0.2 select_reduce_fusion
  25.5 0.1 copy.37
  25.6 0.1 copy.38
  25.8 0.7 sub.42.place
  26.4 4.3 %project_grads.1.grads = bf16[16,64,256]{2,1,0:T(8,128)(2,1)} custom-call(bf16[256,1024]{1,0:T(8,128)(2,1)} %bitcast.75, bf16[16,64,1024]{2,1,0:T(8,128)(2,1)} %weight.3), custom_call_target="tpu_custom_call" | custom-call | tf_op jit(solution)/shard_map/project_grads/pallas_call | solution.py:80
  30.7 13.2 %all-to-all-done.received = bf16[128,4,1152]{2,1,0:T(4,128)(2,1)S(1)} async-done(((bf16[128,4,1152]{2,1,0:T(4,128)(2,1)}), bf16[128,4,1152]{2,1,0:T(4,128)(2,1)S(1)}, u32[]{:S(2)}, u32[]{:S(2)}) %all-to-all-start) | async-done | bytes 1179680 | tf_op jit(solution)/shard_map/all_to_all | solution.py:512
  43.9 1.0 copy-done.3
  44.9 7.3 %project.1 = (bf16[16,256,256]{2,1,0:T(8,128)(2,1)}, bf16[256,1024]{1,0:T(8,128)(2,1)}, bf16[272,1024]{1,0:T(8,128)(2,1)}, f32[8,1024]{1,0:T(8,128)}) custom-call(bf16[128,4,1152]{2,1,0:T(4,128)(2,1)} %copy-done.3, s32[256,1]{1,0:T(8,128)} %sub.42.place, f32[1,1024]{1,0:T(1,128)} %bitcast.97, bf16[256,1024]{1,0:T(8,128)(2,1)} %bitcast.76, ...), custom_call_target="tpu_custom_call" | custom-call | tf_op jit(solution)/shard_map/project/pallas_call | solution.py:99
  52.1 0.0 all-gather.3.cloned.1.call-update
  52.2 41.6 %all_to_all.20.source.projected = bf16[16,256,256]{2,1,0:T(8,128)(2,1)} all-to-all(bf16[16,256,256]{2,1,0:T(8,128)(2,1)} %get-tuple-element.25), channel_id=1, replica_groups=mesh['tile'=8,'seq'=16] {'seq'}, dimensions={0} | all-to-all | bytes 4194304 | tf_op jit(solution)/shard_map/all_to_all | solution.py:533
  93.8 0.3 collective-permute-start.2
  94.1 2.4 collective-permute-start.1
  96.5 58.1 %attend.1 = (bf16[16,256,256]{2,1,0:T(8,128)(2,1)}, bf16[16,64,256]{2,1,0:T(8,128)(2,1)}) custom-call(bf16[16,256,256]{2,1,0:T(8,128)(2,1)} %all_to_all.20.source.projected), custom_call_target="tpu_custom_call" | custom-call | flops 51539607552 | bytes 2097152 | tf_op jit(solution)/shard_map/attend/pallas_call | solution.py:198
  154.7 5.2 %all-to-all-start.2 = ((bf16[16,256,256]{2,1,0:T(8,128)(2,1)}), bf16[16,256,256]{2,1,0:T(8,128)(2,1)}, u32[]{:S(2)}, u32[]{:S(2)}) async-start(bf16[16,256,256]{2,1,0:T(8,128)(2,1)} %get-tuple-element.30.mixed), calls=%async_computation.2 | async-start | bytes 4194304 | tf_op jit(solution)/shard_map/all_to_all | solution.py:541
  160.0 0.1 dynamic-slice_bitcast_fusion.4
  160.0 3.1 %collective-permute-start.5 = (bf16[4,64,256]{2,1,0:T(8,128)(2,1)S(1)}, bf16[4,64,256]{2,1,0:T(8,128)(2,1)S(1)}, u32[]{:S(2)}, u32[]{:S(2)}) collective-permute-start(bf16[4,64,256]{2,1,0:T(8,128)(2,1)S(1)} %get-tuple-element.55), channel_id=1, source_target_pairs={{0,12},{1,13},{2,14},{3,15},{4,0},{5,1},{6,2},{7,3},{8,4},{9,5},{1... | collective-permute-start | bytes 393224 | tf_op jit(solution)/shard_map/ppermute | solution.py:505
  163.1 0.9 collective-permute-start.4
  164.0 0.9 collective-permute-start.3
  164.8 9.5 %weight_grad.1 = (bf16[8,192,128]{2,1,0:T(8,128)(2,1)}, f32[64,128]{1,0:T(8,128)}) custom-call(s32[1]{0:T(128)} %bitcast.16.head, bf16[16,256,256]{2,1,0:T(8,128)(2,1)} %get-tuple-element.30.mixed, bf16[16,256,256]{2,1,0:T(8,128)(2,1)} %all_to_all.20.source.projected, bf16[16,272,1024]{2,1,0:T(8,128)(2,1)} %bitcast.85, bf16[16,192,1024]{2,1,0:T(8,128)(2,1)} %bitcast.83, ...), custom_call_target="tpu_custom_call" | custom-call | tf_op jit(solution)/shard_map/weight_grad/pallas_call | solution.py:296
  174.3 12.5 %collective-permute-done.5.refs_3_ = bf16[4,64,256]{2,1,0:T(8,128)(2,1)S(1)} collective-permute-done((bf16[4,64,256]{2,1,0:T(8,128)(2,1)S(1)}, bf16[4,64,256]{2,1,0:T(8,128)(2,1)S(1)}, u32[]{:S(2)}, u32[]{:S(2)}) %collective-permute-start.5) | collective-permute-done | bytes 131104 | tf_op jit(solution)/shard_map/ppermute | solution.py:505
  186.8 1.7 collective-permute-done.4.refs_2_
  188.5 1.2 collective-permute-done.3.refs_1_
  189.7 0.8 copy-done.2
  190.4 0.7 out_grad.1
  191.2 1.3 collective-permute-start.6
  192.5 0.8 collective-permute-start.8
  193.3 0.7 collective-permute-start.7
  194.0 0.6 add_subtract_fusion.place
  194.6 7.4 %finish_grad.1 = bf16[128,4,1024]{2,1,0:T(4,128)(2,1)} custom-call(bf16[16,256,256]{2,1,0:T(8,128)(2,1)} %all-to-all-done.2.mixed, bf16[16,192,1024]{2,1,0:T(8,128)(2,1)} %bitcast.84, bf16[256,1024]{1,0:T(8,128)(2,1)} %get-tuple-element.31.features, f32[1,1024]{1,0:T(1,128)} %bitcast.99, bf16[256,1024]{1,0:T(8,128)(2,1)} %bitcast.77, ...), custom_call_target="tpu_custom_call" | custom-call | tf_op jit(solution)/shard_map/finish_grad/pallas_call | solution.py:429
  202.0 0.1 fusion.5
  202.2 0.1 convert.5
  202.2 0.1 fusion.3
  202.4 0.1 collective-permute-start.9
  202.5 1.9 collective-permute-done.9
  204.4 0.1 fusion.1
  204.6 0.7 collective-permute-start.10
  205.3 1.7 collective-permute-start.11
  207.1 1.9 collective-permute-start.12
  209.0 8.2 %all-to-all-start.3 = ((bf16[128,4,1024]{2,1,0:T(4,128)(2,1)}), bf16[128,4,1024]{2,1,0:T(4,128)(2,1)S(1)}, u32[]{:S(2)}, u32[]{:S(2)}) async-start(bf16[128,4,1024]{2,1,0:T(4,128)(2,1)} %finish_grad.1), calls=%async_computation.3 | async-start | bytes 2097152 | tf_op jit(solution)/shard_map/all_to_all | solution.py:568
  217.3 2.5 %collective-permute-start.14 = (f32[64,128]{1,0:T(8,128)S(1)}, f32[64,128]{1,0:T(8,128)S(1)}, u32[]{:S(2)}, u32[]{:S(2)}) collective-permute-start(f32[64,128]{1,0:T(8,128)S(1)} %slice.77), channel_id=1, source_target_pairs={{0,2},{1,3},{2,0},{3,1},{4,6},{5,7},{6,4},{7,5},{8,10},{9,11},{10,... | collective-permute-start | bytes 98312 | tf_op jit(solution)/shard_map/ppermute | solution.py:500
  219.8 1.2 collective-permute-start.15
  221.0 0.9 collective-permute-start.13
  221.8 4.3 %finish_output.1 = bf16[256,1024]{1,0:T(8,128)(2,1)} custom-call(bf16[16,256,256]{2,1,0:T(8,128)(2,1)} %all-to-all-done.2.mixed, bf16[16,64,1024]{2,1,0:T(8,128)(2,1)} %weight.3, bf16[256,1024]{1,0:T(8,128)(2,1)} %get-tuple-element.31.features), custom_call_target="tpu_custom_call" | custom-call | flops 1 | bytes 1 | tf_op jit(solution)/shard_map/finish_output/pallas_call | solution.py:380
  226.2 0.6 slice.75
  226.8 5.5 %collective-permute-done.14 = f32[64,128]{1,0:T(8,128)S(1)} collective-permute-done((f32[64,128]{1,0:T(8,128)S(1)}, f32[64,128]{1,0:T(8,128)S(1)}, u32[]{:S(2)}, u32[]{:S(2)}) %collective-permute-start.14) | collective-permute-done | bytes 32800 | tf_op jit(solution)/shard_map/ppermute | solution.py:500
  232.3 0.0 collective-permute-done.13
  232.3 0.6 add_bitcast_fusion
  233.0 0.6 copy.45
  233.6 0.6 slice_bitcast_fusion.6
  234.2 2.2 all-to-all-done.3
  236.4 1.0 copy.48
  (37 shorter events, 0.4 us)
Async XLA Ops:
  7.2 1.7 copy-start
  12.3 31.6 %all-to-all-start = ((bf16[128,4,1152]{2,1,0:T(4,128)(2,1)}), bf16[128,4,1152]{2,1,0:T(4,128)(2,1)S(1)}, u32[]{:S(2)}, u32[]{:S(2)}) async-start(bf16[128,4,1152]{2,1,0:T(4,128)(2,1)} %bitcast.4), calls=%async_computation | async-start | bytes 2359296 | tf_op jit(solution)/shard_map/all_to_all | solution.py:512
  23.5 141.4 %all-gather.3.cloned.1.call-start = ((), (), s32[]{:S(2)}) async-start(), calls=%async_computation.4 | async-start | bytes 9469952 | tf_op jit(solution)/shard_map/all_gather | solution.py:534
  43.9 1.0 copy-start.3
  52.2 41.7 %copy-start.1 = (bf16[1,256,1024]{2,1,0:T(8,128)(2,1)S(1)}, bf16[1,256,1024]{2,1,0:T(8,128)(2,1)}, u32[]{:S(2)}) copy-start(bf16[1,256,1024]{2,1,0:T(8,128)(2,1)} %param.15) | copy-start | bytes 1572868
  93.8 60.8 %collective-permute-start.2 = (bf16[256,1024]{1,0:T(8,128)(2,1)S(1)}, bf16[256,1024]{1,0:T(8,128)(2,1)S(1)}, u32[]{:S(2)}, u32[]{:S(2)}) collective-permute-start(bf16[256,1024]{1,0:T(8,128)(2,1)S(1)} %bitcast.78), channel_id=1, source_target_pairs={{0,3},{1,0},{2,1},{3,2},{4,7},{5,4},{6,5},{7,6},{8,11},{9,8},{10,9... | collective-permute-start | bytes 1572872 | tf_op jit(solution)/shard_map/ppermute | solution.py:500
  94.1 60.5 %collective-permute-start.1 = (bf16[256,1024]{1,0:T(8,128)(2,1)S(1)}, bf16[256,1024]{1,0:T(8,128)(2,1)S(1)}, u32[]{:S(2)}, u32[]{:S(2)}) collective-permute-start(bf16[256,1024]{1,0:T(8,128)(2,1)S(1)} %bitcast.79), channel_id=1, source_target_pairs={{0,2},{1,3},{2,0},{3,1},{4,6},{5,7},{6,4},{7,5},{8,10},{9,11},{10,... | collective-permute-start | bytes 1572872 | tf_op jit(solution)/shard_map/ppermute | solution.py:500
  96.5 58.2 %collective-permute-start = (bf16[256,1024]{1,0:T(8,128)(2,1)S(1)}, bf16[256,1024]{1,0:T(8,128)(2,1)S(1)}, u32[]{:S(2)}, u32[]{:S(2)}) collective-permute-start(bf16[256,1024]{1,0:T(8,128)(2,1)S(1)} %bitcast.80), channel_id=1, source_target_pairs={{0,1},{1,2},{2,3},{3,0},{4,5},{5,6},{6,7},{7,4},{8,9},{9,10},{10,1... | collective-permute-start | bytes 1572872 | tf_op jit(solution)/shard_map/ppermute | solution.py:500
  154.7 5.3 %copy-start.4 = (bf16[16,64,256]{2,1,0:T(8,128)(2,1)S(1)}, bf16[16,64,256]{2,1,0:T(8,128)(2,1)}, u32[]{:S(2)}) copy-start(bf16[16,64,256]{2,1,0:T(8,128)(2,1)} %get-tuple-element.35) | copy-start | bytes 1572868
  154.7 39.9 %all-to-all-start.2 = ((bf16[16,256,256]{2,1,0:T(8,128)(2,1)}), bf16[16,256,256]{2,1,0:T(8,128)(2,1)}, u32[]{:S(2)}, u32[]{:S(2)}) async-start(bf16[16,256,256]{2,1,0:T(8,128)(2,1)} %get-tuple-element.30.mixed), calls=%async_computation.2 | async-start | bytes 4194304 | tf_op jit(solution)/shard_map/all_to_all | solution.py:541
  160.0 26.8 %collective-permute-start.5 = (bf16[4,64,256]{2,1,0:T(8,128)(2,1)S(1)}, bf16[4,64,256]{2,1,0:T(8,128)(2,1)S(1)}, u32[]{:S(2)}, u32[]{:S(2)}) collective-permute-start(bf16[4,64,256]{2,1,0:T(8,128)(2,1)S(1)} %get-tuple-element.55), channel_id=1, source_target_pairs={{0,12},{1,13},{2,14},{3,15},{4,0},{5,1},{6,2},{7,3},{8,4},{9,5},{1... | collective-permute-start | bytes 393224 | tf_op jit(solution)/shard_map/ppermute | solution.py:505
  163.1 25.4 %collective-permute-start.4 = (bf16[4,64,256]{2,1,0:T(8,128)(2,1)S(1)}, bf16[4,64,256]{2,1,0:T(8,128)(2,1)S(1)}, u32[]{:S(2)}, u32[]{:S(2)}) collective-permute-start(bf16[4,64,256]{2,1,0:T(8,128)(2,1)S(1)} %get-tuple-element.56), channel_id=1, source_target_pairs={{0,8},{1,9},{2,10},{3,11},{4,12},{5,13},{6,14},{7,15},{8,0},{9,1},... | collective-permute-start | bytes 393224 | tf_op jit(solution)/shard_map/ppermute | solution.py:505
  164.0 25.7 %collective-permute-start.3 = (bf16[4,64,256]{2,1,0:T(8,128)(2,1)S(1)}, bf16[4,64,256]{2,1,0:T(8,128)(2,1)S(1)}, u32[]{:S(2)}, u32[]{:S(2)}) collective-permute-start(bf16[4,64,256]{2,1,0:T(8,128)(2,1)S(1)} %get-tuple-element.57), channel_id=1, source_target_pairs={{0,4},{1,5},{2,6},{3,7},{4,8},{5,9},{6,10},{7,11},{8,12},{9,13},{1... | collective-permute-start | bytes 393224 | tf_op jit(solution)/shard_map/ppermute | solution.py:505
  189.7 0.8 copy-start.2
  191.2 10.8 %collective-permute-start.6 = (bf16[640,128]{1,0:T(8,128)(2,1)S(1)}, bf16[640,128]{1,0:T(8,128)(2,1)S(1)}, u32[]{:S(2)}, u32[]{:S(2)}) collective-permute-start(bf16[640,128]{1,0:T(8,128)(2,1)S(1)} %get-tuple-element.48), channel_id=1, source_target_pairs={{0,12},{1,13},{2,14},{3,15},{4,0},{5,1},{6,2},{7,3},{8,4},{9,5},{1... | collective-permute-start | bytes 491528 | tf_op jit(solution)/shard_map/ppermute | solution.py:505
  192.5 9.5 %collective-permute-start.8 = (bf16[640,128]{1,0:T(8,128)(2,1)S(1)}, bf16[640,128]{1,0:T(8,128)(2,1)S(1)}, u32[]{:S(2)}, u32[]{:S(2)}) collective-permute-start(bf16[640,128]{1,0:T(8,128)(2,1)S(1)} %get-tuple-element.49), channel_id=1, source_target_pairs={{0,4},{1,5},{2,6},{3,7},{4,8},{5,9},{6,10},{7,11},{8,12},{9,13},{1... | collective-permute-start | bytes 491528 | tf_op jit(solution)/shard_map/ppermute | solution.py:505
  193.3 8.7 %collective-permute-start.7 = (bf16[640,128]{1,0:T(8,128)(2,1)S(1)}, bf16[640,128]{1,0:T(8,128)(2,1)S(1)}, u32[]{:S(2)}, u32[]{:S(2)}) collective-permute-start(bf16[640,128]{1,0:T(8,128)(2,1)S(1)} %get-tuple-element.50), channel_id=1, source_target_pairs={{0,8},{1,9},{2,10},{3,11},{4,12},{5,13},{6,14},{7,15},{8,0},{9,1},... | collective-permute-start | bytes 491528 | tf_op jit(solution)/shard_map/ppermute | solution.py:505
  194.6 7.6 %copy-start.5 = (bf16[8,192,128]{2,1,0:T(8,128)(2,1)S(1)}, bf16[8,192,128]{2,1,0:T(8,128)(2,1)}, u32[]{:S(2)}) copy-start(bf16[8,192,128]{2,1,0:T(8,128)(2,1)} %get-tuple-element.43) | copy-start | bytes 1179652
  202.4 2.0 collective-permute-start.9
  204.6 12.6 %collective-permute-start.10 = (f32[320,128]{1,0:T(8,128)S(1)}, f32[320,128]{1,0:T(8,128)S(1)}, u32[]{:S(2)}, u32[]{:S(2)}) collective-permute-start(f32[320,128]{1,0:T(8,128)S(1)} %get-tuple-element.61), channel_id=1, source_target_pairs={{0,32},{16,48},{32,64},{48,80},{64,96},{80,112},{96,0},{112,16},{1... | collective-permute-start | bytes 491528 | tf_op jit(solution)/shard_map/ppermute | solution.py:466
  205.3 11.9 %collective-permute-start.11 = (f32[320,128]{1,0:T(8,128)S(1)}, f32[320,128]{1,0:T(8,128)S(1)}, u32[]{:S(2)}, u32[]{:S(2)}) collective-permute-start(f32[320,128]{1,0:T(8,128)S(1)} %get-tuple-element.62), channel_id=1, source_target_pairs={{0,64},{16,80},{32,96},{48,112},{64,0},{80,16},{96,32},{112,48},{1... | collective-permute-start | bytes 491528 | tf_op jit(solution)/shard_map/ppermute | solution.py:466
  207.1 10.2 %collective-permute-start.12 = (f32[320,128]{1,0:T(8,128)S(1)}, f32[320,128]{1,0:T(8,128)S(1)}, u32[]{:S(2)}, u32[]{:S(2)}) collective-permute-start(f32[320,128]{1,0:T(8,128)S(1)} %get-tuple-element.63), channel_id=1, source_target_pairs={{0,96},{16,112},{32,0},{48,16},{64,32},{80,48},{96,64},{112,80},{1... | collective-permute-start | bytes 491528 | tf_op jit(solution)/shard_map/ppermute | solution.py:466
  209.0 27.4 %all-to-all-start.3 = ((bf16[128,4,1024]{2,1,0:T(4,128)(2,1)}), bf16[128,4,1024]{2,1,0:T(4,128)(2,1)S(1)}, u32[]{:S(2)}, u32[]{:S(2)}) async-start(bf16[128,4,1024]{2,1,0:T(4,128)(2,1)} %finish_grad.1), calls=%async_computation.3 | async-start | bytes 2097152 | tf_op jit(solution)/shard_map/all_to_all | solution.py:568
  217.3 15.0 %collective-permute-start.14 = (f32[64,128]{1,0:T(8,128)S(1)}, f32[64,128]{1,0:T(8,128)S(1)}, u32[]{:S(2)}, u32[]{:S(2)}) collective-permute-start(f32[64,128]{1,0:T(8,128)S(1)} %slice.77), channel_id=1, source_target_pairs={{0,2},{1,3},{2,0},{3,1},{4,6},{5,7},{6,4},{7,5},{8,10},{9,11},{10,... | collective-permute-start | bytes 98312 | tf_op jit(solution)/shard_map/ppermute | solution.py:500
  219.8 12.5 %collective-permute-start.15 = (f32[64,128]{1,0:T(8,128)S(1)}, f32[64,128]{1,0:T(8,128)S(1)}, u32[]{:S(2)}, u32[]{:S(2)}) collective-permute-start(f32[64,128]{1,0:T(8,128)S(1)} %slice.77), channel_id=1, source_target_pairs={{0,3},{1,0},{2,1},{3,2},{4,7},{5,4},{6,5},{7,6},{8,11},{9,8},{10,9... | collective-permute-start | bytes 98312 | tf_op jit(solution)/shard_map/ppermute | solution.py:500
  221.0 11.3 %collective-permute-start.13 = (f32[64,128]{1,0:T(8,128)S(1)}, f32[64,128]{1,0:T(8,128)S(1)}, u32[]{:S(2)}, u32[]{:S(2)}) collective-permute-start(f32[64,128]{1,0:T(8,128)S(1)} %slice.77), channel_id=1, source_target_pairs={{0,1},{1,2},{2,3},{3,0},{4,5},{5,6},{6,7},{7,4},{8,9},{9,10},{10,1... | collective-permute-start | bytes 98312 | tf_op jit(solution)/shard_map/ppermute | solution.py:500
Sparse Core Ops, SparseCore 0:
  52.3 102.7 all-gather.2

commit v5 on v4

--- a/solution.py
+++ b/solution.py
@@ -127,8 +127,9 @@
 def attend_body(
     source,
     out,
-    only,
     packed,
+    by_query,
+    by_key,
     query,
     grad,
     keys,
@@ -136,6 +137,7 @@
     key_total,
     value_total,
     arrived,
+    left,
     *,
     scale,
     shift,
@@ -147,6 +149,15 @@
     ]
     for copy in copies:
         copy.start()
+
+    def leave(s):
+        rows = pl.ds(0, by_query.shape[1])
+        return pltpu.make_async_copy(by_query.at[s], out.at[s, rows], left.at[0, s])
+
+    def leave_last(s):
+        rows = pl.ds(by_query.shape[1], by_key.shape[1])
+        return pltpu.make_async_copy(by_key.at[s], out.at[s, rows], left.at[1, s])
+
     size = four // 4
     length = shards * rows
     rate = scale * math.log2(math.e)
@@ -180,16 +191,20 @@
             grad_query = grad_query + dot(k, grad_scores, 1, 1)
             key_total[:, part] += dot(q_across, grad_scores, 1, 0)
             value_total[:, part] += dot(g_across, weights, 1, 0)
-        out[i, :size, :] = attended.astype(BF16)
-        only[i] = attended.astype(BF16)
-        out[i, size : 2 * size, :] = (grad_query * scale).astype(BF16)
+        by_query[i, :size, :] = attended.astype(BF16)
+        by_query[i, size:, :] = (grad_query * scale).astype(BF16)
+        leave(i).start()
         return 0
 
     lax.fori_loop(0, shards, one_block, 0)
     for s in range(shards):
         part = slice(s * rows, (s + 1) * rows)
-        out[s, 2 * size : 3 * size, :] = (key_total[:, part] * scale).astype(BF16)
-        out[s, 3 * size :, :] = value_total[:, part].astype(BF16)
+        by_key[s, :size, :] = (key_total[:, part] * scale).astype(BF16)
+        by_key[s, size:, :] = value_total[:, part].astype(BF16)
+        leave_last(s).start()
+    for s in range(shards):
+        leave(s).wait()
+        leave_last(s).wait()
 
 
 def attend(packed, scale, shift):
@@ -198,13 +213,12 @@
     return pl.pallas_call(
         functools.partial(attend_body, scale=scale, shift=shift, step=min(1024, length)),
         in_specs=[pl.BlockSpec(memory_space=pl.ANY)],
-        out_specs=[pl.BlockSpec(memory_space=pltpu.VMEM)] * 2,
-        out_shape=[
-            jax.ShapeDtypeStruct(packed.shape, BF16),
-            jax.ShapeDtypeStruct((shards, size, rows), BF16),
-        ],
+        out_specs=pl.BlockSpec(memory_space=pl.ANY),
+        out_shape=jax.ShapeDtypeStruct(packed.shape, BF16),
         scratch_shapes=[
             pltpu.VMEM(packed.shape, BF16),
+            pltpu.VMEM((shards, 2 * size, rows), BF16),
+            pltpu.VMEM((shards, 2 * size, rows), BF16),
             pltpu.VMEM((length, size), BF16),
             pltpu.VMEM((length, size), BF16),
             pltpu.VMEM((size, length), BF16),
@@ -212,6 +226,7 @@
             pltpu.VMEM((size, length), F32),
             pltpu.VMEM((size, length), F32),
             pltpu.SemaphoreType.DMA((shards,)),
+            pltpu.SemaphoreType.DMA((2, shards)),
         ],
         compiler_params=vmem(60),
         cost_estimate=pl.CostEstimate(
@@ -519,6 +534,7 @@
     map_counts = lax.dynamic_index_in_dim(counts, tile_index, 0, keepdims=False)
     own_counts = lax.dynamic_index_in_dim(map_counts, shard_index, 0, keepdims=False)
     place = pack_positions(own_counts, rows, slots)
+    received, place_row = lax.optimization_barrier((received, place.reshape(1, rows)))
     gain = norm_gain.reshape(1, width)
     weight = project_weight.reshape(count, 3 * size, width)
 
@@ -534,10 +550,8 @@
     all_normed = lax.all_gather(normed, "seq")
     by_head, line_rows = lax.optimization_barrier((by_head, grad_rows))
     line_rows = [line_rows] + [along_line(line_rows, k) for k in range(1, side)]
-    attended, head_attended = attend(by_head, scale, shift)
-    attended, head_attended, line_rows = lax.optimization_barrier(
-        (attended, head_attended, line_rows)
-    )
+    attended = attend(by_head, scale, shift)
+    attended, line_rows = lax.optimization_barrier((attended, line_rows))
     mixed = lax.all_to_all(attended, "seq", split_axis=0, concat_axis=0, tiled=True)
 
     shares, small = weight_grad(
@@ -551,7 +565,7 @@
         tiles,
         factor,
     )
-    head_attended = head_attended.reshape(side, side, size, rows)
+    head_attended = attended.reshape(side, side, 4 * size, rows)[:, :, :size]
     column_attended = [pick(head_attended, line)] + [
         along_column(pick(head_attended, (line + k) % side), k) for k in range(1, side)
     ]
@@ -561,7 +575,7 @@
         out_shares[0].astype(F32),
     )
     outgoing = finish_grad(
-        mixed, weight, features, gain, grad_rows, place.reshape(1, rows), owners, slots
+        mixed, weight, features, gain, grad_rows, place_row, owners, slots
     )
     output = finish_output(mixed, output_weight, features)
     outgoing, out_shares, shares = lax.optimization_barrier((outgoing, out_shares, shares))

time: 245 us -> 245 us (level)
  transfers between devices with their start and end apart: 20 -> 20, of which waited for: 7 -> 7; matrix products, arithmetic and copies ran while one was open for 2% -> 3% of each run, Pallas kernels for 35% -> 35%
where the time goes in v5:
time: 245 us; the launch traced here: 243 us
  Pallas kernels  91.5 us (37%)
  starting transfers between devices  43.8 us (18%)
  blocking collectives  41.6 us (17%)
  waiting for transfers between devices  36.4 us (15%)
  between operations  14.6 us (6%)
  local copies, waits for them, and re-layouts  9.15 us (4%)
  other arithmetic  4.56 us (2%)
    pallas_call x1, Pallas kernels, attend(): pl.pallas_call(functools.partial(attend_body, scale=scale, shift=shift, s...  58 us
    all_to_all x1, blocking collectives, on_device(): lax.all_to_all(packed, 'seq', split_axis=0, concat_axis=0, tiled=True)  41.6 us
    ppermute x6, waiting for transfers between devices, along_column(): lax.ppermute(value, 'seq', [(i, (i + k * side) % shards) for i in range(s...  14.2 us
    all_to_all x1, waiting for transfers between devices, on_device(): lax.all_to_all(embedded.reshape(owners, slots, width + LANES), ('tile', '...  12.6 us
    all_to_all x1, starting transfers between devices, on_device(): lax.all_to_all(embedded.reshape(owners, slots, width + LANES), ('tile', '...  11.1 us
    pallas_call x1, Pallas kernels, weight_grad(): pl.pallas_call(functools.partial(weight_grad_body, factor=factor), grid_s...  9.5 us
    all_to_all x1, starting transfers between devices, on_device(): lax.all_to_all(outgoing, ('tile', 'seq'), split_axis=0, concat_axis=0, ti...  8.22 us
    ppermute x6, starting transfers between devices, along_column(): lax.ppermute(value, 'seq', [(i, (i + k * side) % shards) for i in range(s...  7.65 us
  transfers between devices with their start and end apart: 20, of which 7 were waited for; matrix products, arithmetic and copies ran while one was open for 3% of the time, Pallas kernels for 35%

profile of v5, /device:TPU:0, one launch (start us, length us, event | category | flops | bytes accessed | tf_op | source)
XLA Modules:
  0.0 243.4 jit_solution(10726191706128328607)
XLA Ops:
  7.2 1.0 iota_compare_fusion
  8.2 0.6 copy.34
  8.9 1.8 fusion
  10.7 0.1 pad_maximum_fusion
  10.8 1.5 copy.35
  12.3 11.1 %all-to-all-start = ((bf16[128,4,1152]{2,1,0:T(4,128)(2,1)}), bf16[128,4,1152]{2,1,0:T(4,128)(2,1)S(1)}, u32[]{:S(2)}, u32[]{:S(2)}) async-start(bf16[128,4,1152]{2,1,0:T(4,128)(2,1)} %bitcast.4), calls=%async_computation | async-start | bytes 2359296 | tf_op jit(solution)/shard_map/all_to_all | solution.py:527
  23.5 0.0 all-gather.3.cloned.1.call-start
  23.5 0.7 fusion.11
  24.2 0.1 copy.36
  24.4 0.2 reduce-window.8
  24.5 0.1 reduce
  24.6 0.7 bitcast_subtract_fusion
  25.3 0.2 convert_reduce_fusion
  25.5 0.1 copy.37
  25.7 0.1 copy.38
  25.8 0.7 sub.43.place
  26.5 4.3 %project_grads.1.grads = bf16[16,64,256]{2,1,0:T(8,128)(2,1)} custom-call(bf16[256,1024]{1,0:T(8,128)(2,1)} %bitcast.75, bf16[16,64,1024]{2,1,0:T(8,128)(2,1)} %weight.3), custom_call_target="tpu_custom_call" | custom-call | tf_op jit(solution)/shard_map/project_grads/pallas_call | solution.py:80
  30.7 0.6 add_subtract_fusion.place
  31.3 12.6 %all-to-all-done.received = bf16[128,4,1152]{2,1,0:T(4,128)(2,1)S(1)} async-done(((bf16[128,4,1152]{2,1,0:T(4,128)(2,1)}), bf16[128,4,1152]{2,1,0:T(4,128)(2,1)S(1)}, u32[]{:S(2)}, u32[]{:S(2)}) %all-to-all-start) | async-done | bytes 1179680 | tf_op jit(solution)/shard_map/all_to_all | solution.py:527
  43.9 1.0 copy-done.3
  44.9 7.3 %project.1 = (bf16[16,256,256]{2,1,0:T(8,128)(2,1)}, bf16[256,1024]{1,0:T(8,128)(2,1)}, bf16[272,1024]{1,0:T(8,128)(2,1)}, f32[8,1024]{1,0:T(8,128)}) custom-call(bf16[128,4,1152]{2,1,0:T(4,128)(2,1)} %copy-done.3, s32[256,1]{1,0:T(8,128)} %sub.43.place, f32[1,1024]{1,0:T(1,128)} %bitcast.97, bf16[256,1024]{1,0:T(8,128)(2,1)} %bitcast.76, ...), custom_call_target="tpu_custom_call" | custom-call | tf_op jit(solution)/shard_map/project/pallas_call | solution.py:99
  52.2 0.0 all-gather.3.cloned.1.call-update
  52.2 41.6 %all_to_all.20.source.projected = bf16[16,256,256]{2,1,0:T(8,128)(2,1)} all-to-all(bf16[16,256,256]{2,1,0:T(8,128)(2,1)} %get-tuple-element.25), channel_id=1, replica_groups=mesh['tile'=8,'seq'=16] {'seq'}, dimensions={0} | all-to-all | bytes 4194304 | tf_op jit(solution)/shard_map/all_to_all | solution.py:549
  93.9 0.3 collective-permute-start.2
  94.1 2.4 collective-permute-start.1
  96.5 58.0 %attend.1.mixed = bf16[16,256,256]{2,1,0:T(8,128)(2,1)} custom-call(bf16[16,256,256]{2,1,0:T(8,128)(2,1)} %all_to_all.20.source.projected), custom_call_target="tpu_custom_call" | custom-call | flops 51539607552 | bytes 2097152 | tf_op jit(solution)/shard_map/attend/pallas_call | solution.py:213
  154.6 5.1 %all-to-all-start.2 = ((bf16[16,256,256]{2,1,0:T(8,128)(2,1)}), bf16[16,256,256]{2,1,0:T(8,128)(2,1)}, u32[]{:S(2)}, u32[]{:S(2)}) async-start(bf16[16,256,256]{2,1,0:T(8,128)(2,1)} %attend.1.mixed), calls=%async_computation.2 | async-start | bytes 4194304 | tf_op jit(solution)/shard_map/all_to_all | solution.py:555
  159.7 1.1 slice.73
  160.8 0.1 dynamic-slice_bitcast_fusion.4
  160.9 3.1 %collective-permute-start.5 = (bf16[4,64,256]{2,1,0:T(8,128)(2,1)S(1)}, bf16[4,64,256]{2,1,0:T(8,128)(2,1)S(1)}, u32[]{:S(2)}, u32[]{:S(2)}) collective-permute-start(bf16[4,64,256]{2,1,0:T(8,128)(2,1)S(1)} %get-tuple-element.53), channel_id=1, source_target_pairs={{0,12},{1,13},{2,14},{3,15},{4,0},{5,1},{6,2},{7,3},{8,4},{9,5},{1... | collective-permute-start | bytes 393224 | tf_op jit(solution)/shard_map/ppermute | solution.py:520
  164.0 0.9 collective-permute-start.4
  164.9 0.9 collective-permute-start.3
  165.7 9.5 %weight_grad.1 = (bf16[8,192,128]{2,1,0:T(8,128)(2,1)}, f32[64,128]{1,0:T(8,128)}) custom-call(s32[1]{0:T(128)} %bitcast.16.head, bf16[16,256,256]{2,1,0:T(8,128)(2,1)} %attend.1.mixed, bf16[16,256,256]{2,1,0:T(8,128)(2,1)} %all_to_all.20.source.projected, bf16[16,272,1024]{2,1,0:T(8,128)(2,1)} %bitcast.86, bf16[16,192,1024]{2,1,0:T(8,128)(2,1)} %bitcast.83, ...), custom_call_target="tpu_custom_call" | custom-call | tf_op jit(solution)/shard_map/weight_grad/pallas_call | solution.py:311
  175.2 11.4 %collective-permute-done.5.refs_3_ = bf16[4,64,256]{2,1,0:T(8,128)(2,1)S(1)} collective-permute-done((bf16[4,64,256]{2,1,0:T(8,128)(2,1)S(1)}, bf16[4,64,256]{2,1,0:T(8,128)(2,1)S(1)}, u32[]{:S(2)}, u32[]{:S(2)}) %collective-permute-start.5) | collective-permute-done | bytes 131104 | tf_op jit(solution)/shard_map/ppermute | solution.py:520
  186.6 1.7 collective-permute-done.4.refs_2_
  188.3 1.1 collective-permute-done.3.refs_1_
  189.4 0.8 copy-done.2
  190.2 0.7 out_grad.1
  191.0 1.3 collective-permute-start.6
  192.2 0.8 collective-permute-start.8
  193.1 0.7 collective-permute-start.7
  193.8 7.4 %finish_grad.1 = bf16[128,4,1024]{2,1,0:T(4,128)(2,1)} custom-call(bf16[16,256,256]{2,1,0:T(8,128)(2,1)} %all-to-all-done.2.mixed, bf16[16,192,1024]{2,1,0:T(8,128)(2,1)} %bitcast.84, bf16[256,1024]{1,0:T(8,128)(2,1)} %get-tuple-element.29.features, f32[1,1024]{1,0:T(1,128)} %bitcast.99, bf16[256,1024]{1,0:T(8,128)(2,1)} %bitcast.77, ...), custom_call_target="tpu_custom_call" | custom-call | tf_op jit(solution)/shard_map/finish_grad/pallas_call | solution.py:444
  201.2 0.1 fusion.5
  201.4 0.1 convert.5
  201.4 0.1 fusion.3
  201.6 0.1 collective-permute-start.9
  201.7 1.9 collective-permute-done.9
  203.6 0.1 fusion.1
  203.8 0.7 collective-permute-start.10
  204.5 1.7 collective-permute-start.11
  206.3 1.9 collective-permute-start.12
  208.2 8.2 %all-to-all-start.3 = ((bf16[128,4,1024]{2,1,0:T(4,128)(2,1)}), bf16[128,4,1024]{2,1,0:T(4,128)(2,1)S(1)}, u32[]{:S(2)}, u32[]{:S(2)}) async-start(bf16[128,4,1024]{2,1,0:T(4,128)(2,1)} %finish_grad.1), calls=%async_computation.3 | async-start | bytes 2097152 | tf_op jit(solution)/shard_map/all_to_all | solution.py:582
  216.5 2.5 %collective-permute-start.14 = (f32[64,128]{1,0:T(8,128)S(1)}, f32[64,128]{1,0:T(8,128)S(1)}, u32[]{:S(2)}, u32[]{:S(2)}) collective-permute-start(f32[64,128]{1,0:T(8,128)S(1)} %slice.82), channel_id=1, source_target_pairs={{0,2},{1,3},{2,0},{3,1},{4,6},{5,7},{6,4},{7,5},{8,10},{9,11},{10,... | collective-permute-start | bytes 98312 | tf_op jit(solution)/shard_map/ppermute | solution.py:515
  219.0 1.2 collective-permute-start.15
  220.2 0.9 collective-permute-start.13
  221.0 4.3 %finish_output.1 = bf16[256,1024]{1,0:T(8,128)(2,1)} custom-call(bf16[16,256,256]{2,1,0:T(8,128)(2,1)} %all-to-all-done.2.mixed, bf16[16,64,1024]{2,1,0:T(8,128)(2,1)} %weight.3, bf16[256,1024]{1,0:T(8,128)(2,1)} %get-tuple-element.29.features), custom_call_target="tpu_custom_call" | custom-call | flops 1 | bytes 1 | tf_op jit(solution)/shard_map/finish_output/pallas_call | solution.py:395
  225.4 0.6 slice.80
  226.0 5.5 %collective-permute-done.14 = f32[64,128]{1,0:T(8,128)S(1)} collective-permute-done((f32[64,128]{1,0:T(8,128)S(1)}, f32[64,128]{1,0:T(8,128)S(1)}, u32[]{:S(2)}, u32[]{:S(2)}) %collective-permute-start.14) | collective-permute-done | bytes 32800 | tf_op jit(solution)/shard_map/ppermute | solution.py:515
  231.5 0.0 collective-permute-done.13
  231.5 0.6 add_bitcast_fusion
  232.2 0.6 copy.45
  232.8 0.6 slice_bitcast_fusion.6
  233.4 2.2 all-to-all-done.3
  235.6 1.0 copy.48
  (36 shorter events, 0.4 us)
Async XLA Ops:
  7.2 1.7 copy-start
  12.3 31.6 %all-to-all-start = ((bf16[128,4,1152]{2,1,0:T(4,128)(2,1)}), bf16[128,4,1152]{2,1,0:T(4,128)(2,1)S(1)}, u32[]{:S(2)}, u32[]{:S(2)}) async-start(bf16[128,4,1152]{2,1,0:T(4,128)(2,1)} %bitcast.4), calls=%async_computation | async-start | bytes 2359296 | tf_op jit(solution)/shard_map/all_to_all | solution.py:527
  23.5 142.2 %all-gather.3.cloned.1.call-start = ((), (), s32[]{:S(2)}) async-start(), calls=%async_computation.4 | async-start | bytes 9469952 | tf_op jit(solution)/shard_map/all_gather | solution.py:550
  43.9 1.0 copy-start.3
  52.2 41.7 %copy-start.1 = (bf16[1,256,1024]{2,1,0:T(8,128)(2,1)S(1)}, bf16[1,256,1024]{2,1,0:T(8,128)(2,1)}, u32[]{:S(2)}) copy-start(bf16[1,256,1024]{2,1,0:T(8,128)(2,1)} %param.15) | copy-start | bytes 1572868
  93.9 60.7 %collective-permute-start.2 = (bf16[256,1024]{1,0:T(8,128)(2,1)S(1)}, bf16[256,1024]{1,0:T(8,128)(2,1)S(1)}, u32[]{:S(2)}, u32[]{:S(2)}) collective-permute-start(bf16[256,1024]{1,0:T(8,128)(2,1)S(1)} %bitcast.78), channel_id=1, source_target_pairs={{0,3},{1,0},{2,1},{3,2},{4,7},{5,4},{6,5},{7,6},{8,11},{9,8},{10,9... | collective-permute-start | bytes 1572872 | tf_op jit(solution)/shard_map/ppermute | solution.py:515
  94.1 60.4 %collective-permute-start.1 = (bf16[256,1024]{1,0:T(8,128)(2,1)S(1)}, bf16[256,1024]{1,0:T(8,128)(2,1)S(1)}, u32[]{:S(2)}, u32[]{:S(2)}) collective-permute-start(bf16[256,1024]{1,0:T(8,128)(2,1)S(1)} %bitcast.79), channel_id=1, source_target_pairs={{0,2},{1,3},{2,0},{3,1},{4,6},{5,7},{6,4},{7,5},{8,10},{9,11},{10,... | collective-permute-start | bytes 1572872 | tf_op jit(solution)/shard_map/ppermute | solution.py:515
  96.5 58.0 %collective-permute-start = (bf16[256,1024]{1,0:T(8,128)(2,1)S(1)}, bf16[256,1024]{1,0:T(8,128)(2,1)S(1)}, u32[]{:S(2)}, u32[]{:S(2)}) collective-permute-start(bf16[256,1024]{1,0:T(8,128)(2,1)S(1)} %bitcast.80), channel_id=1, source_target_pairs={{0,1},{1,2},{2,3},{3,0},{4,5},{5,6},{6,7},{7,4},{8,9},{9,10},{10,1... | collective-permute-start | bytes 1572872 | tf_op jit(solution)/shard_map/ppermute | solution.py:515
  154.6 39.2 %all-to-all-start.2 = ((bf16[16,256,256]{2,1,0:T(8,128)(2,1)}), bf16[16,256,256]{2,1,0:T(8,128)(2,1)}, u32[]{:S(2)}, u32[]{:S(2)}) async-start(bf16[16,256,256]{2,1,0:T(8,128)(2,1)} %attend.1.mixed), calls=%async_computation.2 | async-start | bytes 4194304 | tf_op jit(solution)/shard_map/all_to_all | solution.py:555
  160.9 25.7 %collective-permute-start.5 = (bf16[4,64,256]{2,1,0:T(8,128)(2,1)S(1)}, bf16[4,64,256]{2,1,0:T(8,128)(2,1)S(1)}, u32[]{:S(2)}, u32[]{:S(2)}) collective-permute-start(bf16[4,64,256]{2,1,0:T(8,128)(2,1)S(1)} %get-tuple-element.53), channel_id=1, source_target_pairs={{0,12},{1,13},{2,14},{3,15},{4,0},{5,1},{6,2},{7,3},{8,4},{9,5},{1... | collective-permute-start | bytes 393224 | tf_op jit(solution)/shard_map/ppermute | solution.py:520
  164.0 24.3 %collective-permute-start.4 = (bf16[4,64,256]{2,1,0:T(8,128)(2,1)S(1)}, bf16[4,64,256]{2,1,0:T(8,128)(2,1)S(1)}, u32[]{:S(2)}, u32[]{:S(2)}) collective-permute-start(bf16[4,64,256]{2,1,0:T(8,128)(2,1)S(1)} %get-tuple-element.54), channel_id=1, source_target_pairs={{0,8},{1,9},{2,10},{3,11},{4,12},{5,13},{6,14},{7,15},{8,0},{9,1},... | collective-permute-start | bytes 393224 | tf_op jit(solution)/shard_map/ppermute | solution.py:520
  164.9 24.6 %collective-permute-start.3 = (bf16[4,64,256]{2,1,0:T(8,128)(2,1)S(1)}, bf16[4,64,256]{2,1,0:T(8,128)(2,1)S(1)}, u32[]{:S(2)}, u32[]{:S(2)}) collective-permute-start(bf16[4,64,256]{2,1,0:T(8,128)(2,1)S(1)} %get-tuple-element.55), channel_id=1, source_target_pairs={{0,4},{1,5},{2,6},{3,7},{4,8},{5,9},{6,10},{7,11},{8,12},{9,13},{1... | collective-permute-start | bytes 393224 | tf_op jit(solution)/shard_map/ppermute | solution.py:520
  189.4 0.8 copy-start.2
  191.0 10.3 %collective-permute-start.6 = (bf16[640,128]{1,0:T(8,128)(2,1)S(1)}, bf16[640,128]{1,0:T(8,128)(2,1)S(1)}, u32[]{:S(2)}, u32[]{:S(2)}) collective-permute-start(bf16[640,128]{1,0:T(8,128)(2,1)S(1)} %get-tuple-element.46), channel_id=1, source_target_pairs={{0,12},{1,13},{2,14},{3,15},{4,0},{5,1},{6,2},{7,3},{8,4},{9,5},{1... | collective-permute-start | bytes 491528 | tf_op jit(solution)/shard_map/ppermute | solution.py:520
  192.2 9.0 %collective-permute-start.8 = (bf16[640,128]{1,0:T(8,128)(2,1)S(1)}, bf16[640,128]{1,0:T(8,128)(2,1)S(1)}, u32[]{:S(2)}, u32[]{:S(2)}) collective-permute-start(bf16[640,128]{1,0:T(8,128)(2,1)S(1)} %get-tuple-element.47), channel_id=1, source_target_pairs={{0,4},{1,5},{2,6},{3,7},{4,8},{5,9},{6,10},{7,11},{8,12},{9,13},{1... | collective-permute-start | bytes 491528 | tf_op jit(solution)/shard_map/ppermute | solution.py:520
  193.1 8.2 %collective-permute-start.7 = (bf16[640,128]{1,0:T(8,128)(2,1)S(1)}, bf16[640,128]{1,0:T(8,128)(2,1)S(1)}, u32[]{:S(2)}, u32[]{:S(2)}) collective-permute-start(bf16[640,128]{1,0:T(8,128)(2,1)S(1)} %get-tuple-element.48), channel_id=1, source_target_pairs={{0,8},{1,9},{2,10},{3,11},{4,12},{5,13},{6,14},{7,15},{8,0},{9,1},... | collective-permute-start | bytes 491528 | tf_op jit(solution)/shard_map/ppermute | solution.py:520
  193.8 7.6 %copy-start.4 = (bf16[8,192,128]{2,1,0:T(8,128)(2,1)S(1)}, bf16[8,192,128]{2,1,0:T(8,128)(2,1)}, u32[]{:S(2)}) copy-start(bf16[8,192,128]{2,1,0:T(8,128)(2,1)} %get-tuple-element.41) | copy-start | bytes 1179652
  201.6 2.0 collective-permute-start.9
  203.8 12.6 %collective-permute-start.10 = (f32[320,128]{1,0:T(8,128)S(1)}, f32[320,128]{1,0:T(8,128)S(1)}, u32[]{:S(2)}, u32[]{:S(2)}) collective-permute-start(f32[320,128]{1,0:T(8,128)S(1)} %get-tuple-element.59), channel_id=1, source_target_pairs={{0,32},{16,48},{32,64},{48,80},{64,96},{80,112},{96,0},{112,16},{1... | collective-permute-start | bytes 491528 | tf_op jit(solution)/shard_map/ppermute | solution.py:481
  204.5 11.9 %collective-permute-start.11 = (f32[320,128]{1,0:T(8,128)S(1)}, f32[320,128]{1,0:T(8,128)S(1)}, u32[]{:S(2)}, u32[]{:S(2)}) collective-permute-start(f32[320,128]{1,0:T(8,128)S(1)} %get-tuple-element.60), channel_id=1, source_target_pairs={{0,64},{16,80},{32,96},{48,112},{64,0},{80,16},{96,32},{112,48},{1... | collective-permute-start | bytes 491528 | tf_op jit(solution)/shard_map/ppermute | solution.py:481
  206.3 10.1 %collective-permute-start.12 = (f32[320,128]{1,0:T(8,128)S(1)}, f32[320,128]{1,0:T(8,128)S(1)}, u32[]{:S(2)}, u32[]{:S(2)}) collective-permute-start(f32[320,128]{1,0:T(8,128)S(1)} %get-tuple-element.61), channel_id=1, source_target_pairs={{0,96},{16,112},{32,0},{48,16},{64,32},{80,48},{96,64},{112,80},{1... | collective-permute-start | bytes 491528 | tf_op jit(solution)/shard_map/ppermute | solution.py:481
  208.2 27.4 %all-to-all-start.3 = ((bf16[128,4,1024]{2,1,0:T(4,128)(2,1)}), bf16[128,4,1024]{2,1,0:T(4,128)(2,1)S(1)}, u32[]{:S(2)}, u32[]{:S(2)}) async-start(bf16[128,4,1024]{2,1,0:T(4,128)(2,1)} %finish_grad.1), calls=%async_computation.3 | async-start | bytes 2097152 | tf_op jit(solution)/shard_map/all_to_all | solution.py:582
  216.5 15.0 %collective-permute-start.14 = (f32[64,128]{1,0:T(8,128)S(1)}, f32[64,128]{1,0:T(8,128)S(1)}, u32[]{:S(2)}, u32[]{:S(2)}) collective-permute-start(f32[64,128]{1,0:T(8,128)S(1)} %slice.82), channel_id=1, source_target_pairs={{0,2},{1,3},{2,0},{3,1},{4,6},{5,7},{6,4},{7,5},{8,10},{9,11},{10,... | collective-permute-start | bytes 98312 | tf_op jit(solution)/shard_map/ppermute | solution.py:515
  219.0 12.5 %collective-permute-start.15 = (f32[64,128]{1,0:T(8,128)S(1)}, f32[64,128]{1,0:T(8,128)S(1)}, u32[]{:S(2)}, u32[]{:S(2)}) collective-permute-start(f32[64,128]{1,0:T(8,128)S(1)} %slice.82), channel_id=1, source_target_pairs={{0,3},{1,0},{2,1},{3,2},{4,7},{5,4},{6,5},{7,6},{8,11},{9,8},{10,9... | collective-permute-start | bytes 98312 | tf_op jit(solution)/shard_map/ppermute | solution.py:515
  220.2 11.3 %collective-permute-start.13 = (f32[64,128]{1,0:T(8,128)S(1)}, f32[64,128]{1,0:T(8,128)S(1)}, u32[]{:S(2)}, u32[]{:S(2)}) collective-permute-start(f32[64,128]{1,0:T(8,128)S(1)} %slice.82), channel_id=1, source_target_pairs={{0,1},{1,2},{2,3},{3,0},{4,5},{5,6},{6,7},{7,4},{8,9},{9,10},{10,1... | collective-permute-start | bytes 98312 | tf_op jit(solution)/shard_map/ppermute | solution.py:515
Sparse Core Ops, SparseCore 0:
  52.3 102.7 all-gather.2
